TPU v7x, 128 devices: a whole 4x4x4 slice. The times are simulated.
128 devices in a mesh: pulse: 8 (over z, y_lo), tile: 16 (over y_hi, x, core).
Axes of the slice: x: 4, y: 4 (y_hi: 2, y_lo: 2; y = y_hi * 2 + y_lo), z: 4, core: 2. Of those that a mesh axis runs over, the one named last changes fastest.
Arguments:
- raw: bfloat16 [2, 512, 2048], P(None, ('pulse', 'tile')), may hold values from -6 to 6
- filt: bfloat16 [2, 1024, 2048], replicated, may hold values from -0.125 to 0.125
- range_off: int32 [512], P(('pulse', 'tile')), may hold values from 0 to 1024
- fine: int32 [512], P(('pulse', 'tile')), may hold values from 0 to 3
- dop: int32 [512], P(('pulse', 'tile')), may hold values from 0 to 1023
- pulse_order: int32 [128, 4], P(('pulse', 'tile')), may hold values from 0 to 3, each once within a row
- band_idx: int32 [16, 512], P(None, ('pulse', 'tile')), may hold values from 0 to 1023
Outputs:
- image: bfloat16 [2, 1024, 65536], P(None, 'pulse', 'tile')
Inputs may be any that keep to these rules, and one draw needn't show every extreme that they name: `pulse_order`: each row is a permutation of 0 .. 3.
All inputs are finite; a program needn't handle non-finite values.
Results may differ from a plain program's by a relative error of at most 0.0065.
Values may be sent and summed in bfloat16 or wider, within the bound.
No kernel may reach another device: no remote copies, remote signals or barrier semaphores. Data moves between devices by JAX's collectives and lax.ppermute only.
A program may use at most 192 MiB of HBM per device.

v0:
```python
import jax
import jax.numpy as jnp
from jax import lax
from jax.sharding import PartitionSpec as P

BAND = 1024
STEPS = 4
PS = 1
R_DEV = 128


def compress(windows, filt):
    wr = windows[:, 0]
    wi = windows[:, 1]
    prof_re = jnp.dot(wr, filt[0], preferred_element_type=jnp.float32) - jnp.dot(
        wi, filt[1], preferred_element_type=jnp.float32
    )
    prof_im = jnp.dot(wr, filt[1], preferred_element_type=jnp.float32) + jnp.dot(
        wi, filt[0], preferred_element_type=jnp.float32
    )
    return jnp.stack([prof_re, prof_im], 1).astype(jnp.bfloat16)


def cut_band(profile, start):
    segment = lax.dynamic_slice_in_dim(profile, start, BAND + 1, 1)
    return (segment[:, :BAND], segment[:, BAND])


def interpolate(pieces, edges, shifts):
    first = pieces.astype(jnp.float32)
    second = jnp.concatenate([first[..., 1:], edges.astype(jnp.float32)[..., None]], -1)
    first = jnp.repeat(first, 4, axis=-1)
    second = jnp.repeat(second, 4, axis=-1)
    phase_q = (jnp.arange(4 * BAND, dtype=jnp.int32) % 4).astype(jnp.float32)
    weight = (4.0 * phase_q[None, :] + shifts.astype(jnp.float32)[:, None]) / 16.0
    weight = weight[:, None, :]
    return first * (1.0 - weight) + second * weight


def gradient_terms(samples, summed):
    sr = samples[:, 0]
    si = samples[:, 1]
    g_re = jnp.sum(sr * summed[None, 0] + si * summed[None, 1], axis=-1)
    g_im = jnp.sum(si * summed[None, 0] - sr * summed[None, 1], axis=-1)
    return (g_re, g_im)


def shards(raw, filt, range_off, fine, dop, pulse_order, band_idx):
    n_pulse = lax.axis_size("pulse")
    n_tile = lax.axis_size("tile")
    devices = n_pulse * n_tile
    pulse_index = lax.axis_index("pulse")
    p_dev = raw.shape[1]
    win = filt.shape[1]
    pulses = p_dev * devices
    total_rows = R_DEV * n_pulse
    cols = 4 * BAND
    all_order, all_dop, all_fine = (
        lax.all_gather(pulse_order, ("pulse", "tile"), axis=0, tiled=True),
        lax.all_gather(dop, ("pulse", "tile"), axis=0, tiled=True),
        lax.all_gather(fine, ("pulse", "tile"), axis=0, tiled=True),
    )
    owners = jnp.arange(devices, dtype=jnp.int32)[:, None] * p_dev
    rows_here = pulse_index * R_DEV + jnp.arange(R_DEV, dtype=jnp.int32)
    accumulated = jnp.zeros((2, R_DEV, cols), jnp.float32)
    for step in range(STEPS):
        local_sel = pulse_order[0, step * PS : (step + 1) * PS]
        picked = jnp.take(raw, local_sel, axis=1)
        offsets = jnp.take(range_off, local_sel)
        windows = jax.vmap(
            lambda row, off: lax.dynamic_slice_in_dim(row, off, win, 1), in_axes=(1, 0)
        )(picked, offsets)
        profile = compress(windows, filt)
        chosen = (owners + all_order[:, step * PS : (step + 1) * PS]).reshape(-1)
        starts = jnp.take(band_idx, local_sel, axis=1)
        pieces, edges = jax.vmap(jax.vmap(cut_band, in_axes=(0, 0)), in_axes=(None, 0))(
            profile, starts
        )
        pieces = pieces.reshape(n_tile * PS, 2, BAND)
        edges = edges.reshape(n_tile * PS, 2)
        mine_pieces, mine_edges = (
            lax.all_to_all(pieces, "tile", split_axis=0, concat_axis=0, tiled=True),
            lax.all_to_all(edges, "tile", split_axis=0, concat_axis=0, tiled=True),
        )
        pieces, edges = (
            lax.all_gather(mine_pieces, "pulse", axis=0, tiled=True),
            lax.all_gather(mine_edges, "pulse", axis=0, tiled=True),
        )
        shifts = jnp.take(all_fine, chosen)
        samples = interpolate(pieces, edges, shifts)
        summed = jnp.sum(samples, axis=0)
        g_re, g_im = gradient_terms(samples, summed)
        g_re, g_im = lax.psum((g_re, g_im), "tile")
        scale = jnp.sqrt(g_re * g_re + g_im * g_im + 1.0)
        c_re = (g_re / scale)[:, None]
        c_im = (-g_im / scale)[:, None]
        sr = samples[:, 0]
        si = samples[:, 1]
        right = jnp.concatenate([c_re * sr - c_im * si, c_re * si + c_im * sr], 0).astype(
            jnp.bfloat16
        )
        dops = jnp.take(all_dop, chosen)
        angle = (
            2.0
            * jnp.pi
            * (dops[:, None] * rows_here[None, :] % total_rows).astype(jnp.float32)
            / total_rows
        )
        norm_scale = jnp.sqrt(jnp.float32(pulses))
        e_re = (jnp.cos(angle) / norm_scale).astype(jnp.bfloat16)
        e_im = (jnp.sin(angle) / norm_scale).astype(jnp.bfloat16)
        left = jnp.stack([jnp.concatenate([e_re, -e_im], 0), jnp.concatenate([e_im, e_re], 0)], 0)
        accumulated = accumulated + jnp.einsum(
            "zkr,kc->zrc", left, right, preferred_element_type=jnp.float32
        )
    return accumulated.astype(jnp.bfloat16)


def solution(mesh):
    return jax.shard_map(
        shards,
        mesh=mesh,
        in_specs=(
            P(None, ("pulse", "tile"), None),
            P(),
            P(("pulse", "tile")),
            P(("pulse", "tile")),
            P(("pulse", "tile")),
            P(("pulse", "tile"), None),
            P(None, ("pulse", "tile")),
        ),
        out_specs=P(None, "pulse", "tile"),
        check_vma=False,
    )
```

profile of v0, /device:TPU:1, one launch (start us, length us, event | category | flops | bytes accessed | tf_op | source)
XLA Modules:
  0.0 910.3 jit_solution(4662210648814878389)
XLA Ops:
  14.1 3.0 fusion.19
  17.1 3.3 fusion.3
  21.9 19.8 %while.17 = (s32[]{:T(128)}, bf16[1,2,2048]{2,1,0:T(2,128)(2,1)S(1)}, s32[16,3]{0,1:T(4,128)S(1)}, bf16[16,2,1025]{2,1,0:T(2,128)(2,1)S(1)}, s32[]{:T(128)}) while((s32[]{:T(128)}, bf16[1,2,2048]{2,1,0:T(2,128)(2,1)S(1)}, s32[16,3]{0,1:T(4,128)S(1)}, bf16[16,2,1025]{2,1,0:T(2,128)(2,1)S(1)}, s32[]{:T(128)}) %tuple.189), condition=%wide.while_cond.13, body=%wide.while_body.13.sunk | while | flops 2 | bytes 9321 | solution.py:25
  42.5 8.4 all-to-all-start.7
  51.6 178.0 %all-gather.4 = s32[128,1,4]{2,1,0:T(1,128)S(1)} all-gather(s32[1,1,4]{2,1,0:T(1,128)S(1)} %bitcast.325), channel_id=1, replica_groups=mesh['pulse'=8,'tile'=16] {'pulse','tile'}, dimensions={0}, use_global_device_ids=true | all-gather | bytes 2064 | tf_op jit(solution)/shard_map/all_gather | solution.py:59
  230.4 62.0 %all-reduce.6 = (s32[512]{0:T(512)S(1)}, s32[512]{0:T(512)S(1)}) all-reduce(s32[512]{0:T(512)S(1)} %dynamic-update-slice.19, s32[512]{0:T(512)S(1)} %dynamic-update-slice.18), channel_id=1, replica_groups=mesh['pulse'=8,'tile'=16] {'pulse','tile'}, use_global_device_ids=true, to_apply=%add.5 | all-reduce | flops 1024 | bytes 8192
  302.9 2.8 fusion.23
  305.7 2.8 fusion.7
  308.6 2.8 fusion.5
  311.4 2.8 fusion.21
  314.4 23.1 %while.16 = (s32[]{:T(128)}, bf16[1,2,2048]{2,1,0:T(2,128)(2,1)S(1)}, s32[16,3]{0,1:T(4,128)S(1)}, bf16[16,2,1025]{2,1,0:T(2,128)(2,1)S(1)}, s32[]{:T(128)}) while((s32[]{:T(128)}, bf16[1,2,2048]{2,1,0:T(2,128)(2,1)S(1)}, s32[16,3]{0,1:T(4,128)S(1)}, bf16[16,2,1025]{2,1,0:T(2,128)(2,1)S(1)}, s32[]{:T(128)}) %tuple.186), condition=%wide.while_cond.10, body=%wide.while_body.10.sunk | while | flops 2 | bytes 9321 | solution.py:25
  338.1 2.8 fusion.27
  341.0 2.8 fusion.11
  343.8 2.8 fusion.9
  346.7 2.8 fusion.25
  349.6 21.6 %while.15 = (s32[]{:T(128)}, bf16[1,2,2048]{2,1,0:T(2,128)(2,1)S(1)}, s32[16,3]{0,1:T(4,128)S(1)}, bf16[16,2,1025]{2,1,0:T(2,128)(2,1)S(1)}, s32[]{:T(128)}) while((s32[]{:T(128)}, bf16[1,2,2048]{2,1,0:T(2,128)(2,1)S(1)}, s32[16,3]{0,1:T(4,128)S(1)}, bf16[16,2,1025]{2,1,0:T(2,128)(2,1)S(1)}, s32[]{:T(128)}) %tuple.183), condition=%wide.while_cond.7, body=%wide.while_body.7.sunk | while | flops 2 | bytes 9321 | solution.py:25
  371.9 2.8 fusion.31
  374.8 2.8 fusion.15
  377.6 2.8 fusion.13
  380.5 2.8 fusion.29
  383.4 20.2 %while.14 = (s32[]{:T(128)}, bf16[1,2,2048]{2,1,0:T(2,128)(2,1)S(1)}, s32[16,3]{0,1:T(4,128)S(1)}, bf16[16,2,1025]{2,1,0:T(2,128)(2,1)S(1)}, s32[]{:T(128)}) while((s32[]{:T(128)}, bf16[1,2,2048]{2,1,0:T(2,128)(2,1)S(1)}, s32[16,3]{0,1:T(4,128)S(1)}, bf16[16,2,1025]{2,1,0:T(2,128)(2,1)S(1)}, s32[]{:T(128)}) %tuple.180), condition=%wide.while_cond.4, body=%wide.while_body.4.sunk | while | flops 2 | bytes 9321 | solution.py:25
  406.6 6.3 broadcast_subtract_fusion.4
  412.9 7.2 broadcast_subtract_fusion
  425.2 5.2 all-to-all-start.5
  430.4 21.9 %all-gather.3 = bf16[128,1,2]{2,1,0:T(2,128)(2,1)S(1)} all-gather(bf16[16,1,2]{2,1,0:T(2,128)(2,1)S(1)} %all-to-all-done.7), channel_id=5, replica_groups=mesh['pulse'=8,'tile'=16] {'pulse'}, dimensions={0}, use_global_device_ids=true | all-gather | bytes 576 | tf_op jit(solution)/shard_map/all_gather | solution.py:87
  452.4 13.6 %all-to-all-start.3 = ((bf16[16,1,2]{2,1,0:T(2,128)(2,1)}), bf16[16,1,2]{2,1,0:T(2,128)(2,1)S(1)}, u32[]{:S(2)}, u32[]{:S(2)}) async-start(bf16[16,1,2]{2,1,0:T(2,128)(2,1)} %copy.119), calls=%async_computation.3 | async-start | bytes 16384 | tf_op jit(solution)/shard_map/all_to_all | solution.py:83
  466.0 21.9 %all-gather.2 = bf16[128,1,2]{2,1,0:T(2,128)(2,1)S(1)} all-gather(bf16[16,1,2]{2,1,0:T(2,128)(2,1)S(1)} %all-to-all-done.5), channel_id=4, replica_groups=mesh['pulse'=8,'tile'=16] {'pulse'}, dimensions={0}, use_global_device_ids=true | all-gather | bytes 576 | tf_op jit(solution)/shard_map/all_gather | solution.py:87
  487.9 13.6 %all-to-all-start.1 = ((bf16[16,1,2]{2,1,0:T(2,128)(2,1)}), bf16[16,1,2]{2,1,0:T(2,128)(2,1)S(1)}, u32[]{:S(2)}, u32[]{:S(2)}) async-start(bf16[16,1,2]{2,1,0:T(2,128)(2,1)} %copy.111), calls=%async_computation.1 | async-start | bytes 16384 | tf_op jit(solution)/shard_map/all_to_all | solution.py:83
  501.5 21.9 %all-gather.1 = bf16[128,1,2]{2,1,0:T(2,128)(2,1)S(1)} all-gather(bf16[16,1,2]{2,1,0:T(2,128)(2,1)S(1)} %all-to-all-done.3), channel_id=3, replica_groups=mesh['pulse'=8,'tile'=16] {'pulse'}, dimensions={0}, use_global_device_ids=true | all-gather | bytes 576 | tf_op jit(solution)/shard_map/all_gather | solution.py:87
  523.5 13.6 %all-to-all-start.6 = ((bf16[16,2,1024]{2,1,0:T(2,128)(2,1)}), bf16[16,2,1024]{2,1,0:T(2,128)(2,1)S(1)}, u32[]{:S(2)}, u32[]{:S(2)}) async-start(bf16[16,2,1024]{2,1,0:T(2,128)(2,1)} %slice_bitcast_fusion.8), calls=%async_computation.6 | async-start | bytes 131072 | tf_op jit(solution)/shard_map/all_to_all | solution.py:82
  537.0 22.4 %all-gather = bf16[128,1,2]{2,1,0:T(2,128)(2,1)S(1)} all-gather(bf16[16,1,2]{2,1,0:T(2,128)(2,1)S(1)} %all-to-all-done.1), channel_id=2, replica_groups=mesh['pulse'=8,'tile'=16] {'pulse'}, dimensions={0}, use_global_device_ids=true | all-gather | bytes 576 | tf_op jit(solution)/shard_map/all_gather | solution.py:87
  560.9 13.0 %all-to-all-start.4 = ((bf16[16,2,1024]{2,1,0:T(2,128)(2,1)}), bf16[16,2,1024]{2,1,0:T(2,128)(2,1)S(1)}, u32[]{:S(2)}, u32[]{:S(2)}) async-start(bf16[16,2,1024]{2,1,0:T(2,128)(2,1)} %slice_bitcast_fusion.9), calls=%async_computation.4 | async-start | bytes 131072 | tf_op jit(solution)/shard_map/all_to_all | solution.py:82
  573.9 24.9 %all_gather.42 = bf16[128,2,1024]{2,1,0:T(2,128)(2,1)S(1)} all-gather(bf16[16,2,1024]{2,1,0:T(2,128)(2,1)S(1)} %all-to-all-done.6), channel_id=1, replica_groups=mesh['pulse'=8,'tile'=16] {'pulse'}, dimensions={0}, use_global_device_ids=true | all-gather | bytes 589824 | tf_op jit(solution)/shard_map/all_gather | solution.py:86
  598.8 12.3 %all-to-all-start.2 = ((bf16[16,2,1024]{2,1,0:T(2,128)(2,1)}), bf16[16,2,1024]{2,1,0:T(2,128)(2,1)S(1)}, u32[]{:S(2)}, u32[]{:S(2)}) async-start(bf16[16,2,1024]{2,1,0:T(2,128)(2,1)} %slice_bitcast_fusion.10), calls=%async_computation.2 | async-start | bytes 131072 | tf_op jit(solution)/shard_map/all_to_all | solution.py:82
  611.1 24.6 %all_gather.40 = bf16[128,2,1024]{2,1,0:T(2,128)(2,1)S(1)} all-gather(bf16[16,2,1024]{2,1,0:T(2,128)(2,1)S(1)} %all-to-all-done.4), channel_id=1, replica_groups=mesh['pulse'=8,'tile'=16] {'pulse'}, dimensions={0}, use_global_device_ids=true | all-gather | bytes 589824 | tf_op jit(solution)/shard_map/all_gather | solution.py:86
  635.7 12.6 %all-to-all-start = ((bf16[16,2,1024]{2,1,0:T(2,128)(2,1)}), bf16[16,2,1024]{2,1,0:T(2,128)(2,1)}, u32[]{:S(2)}, u32[]{:S(2)}) async-start(bf16[16,2,1024]{2,1,0:T(2,128)(2,1)} %slice_bitcast_fusion.11), calls=%async_computation | async-start | bytes 131072 | tf_op jit(solution)/shard_map/all_to_all | solution.py:82
  648.2 24.6 %all_gather.38 = bf16[128,2,1024]{2,1,0:T(2,128)(2,1)S(1)} all-gather(bf16[16,2,1024]{2,1,0:T(2,128)(2,1)S(1)} %all-to-all-done.2), channel_id=1, replica_groups=mesh['pulse'=8,'tile'=16] {'pulse'}, dimensions={0}, use_global_device_ids=true | all-gather | bytes 589824 | tf_op jit(solution)/shard_map/all_gather | solution.py:86
  681.3 24.3 %all_gather.35 = bf16[128,2,1024]{2,1,0:T(2,128)(2,1)S(1)} all-gather(bf16[16,2,1024]{2,1,0:T(2,128)(2,1)} %all-to-all-done), channel_id=1, replica_groups=mesh['pulse'=8,'tile'=16] {'pulse'}, dimensions={0}, use_global_device_ids=true | all-gather | bytes 589824 | tf_op jit(solution)/shard_map/all_gather | solution.py:86
  709.7 2.8 pad_maximum_fusion.3
  714.8 4.0 broadcast_in_dim.162
  718.8 5.7 copy.139
  724.5 3.9 broadcast_in_dim.159
  728.4 5.7 copy.133
  734.1 5.2 add_reduce_fusion
  743.6 2.8 pad_maximum_fusion.2
  748.6 3.9 broadcast_in_dim.155
  752.5 5.6 copy.131
  760.8 5.6 copy.125
  766.4 5.0 add_reduce_fusion.1
  772.1 2.7 pad_maximum_fusion.1
  776.5 2.7 broadcast_in_dim.148
  779.3 5.7 copy.123
  787.7 5.7 copy.117
  793.4 4.9 add_reduce_fusion.2
  801.2 4.9 add_reduce_fusion.3
  809.4 5.6 copy.115
  815.0 2.8 broadcast_in_dim.138
  817.8 5.9 copy.109
  823.7 5.9 multiply_add_fusion
  833.5 3.0 multiply_add_fusion.1
  840.2 3.5 multiply_add_fusion.2
  847.6 2.8 multiply_add_fusion.3
  853.2 44.6 %all-reduce.7 = (f32[128]{0:T(128)S(1)}, f32[128]{0:T(128)S(1)}, f32[128]{0:T(128)S(1)}, f32[128]{0:T(128)S(1)}, f32[128]{0:T(128)S(1)}, /*index=5*/f32[128]{0:T(128)S(1)}, f32[128]{0:T(128)S(1)}, f32[128]{0:T(128)S(1)}) all-reduce(f32[128]{0:T(128)S(1)} %get-tuple-element.157, ...), channel_id=1, replica_groups=mesh['pulse'=8,'tile'=16] {'tile'}, use_global_device_ids=true, to_apply=%region_4.8 | all-reduce | flops 1024 | bytes 8192 | tf_op jit(solution)/shard_map/psum | solution.py:93
  897.7 3.0 subtract_convert_fusion
  (399 shorter events, 171.5 us)
Async XLA Ops:
  14.1 6.3 copy-start
  20.4 1.4 copy-start.28
  20.4 31.2 %copy-start.27 = (s32[1,4]{1,0:T(1,128)S(1)}, s32[1,4]{1,0:T(1,128)}, u32[]{:S(2)}) copy-start(s32[1,4]{1,0:T(1,128)} %param.18) | copy-start | bytes 52
  20.4 209.5 %copy-start.29 = (s32[4]{0:T(128)S(1)}, s32[4]{0:T(128)}, u32[]{:S(2)}) copy-start(s32[4]{0:T(128)} %param.17) | copy-start | bytes 52
  20.4 209.8 %copy-start.30 = (s32[4]{0:T(128)S(1)}, s32[4]{0:T(128)}, u32[]{:S(2)}) copy-start(s32[4]{0:T(128)} %param.16) | copy-start | bytes 52
  42.5 382.7 %all-to-all-start.7 = ((bf16[16,1,2]{2,1,0:T(2,128)(2,1)}), bf16[16,1,2]{2,1,0:T(2,128)(2,1)S(1)}, u32[]{:S(2)}, u32[]{:S(2)}) async-start(bf16[16,1,2]{2,1,0:T(2,128)(2,1)} %copy.135), calls=%async_computation.7 | async-start | bytes 16384 | tf_op jit(solution)/shard_map/all_to_all | solution.py:83
  425.2 27.2 %all-to-all-start.5 = ((bf16[16,1,2]{2,1,0:T(2,128)(2,1)}), bf16[16,1,2]{2,1,0:T(2,128)(2,1)S(1)}, u32[]{:S(2)}, u32[]{:S(2)}) async-start(bf16[16,1,2]{2,1,0:T(2,128)(2,1)} %copy.127), calls=%async_computation.5 | async-start | bytes 16384 | tf_op jit(solution)/shard_map/all_to_all | solution.py:83
  452.4 35.5 %all-to-all-start.3 = ((bf16[16,1,2]{2,1,0:T(2,128)(2,1)}), bf16[16,1,2]{2,1,0:T(2,128)(2,1)S(1)}, u32[]{:S(2)}, u32[]{:S(2)}) async-start(bf16[16,1,2]{2,1,0:T(2,128)(2,1)} %copy.119), calls=%async_computation.3 | async-start | bytes 16384 | tf_op jit(solution)/shard_map/all_to_all | solution.py:83
  487.9 35.5 %all-to-all-start.1 = ((bf16[16,1,2]{2,1,0:T(2,128)(2,1)}), bf16[16,1,2]{2,1,0:T(2,128)(2,1)S(1)}, u32[]{:S(2)}, u32[]{:S(2)}) async-start(bf16[16,1,2]{2,1,0:T(2,128)(2,1)} %copy.111), calls=%async_computation.1 | async-start | bytes 16384 | tf_op jit(solution)/shard_map/all_to_all | solution.py:83
  523.5 37.4 %all-to-all-start.6 = ((bf16[16,2,1024]{2,1,0:T(2,128)(2,1)}), bf16[16,2,1024]{2,1,0:T(2,128)(2,1)S(1)}, u32[]{:S(2)}, u32[]{:S(2)}) async-start(bf16[16,2,1024]{2,1,0:T(2,128)(2,1)} %slice_bitcast_fusion.8), calls=%async_computation.6 | async-start | bytes 131072 | tf_op jit(solution)/shard_map/all_to_all | solution.py:82
  560.9 37.9 %all-to-all-start.4 = ((bf16[16,2,1024]{2,1,0:T(2,128)(2,1)}), bf16[16,2,1024]{2,1,0:T(2,128)(2,1)S(1)}, u32[]{:S(2)}, u32[]{:S(2)}) async-start(bf16[16,2,1024]{2,1,0:T(2,128)(2,1)} %slice_bitcast_fusion.9), calls=%async_computation.4 | async-start | bytes 131072 | tf_op jit(solution)/shard_map/all_to_all | solution.py:82
  598.8 36.9 %all-to-all-start.2 = ((bf16[16,2,1024]{2,1,0:T(2,128)(2,1)}), bf16[16,2,1024]{2,1,0:T(2,128)(2,1)S(1)}, u32[]{:S(2)}, u32[]{:S(2)}) async-start(bf16[16,2,1024]{2,1,0:T(2,128)(2,1)} %slice_bitcast_fusion.10), calls=%async_computation.2 | async-start | bytes 131072 | tf_op jit(solution)/shard_map/all_to_all | solution.py:82
  635.7 45.6 %all-to-all-start = ((bf16[16,2,1024]{2,1,0:T(2,128)(2,1)}), bf16[16,2,1024]{2,1,0:T(2,128)(2,1)}, u32[]{:S(2)}, u32[]{:S(2)}) async-start(bf16[16,2,1024]{2,1,0:T(2,128)(2,1)} %slice_bitcast_fusion.11), calls=%async_computation | async-start | bytes 131072 | tf_op jit(solution)/shard_map/all_to_all | solution.py:82
  672.8 5.3 copy-start.14
  705.6 0.8 copy-start.15
  823.7 6.0 copy-start.26
  823.7 8.1 copy-start.9
  823.7 8.1 copy-start.17
  829.6 2.1 copy-start.7
  829.7 3.8 copy-start.8
  833.5 5.1 copy-start.11
  836.5 2.1 copy-start.5
  836.5 3.7 copy-start.10
  840.2 5.6 copy-start.13
  840.2 5.6 copy-start.16
  843.7 2.1 copy-start.3
  843.7 3.9 copy-start.12
  850.4 1.9 copy-start.1
  897.7 3.4 copy-start.6
  900.8 2.3 copy-start.4
  901.9 2.5 copy-start.2
  903.8 1.4 copy-start.20
  903.8 1.4 copy-start.21
  905.1 0.8 copy-start.24
  905.1 0.9 copy-start.25
  906.0 0.8 copy-start.22
  906.0 0.9 copy-start.23
  906.8 0.8 copy-start.18
  906.8 0.9 copy-start.19
where the time goes:
time: 918 us; the launch traced here: 910 us
  blocking collectives  471 us (51%)
  local copies, waits for them, and re-layouts  215 us (23%)
  starting transfers between devices  92.3 us (10%)
  other arithmetic  74 us (8%)
  matrix products  46 us (5%)
  between operations  11.6 us (1%)
    all_gather x1, blocking collectives, shards(): lax.all_gather(pulse_order, ('pulse', 'tile'), axis=0, tiled=True)  178 us
    all_gather x4, blocking collectives, shards(): lax.all_gather(mine_pieces, 'pulse', axis=0, tiled=True)  98.4 us
    all_gather x4, blocking collectives, shards(): lax.all_gather(mine_edges, 'pulse', axis=0, tiled=True)  88 us
    gather x192, local copies, waits for them, and re-layouts  84 us
    unnamed x1, blocking collectives  62 us
    all_to_all x4, starting transfers between devices, shards(): lax.all_to_all(pieces, 'tile', split_axis=0, concat_axis=0, tiled=True)  51.4 us
    psum x1, blocking collectives, shards(): g_re, g_im = lax.psum((g_re, g_im), 'tile')  44.6 us
    all_to_all x4, starting transfers between devices, shards(): lax.all_to_all(edges, 'tile', split_axis=0, concat_axis=0, tiled=True)  40.8 us
  transfers between devices with their start and end apart: 8, of which 0 were waited for; matrix products, arithmetic and copies ran while one was open for 16% of the time, Pallas kernels for 0%

commit v1 on v0

v1 whole, which is shorter than its diff:
```python
import jax
import jax.numpy as jnp
from jax import lax
from jax.experimental import pallas as pl
from jax.experimental.pallas import tpu as pltpu
from jax.sharding import PartitionSpec as P

AXES = ("pulse", "tile")
WIN = 1024
UPS = 2048
MSG = 2 * WIN + 128
GROUP = 64
HALF = 256
BW = 1152
ROWS = 128
STEPS = (0, 1, 3, 2)
F32 = jnp.float32
BF16 = jnp.bfloat16
NT = (((1,), (1,)), ((), ()))


def linear(z, y, x, core):
    return (z * 2 + y % 2) * 16 + ((y // 2) * 4 + x) * 2 + core


def moves(target):
    return [
        (linear(z, y, x, c), linear(*target(z, y, x, c)))
        for z in range(4)
        for y in range(4)
        for x in range(4)
        for c in range(2)
    ]


def along_z(k):
    return moves(lambda z, y, x, c: ((z + k) % 4, y, x, c))


def along_y(k):
    return moves(lambda z, y, x, c: (z, (y + k) % 4, x, c))


def along_x(k):
    return moves(lambda z, y, x, c: (z, y, (x + k) % 4, c))


def other_core():
    return moves(lambda z, y, x, c: (z, y, x, 1 - c))


def iota(shape, axis):
    return lax.broadcasted_iota(jnp.int32, shape, axis)


def window_kernel(order, off, fine, dop, band, raw, out):
    x = jnp.concatenate([raw[0].astype(F32), raw[1].astype(F32)], 0)
    row8 = iota((8, WIN), 0)
    row4 = iota((4, WIN), 0)
    lane = iota((1, 128), 1)
    meta_row = iota((4, 128), 0)
    re = jnp.zeros((4, WIN), F32)
    im = jnp.zeros((4, WIN), F32)
    meta = jnp.zeros((4, 128), jnp.int32)
    for j in range(4):
        k = order[0, j]
        y = pltpu.roll(x, lax.rem(UPS - off[k], UPS), 1)[:, :WIN]
        one_re = jnp.sum(jnp.where(row8 == k, y, 0.0), axis=0, keepdims=True)
        one_im = jnp.sum(jnp.where(row8 == k + 4, y, 0.0), axis=0, keepdims=True)
        re = jnp.where(row4 == j, one_re, re)
        im = jnp.where(row4 == j, one_im, im)
        d = dop[k]
        v = jnp.where(lane == 1, fine[k], 0)
        v = jnp.where(lane == 2, d >> 5, v)
        v = jnp.where(lane == 3, d & 31, v)
        for t in range(16):
            b = band[t, k]
            v = jnp.where(lane == 16 + t, b >> 5, v)
            v = jnp.where(lane == 32 + t, b & 31, v)
        meta = jnp.where(meta_row == j, v, meta)
    out[:, :WIN] = re.astype(BF16)
    out[:, WIN : 2 * WIN] = im.astype(BF16)
    out[:, 2 * WIN :] = meta.astype(F32).astype(BF16)


def band_kernel(m0, m1, m2, m3, filt, mine, theirs, w, info, prof, cut, starts_v, starts_s, sem):
    n = pl.program_id(0)
    tile = lax.axis_index("tile")

    @pl.when(n == 0)
    def _():
        x_here = lax.rem(tile // 2, 4)
        y_here = tile // 8 * 2 + lax.rem(lax.axis_index("pulse"), 2)
        for m, dx in zip((m0, m1, m2, m3), STEPS):
            from_x = lax.rem(x_here + 4 - dx, 4)
            for i, dy in enumerate(STEPS):
                from_y = lax.rem(y_here + 4 - dy, 4)
                at = pl.multiple_of(from_x * GROUP + from_y * 16, 16)
                wr = m[16 * i : 16 * i + 16, :WIN]
                wi = m[16 * i : 16 * i + 16, WIN : 2 * WIN]
                w[pl.ds(at, 16), :WIN] = wr
                w[pl.ds(at, 16), WIN:] = -wi
                w[pl.ds(at + HALF, 16), :WIN] = wi
                w[pl.ds(at + HALF, 16), WIN:] = wr
                info[pl.ds(at, 16), :] = m[16 * i : 16 * i + 16, 2 * WIN :]

    f = filt[...].reshape(2 * WIN, 256)
    r = jnp.dot(w[...], f, preferred_element_type=F32)
    for comp in range(2):
        for h in range(2):
            base = pl.multiple_of((comp * 16 + 2 * n + h) * 8, 8)
            for g in range(32):
                prof[pl.ds(base + g * 256, 8), :] = r[
                    comp * HALF + 8 * g : comp * HALF + 8 * g + 8, 128 * h : 128 * h + 128
                ]

    @pl.when(n == 7)
    def _():
        sibling = tile + 1 - 2 * lax.rem(tile, 2)
        row = iota((8, 128), 0)
        lane = iota((8, 128), 1)
        want = jnp.where(row == 0, tile, sibling)
        pick = jnp.where(lane == want + 16, 32.0, jnp.where(lane == want + 32, 1.0, 0.0)).astype(BF16)
        got = lax.dot_general(pick, info[...], NT, preferred_element_type=F32)
        starts_v[...] = got.astype(jnp.int32)
        copy = pltpu.make_async_copy(starts_v, starts_s, sem)
        copy.start()
        copy.wait()
        lane8 = iota((8, 128), 1)

        def per_group(g, _):
            for sub in range(8):
                for which in range(2):
                    start = starts_s[which, g * 8 + sub]
                    a = start >> 7
                    r = start & 127
                    turn = (128 - r) & 127
                    inside = lane8 < 128 - r
                    for comp in range(2):
                        at = g * 256 + (comp * 16 + a) * 8 + sub
                        low = pltpu.roll(prof[pl.ds(at, 8, 8), :], turn, 1)
                        high = pltpu.roll(prof[pl.ds(at + 8, 8, 8), :], turn, 1)
                        to = g * 144 + comp * 72 + sub
                        cut[which, pl.ds(to + 8, 8, 8), :] = high
                        cut[which, pl.ds(to, 8, 8), :] = jnp.where(inside, low, high)
            return 0

        lax.fori_loop(0, 32, per_group, 0)
        lane16 = iota((16, 128), 1)
        for which, out in enumerate((mine, theirs)):
            for top in range(0, HALF, 16):
                meta = info[top : top + 16, :].astype(F32)
                for comp in range(2):
                    for c in range(9):
                        at = (top // 8) * 144 + comp * 72 + c * 8
                        v = jnp.concatenate(
                            [cut[which, at : at + 8, :], cut[which, at + 144 : at + 152, :]], 0
                        )
                        if c == 8:
                            v = jnp.where(lane16 == 0, v, jnp.where(lane16 < 4, meta, 0.0))
                        to = comp * HALF + top
                        out[to : to + 16, 128 * c : 128 * c + 128] = v.astype(BF16)


def gradient_kernel(ba, bb, g_out, meta_out):
    row = iota((8, 128), 0)
    lane = iota((8, 128), 1)
    pick = jnp.where(
        row == 0,
        jnp.where(lane == 1, 1.0, 0.0),
        jnp.where(lane == 2, 32.0, jnp.where(lane == 3, 1.0, 0.0)),
    ).astype(BF16)
    block = iota((8, HALF), 0) % 4
    keep = jnp.where(iota((8, HALF), 1) % 4 == block, 1.0, 0.0)
    sums_re = jnp.zeros((16, BW), F32)
    sums_im = jnp.zeros((16, BW), F32)
    weights = []
    for i, b in enumerate((ba, bb)):
        meta = lax.dot_general(pick, b[:HALF, WIN:], NT, preferred_element_type=F32)
        meta_out[:, HALF * i : HALF * (i + 1)] = meta
        shift = meta[0:1] / 16.0
        lhs = jnp.concatenate([keep, keep * shift], 0).astype(BF16)
        sums_re += jnp.dot(lhs, b[:HALF], preferred_element_type=F32)
        sums_im += jnp.dot(lhs, b[HALF:], preferred_element_type=F32)
        weights.append(jnp.where(iota((8, HALF), 0) < 4, keep, keep * shift))
    m = iota((8, BW), 1)
    top = iota((8, BW), 0) < 4
    parts = []
    for sums in (sums_re, sums_im):
        s = sums[:8]
        t = sums[8:]
        x0 = s + pltpu.roll(t, BW - 1, 1) - t
        dr = pltpu.roll(s, BW - 1, 1) - s
        a = jnp.where(m < WIN, 4.0 * x0 + 1.5 * dr, 0.0)
        b = jnp.where(m < WIN, 1.5 * x0 + 0.875 * dr, 0.0)
        p = a - b + pltpu.roll(b, 1, 1)
        q = pltpu.roll(a, 1, 1) - a
        parts.append(jnp.where(top, p, q))
    both = jnp.concatenate(parts, 0)
    high = both.astype(BF16)
    low = (both - high.astype(F32)).astype(BF16)
    lhs = jnp.concatenate([high, low], 0)
    halves = []
    for i, b in enumerate((ba, bb)):
        g = lax.dot_general(lhs, b[...], NT, preferred_element_type=F32)
        g = g[:16] + g[16:]
        re = g[:8, :HALF] + g[8:, HALF:]
        im = g[:8, HALF:] - g[8:, :HALF]
        g_re = jnp.sum(re * weights[i], axis=0, keepdims=True)
        g_im = jnp.sum(im * weights[i], axis=0, keepdims=True)
        halves.append(jnp.concatenate([g_re, g_im], 0))
    first = lax.rem(lax.axis_index("tile"), 2) == 0
    g_out[:, :HALF] = jnp.where(first, halves[0], halves[1])
    g_out[:, HALF:] = jnp.where(first, halves[1], halves[0])


def image_kernel(g, meta, ba, bb, out, lhs, xd):
    first = lax.rem(lax.axis_index("tile"), 2) == 0
    both = jnp.concatenate(
        [jnp.where(first, g[:, :HALF], g[:, HALF:]), jnp.where(first, g[:, HALF:], g[:, :HALF])], 1
    )
    g_re = both[0:1]
    g_im = both[1:2]
    inv = 1.0 / jnp.sqrt(g_re * g_re + g_im * g_im + 1.0)
    inv = inv * (512.0**-0.5)
    c_re = g_re * inv
    c_im = -g_im * inv
    shift = meta[0:1] / 16.0
    dop = meta[1:2].astype(jnp.int32)
    pulse = lax.axis_index("pulse")
    step = 2.0 * jnp.pi / 1024.0
    coarse = ((iota((16, 512), 0) * 8 + pulse * ROWS) * dop & 1023).astype(F32) * step
    finer = (iota((8, 512), 0) * dop & 1023).astype(F32) * step
    cu = jnp.cos(coarse)
    su = jnp.sin(coarse)
    cv = jnp.cos(finer)
    sv = jnp.sin(finer)
    vr = cv * c_re - sv * c_im
    vi = cv * c_im + sv * c_re
    for u in range(16):
        ur = cu[u : u + 1]
        ui = su[u : u + 1]
        lr = ur * vr - ui * vi
        li = ur * vi + ui * vr
        for scale, at in ((None, 0), (shift, 256)):
            r = lr if scale is None else lr * scale
            i = li if scale is None else li * scale
            for half in range(2):
                rr = r[:, HALF * half : HALF * (half + 1)]
                ii = i[:, HALF * half : HALF * (half + 1)]
                a = at + 8 * u
                lhs[a : a + 8, 512 * half : 512 * half + HALF] = rr
                lhs[a : a + 8, 512 * half + HALF : 512 * half + 512] = -ii
                lhs[a + 128 : a + 136, 512 * half : 512 * half + HALF] = ii
                lhs[a + 128 : a + 136, 512 * half + HALF : 512 * half + 512] = rr
    uv = jnp.dot(lhs[:, :512].astype(BF16), ba[...], preferred_element_type=F32) + jnp.dot(
        lhs[:, 512:].astype(BF16), bb[...], preferred_element_type=F32
    )
    later = pltpu.roll(uv, BW - 1, 1)
    diff = later - uv
    xd[:, :WIN] = (uv[:256] + diff[256:])[:, :WIN].astype(BF16)
    xd[:, WIN:] = diff[:256, :WIN].astype(BF16)
    k = iota((256, 512), 0)
    col = iota((256, 512), 1)
    same = (k % 128) == (col // 4)
    quarter = (col % 4).astype(F32) * 0.25
    spread = jnp.where(same, jnp.where(k < 128, 1.0, quarter), 0.0).astype(BF16)
    for j in range(8):
        part = jnp.concatenate(
            [xd[:, 128 * j : 128 * j + 128], xd[:, WIN + 128 * j : WIN + 128 * j + 128]], 1
        )
        res = jnp.dot(part, spread, preferred_element_type=F32).astype(BF16)
        out[0, :, 512 * j : 512 * j + 512] = res[:128]
        out[1, :, 512 * j : 512 * j + 512] = res[128:]


def vmem():
    return pl.BlockSpec(memory_space=pltpu.VMEM)


def smem():
    return pl.BlockSpec(memory_space=pltpu.SMEM)


def params():
    return pltpu.CompilerParams(vmem_limit_bytes=48 * 1024 * 1024)


def shards(raw, filt, range_off, fine, dop, pulse_order, band_idx):
    own = pl.pallas_call(
        window_kernel,
        out_shape=jax.ShapeDtypeStruct((4, MSG), BF16),
        in_specs=[smem()] * 5 + [vmem()],
        out_specs=vmem(),
        compiler_params=params(),
    )(pulse_order, range_off, fine, dop, band_idx, raw)
    line = jnp.concatenate([own] + [lax.ppermute(own, AXES, along_z(k)) for k in STEPS[1:]], 0)
    plane = jnp.concatenate([line] + [lax.ppermute(line, AXES, along_y(k)) for k in STEPS[1:]], 0)
    groups = [plane] + [lax.ppermute(plane, AXES, along_x(k)) for k in STEPS[1:]]
    whole = pl.BlockSpec((GROUP, MSG), lambda n: (0, 0))
    mine, theirs = pl.pallas_call(
        band_kernel,
        grid=(8,),
        out_shape=[jax.ShapeDtypeStruct((2 * HALF, BW), BF16)] * 2,
        in_specs=[whole] * 4 + [pl.BlockSpec((2, WIN, 256), lambda n: (0, 0, n))],
        out_specs=[pl.BlockSpec((2 * HALF, BW), lambda n: (0, 0))] * 2,
        scratch_shapes=[
            pltpu.VMEM((2 * HALF, 2 * WIN), BF16),
            pltpu.VMEM((HALF, 128), BF16),
            pltpu.VMEM((8192, 128), F32),
            pltpu.VMEM((2, 4608, 128), F32),
            pltpu.VMEM((8, HALF), jnp.int32),
            pltpu.SMEM((8, HALF), jnp.int32),
            pltpu.SemaphoreType.DMA,
        ],
        compiler_params=params(),
    )(*groups, filt)
    given = lax.ppermute(theirs, AXES, other_core())
    partial, meta = pl.pallas_call(
        gradient_kernel,
        out_shape=[jax.ShapeDtypeStruct((2, 512), F32), jax.ShapeDtypeStruct((8, 512), F32)],
        in_specs=[vmem()] * 2,
        out_specs=[vmem()] * 2,
        compiler_params=params(),
    )(mine, given)
    sent = jnp.broadcast_to(partial[None], (16, 2, 512))
    grads = jnp.sum(lax.all_to_all(sent, "tile", split_axis=0, concat_axis=0, tiled=True), axis=0)
    return pl.pallas_call(
        image_kernel,
        out_shape=jax.ShapeDtypeStruct((2, ROWS, 4 * WIN), BF16),
        in_specs=[vmem()] * 4,
        out_specs=vmem(),
        scratch_shapes=[pltpu.VMEM((512, 1024), F32), pltpu.VMEM((256, 2 * WIN), BF16)],
        compiler_params=params(),
    )(grads, meta, mine, given)


def solution(mesh):
    return jax.shard_map(
        shards,
        mesh=mesh,
        in_specs=(
            P(None, AXES, None),
            P(),
            P(AXES),
            P(AXES),
            P(AXES),
            P(AXES, None),
            P(None, AXES),
        ),
        out_specs=P(None, "pulse", "tile"),
        check_vma=False,
    )
```

time: 918 us -> 74 us (0.08)
  blocking collectives: 471 us -> 11.5 us
  local copies, waits for them, and re-layouts: 215 us -> 4.29 us
  starting transfers between devices: 92.3 us -> 18 us
  other arithmetic: 74 us -> 0.08 us
  matrix products: 46 us -> 0 us
  Pallas kernels: 0 us -> 21 us
  waiting for transfers between devices: 0.02 us -> 18.6 us
  between operations: 11.6 us -> 0.06 us
    all_gather x9 -> x0, blocking collectives: 364 us -> none  [the longest x1 178 us: shards(): lax.all_gather(pulse_order, ('pulse', 'tile'), axis=0, tiled=True)]
    gather x203 -> x0, local copies, waits for them, and re-layouts: 95.7 us -> none
    all_to_all x8 -> x0, starting transfers between devices: 92.3 us -> none  [the longest x4 51.4 us: shards(): lax.all_to_all(pieces, 'tile', split_axis=0, concat_axis=0, tiled=True)]
    unnamed x1 -> x0, blocking collectives: 62 us -> none
    reshape x12 -> x0, local copies, waits for them, and re-layouts: 48.2 us -> none  [the longest x4 22.9 us: interpolate(): first = jnp.repeat(first, 4, axis=-1)]
    dot_general x20 -> x0, matrix products: 46 us -> none  [the longest x4 11.9 us: compress(): jnp.dot(wi, filt[1], preferred_element_type=jnp.float32)]
    psum x1 -> x0, blocking collectives: 44.6 us -> none  [shards(): g_re, g_im = lax.psum((g_re, g_im), 'tile')]
    broadcast_in_dim x12 -> x1, local copies, waits for them, and re-layouts: 26.6 us -> 0.02 us  [shards(): sent = jnp.broadcast_to(partial[None], (16, 2, 512))]
  transfers between devices with their start and end apart: 8 -> 10, of which waited for: 0 -> 9; matrix products, arithmetic and copies ran while one was open for 16% -> 0% of each run, Pallas kernels for 0% -> 0%
where the time goes in v1:
time: 74 us; the launch traced here: 73.5 us
  Pallas kernels  21 us (28%)
  waiting for transfers between devices  18.6 us (25%)
  starting transfers between devices  18 us (24%)
  blocking collectives  11.5 us (16%)
  local copies, waits for them, and re-layouts  4.29 us (6%)
    pallas_call x1, Pallas kernels, shards(): pl.pallas_call(band_kernel, grid=(8,), out_shape=[jax.ShapeDtypeStruct((2...  15 us
    all_to_all x1, blocking collectives, shards(): lax.all_to_all(sent, 'tile', split_axis=0, concat_axis=0, tiled=True)  11.5 us
    ppermute x3, waiting for transfers between devices, shards(): lax.ppermute(plane, AXES, along_x(k))  9.44 us
    ppermute x3, starting transfers between devices, shards(): lax.ppermute(own, AXES, along_z(k))  5.97 us
    ppermute x3, starting transfers between devices, shards(): lax.ppermute(line, AXES, along_y(k))  4.46 us
    ppermute x3, starting transfers between devices, shards(): lax.ppermute(plane, AXES, along_x(k))  4.29 us
    unnamed x11, local copies, waits for them, and re-layouts  4.13 us
    ppermute x3, waiting for transfers between devices, shards(): lax.ppermute(line, AXES, along_y(k))  3.91 us
  transfers between devices with their start and end apart: 10, of which 9 were waited for; matrix products, arithmetic and copies ran while one was open for 0% of the time, Pallas kernels for 0%

profile of v1, /device:TPU:1, one launch (start us, length us, event | category | flops | bytes accessed | tf_op | source)
XLA Modules:
  0.0 73.5 jit_solution(14229223558900128261)
XLA Ops:
  0.0 0.8 %copy.10.band = s32[16,4]{1,0:T(8,128)S(1)} copy(s32[16,4]{0,1:T(4,128)} %param.13) | data formatting | bytes 512 | tf_op args[6]
  0.8 0.0 copy-start
  0.8 0.8 %copy-done = bf16[2,4,2048]{2,1,0:T(4,128)(2,1)S(1)} copy-done((bf16[2,4,2048]{2,1,0:T(4,128)(2,1)S(1)}, bf16[2,4,2048]{2,1,0:T(4,128)(2,1)}, u32[]{:S(2)}) %copy-start) | copy-done | bytes 32792
  1.5 0.0 copy-start.1
  1.5 0.7 copy-done.1
  2.2 0.0 copy-start.2
  2.2 0.7 copy-done.2
  2.8 0.0 copy-start.3
  2.8 0.7 copy-done.3
  3.5 0.0 copy-start.4
  3.5 0.7 copy-done.4
  4.1 0.9 %shard_map.73 = bf16[4,2176]{1,0:T(4,128)(2,1)S(1)} custom-call(s32[1,4]{1,0:T(1,128)S(1)} %copy-done.1, s32[4]{0:T(128)S(1)} %copy-done.2, s32[4]{0:T(128)S(1)} %copy-done.3, s32[4]{0:T(128)S(1)} %copy-done.4, s32[16,4]{1,0:T(8,128)S(1)} %copy.10.band, bf16[2,4,2048]{2,1,0:T(4,128)(2,1)S(1)} %copy-done), custom_call_target="tpu_custom_call" | custom-call | tf_op jit(solution)/shard_map/pallas_call | solution.py:290
  5.1 4.5 %collective-permute-start.2 = (bf16[4,2176]{1,0:T(4,128)(2,1)S(1)}, bf16[4,2176]{1,0:T(4,128)(2,1)S(1)}, u32[]{:S(2)}, u32[]{:S(2)}) collective-permute-start(bf16[4,2176]{1,0:T(4,128)(2,1)S(1)} %shard_map.73), channel_id=1, source_target_pairs={{0,64},{1,65},{2,66},{3,67},{4,68},{5,69},{6,70},{7,71},{16,80},{1... | collective-permute-start | bytes 52232 | tf_op jit(solution)/shard_map/ppermute | solution.py:297
  9.6 0.4 collective-permute-start.1
  10.0 1.0 %collective-permute-start = (bf16[4,2176]{1,0:T(4,128)(2,1)S(1)}, bf16[4,2176]{1,0:T(4,128)(2,1)S(1)}, u32[]{:S(2)}, u32[]{:S(2)}) collective-permute-start(bf16[4,2176]{1,0:T(4,128)(2,1)S(1)} %shard_map.73), channel_id=1, source_target_pairs={{0,32},{1,33},{2,34},{3,35},{4,36},{5,37},{6,38},{7,39},{16,48},{1... | collective-permute-start | bytes 52232 | tf_op jit(solution)/shard_map/ppermute | solution.py:297
  11.0 0.0 collective-permute-done.2
  11.1 1.1 %collective-permute-done.1 = bf16[4,2176]{1,0:T(4,128)(2,1)S(1)} collective-permute-done((bf16[4,2176]{1,0:T(4,128)(2,1)S(1)}, bf16[4,2176]{1,0:T(4,128)(2,1)S(1)}, u32[]{:S(2)}, u32[]{:S(2)}) %collective-permute-start.1) | collective-permute-done | bytes 17440 | tf_op jit(solution)/shard_map/ppermute | solution.py:297
  12.2 1.6 %collective-permute-done = bf16[4,2176]{1,0:T(4,128)(2,1)S(1)} collective-permute-done((bf16[4,2176]{1,0:T(4,128)(2,1)S(1)}, bf16[4,2176]{1,0:T(4,128)(2,1)S(1)}, u32[]{:S(2)}, u32[]{:S(2)}) %collective-permute-start) | collective-permute-done | bytes 17440 | tf_op jit(solution)/shard_map/ppermute | solution.py:297
  13.9 3.0 %collective-permute-start.5 = (bf16[16,2176]{1,0:T(8,128)(2,1)S(1)}, bf16[16,2176]{1,0:T(8,128)(2,1)S(1)}, u32[]{:S(2)}, u32[]{:S(2)}) collective-permute-start(bf16[16,2176]{1,0:T(8,128)(2,1)S(1)} %pad_maximum_fusion), channel_id=1, source_target_pairs={{0,8},{1,9},{2,10},{3,11},{4,12},{5,13},{6,14},{7,15},{16,24},{17,... | collective-permute-start | bytes 208904 | tf_op jit(solution)/shard_map/ppermute | solution.py:298
  16.9 0.8 %collective-permute-start.4 = (bf16[16,2176]{1,0:T(8,128)(2,1)S(1)}, bf16[16,2176]{1,0:T(8,128)(2,1)S(1)}, u32[]{:S(2)}, u32[]{:S(2)}) collective-permute-start(bf16[16,2176]{1,0:T(8,128)(2,1)S(1)} %pad_maximum_fusion), channel_id=1, source_target_pairs={{0,24},{1,25},{2,26},{3,27},{4,28},{5,29},{6,30},{7,31},{16,0},{17... | collective-permute-start | bytes 208904 | tf_op jit(solution)/shard_map/ppermute | solution.py:298
  17.6 0.7 collective-permute-start.3
  18.3 0.3 collective-permute-done.5
  18.6 1.4 %collective-permute-done.4 = bf16[16,2176]{1,0:T(8,128)(2,1)S(1)} collective-permute-done((bf16[16,2176]{1,0:T(8,128)(2,1)S(1)}, bf16[16,2176]{1,0:T(8,128)(2,1)S(1)}, u32[]{:S(2)}, u32[]{:S(2)}) %collective-permute-start.4) | collective-permute-done | bytes 69664 | tf_op jit(solution)/shard_map/ppermute | solution.py:298
  20.0 2.2 %collective-permute-done.3 = bf16[16,2176]{1,0:T(8,128)(2,1)S(1)} collective-permute-done((bf16[16,2176]{1,0:T(8,128)(2,1)S(1)}, bf16[16,2176]{1,0:T(8,128)(2,1)S(1)}, u32[]{:S(2)}, u32[]{:S(2)}) %collective-permute-start.3) | collective-permute-done | bytes 69664 | tf_op jit(solution)/shard_map/ppermute | solution.py:298
  22.2 0.1 concatenate.8.m0
  22.4 2.8 %collective-permute-start.8 = (bf16[64,2176]{1,0:T(8,128)(2,1)S(1)}, bf16[64,2176]{1,0:T(8,128)(2,1)S(1)}, u32[]{:S(2)}, u32[]{:S(2)}) collective-permute-start(bf16[64,2176]{1,0:T(8,128)(2,1)S(1)} %concatenate.8.m0), channel_id=1, source_target_pairs={{0,4},{1,5},{2,6},{3,7},{4,0},{5,1},{6,2},{7,3},{16,20},{17,21},{1... | collective-permute-start | bytes 835592 | tf_op jit(solution)/shard_map/ppermute | solution.py:299
  25.2 0.9 %collective-permute-start.7 = (bf16[64,2176]{1,0:T(8,128)(2,1)S(1)}, bf16[64,2176]{1,0:T(8,128)(2,1)S(1)}, u32[]{:S(2)}, u32[]{:S(2)}) collective-permute-start(bf16[64,2176]{1,0:T(8,128)(2,1)S(1)} %concatenate.8.m0), channel_id=1, source_target_pairs={{0,6},{1,7},{2,0},{3,1},{4,2},{5,3},{6,4},{7,5},{16,22},{17,23},{1... | collective-permute-start | bytes 835592 | tf_op jit(solution)/shard_map/ppermute | solution.py:299
  26.1 0.6 collective-permute-start.6
  26.7 2.7 %collective-permute-done.8.m3 = bf16[64,2176]{1,0:T(8,128)(2,1)S(1)} collective-permute-done((bf16[64,2176]{1,0:T(8,128)(2,1)S(1)}, bf16[64,2176]{1,0:T(8,128)(2,1)S(1)}, u32[]{:S(2)}, u32[]{:S(2)}) %collective-permute-start.8) | collective-permute-done | bytes 278560 | tf_op jit(solution)/shard_map/ppermute | solution.py:299
  29.4 6.2 %collective-permute-done.7.m2 = bf16[64,2176]{1,0:T(8,128)(2,1)S(1)} collective-permute-done((bf16[64,2176]{1,0:T(8,128)(2,1)S(1)}, bf16[64,2176]{1,0:T(8,128)(2,1)S(1)}, u32[]{:S(2)}, u32[]{:S(2)}) %collective-permute-start.7) | collective-permute-done | bytes 278560 | tf_op jit(solution)/shard_map/ppermute | solution.py:299
  35.5 0.6 collective-permute-done.6.m1
  36.1 15.0 %shard_map.74 = (bf16[512,1152]{1,0:T(8,128)(2,1)S(1)}, bf16[512,1152]{1,0:T(8,128)(2,1)S(1)}) custom-call(bf16[64,2176]{1,0:T(8,128)(2,1)S(1)} %concatenate.8.m0, bf16[64,2176]{1,0:T(8,128)(2,1)S(1)} %collective-permute-done.6.m1, bf16[64,2176]{1,0:T(8,128)(2,1)S(1)} %collective-permute-done.7.m2, bf16[64,2176]{1,0:T(8,128)(2,1)S(1)} %collective-permute-done.8.m3, ...), custom_call_target="tpu_custom_call" | custom-call | tf_op jit(solution)/shard_map/pallas_call | solution.py:301
  51.1 3.3 %collective-permute-start.9 = (bf16[512,1152]{1,0:T(8,128)(2,1)S(1)}, bf16[512,1152]{1,0:T(8,128)(2,1)S(1)}, u32[]{:S(2)}, u32[]{:S(2)}) collective-permute-start(bf16[512,1152]{1,0:T(8,128)(2,1)S(1)} %get-tuple-element.10), channel_id=1, source_target_pairs={{0,1},{1,0},{2,3},{3,2},{4,5},{5,4},{6,7},{7,6},{16,17},{17,16},{1... | collective-permute-start | bytes 3538952 | tf_op jit(solution)/shard_map/ppermute | solution.py:318
  54.4 2.5 %collective-permute-done.9.bb = bf16[512,1152]{1,0:T(8,128)(2,1)S(1)} collective-permute-done((bf16[512,1152]{1,0:T(8,128)(2,1)S(1)}, bf16[512,1152]{1,0:T(8,128)(2,1)S(1)}, u32[]{:S(2)}, u32[]{:S(2)}) %collective-permute-start.9) | collective-permute-done | bytes 1179680 | tf_op jit(solution)/shard_map/ppermute | solution.py:318
  56.9 1.4 %shard_map.75 = (f32[2,512]{1,0:T(2,128)S(1)}, f32[8,512]{1,0:T(8,128)S(1)}) custom-call(bf16[512,1152]{1,0:T(8,128)(2,1)S(1)} %get-tuple-element.9.ba, bf16[512,1152]{1,0:T(8,128)(2,1)S(1)} %collective-permute-done.9.bb), custom_call_target="tpu_custom_call" | custom-call | tf_op jit(solution)/shard_map/pallas_call | solution.py:319
  58.3 11.5 %all_to_all.5 = f32[16,2,512]{2,1,0:T(2,128)S(1)} all-to-all(f32[16,2,512]{2,1,0:T(2,128)S(1)} %broadcast_in_dim.2), channel_id=1, replica_groups=mesh['pulse'=8,'tile'=16] {'tile'}, dimensions={0} | all-to-all | bytes 131072 | tf_op jit(solution)/shard_map/all_to_all | solution.py:327
  69.9 3.7 %shard_map.76 = bf16[2,128,4096]{2,1,0:T(8,128)(2,1)} custom-call(f32[2,512]{1,0:T(2,128)S(1)} %reduce_sum.9.g, f32[8,512]{1,0:T(8,128)S(1)} %get-tuple-element.12.meta, bf16[512,1152]{1,0:T(8,128)(2,1)S(1)} %get-tuple-element.9.ba, bf16[512,1152]{1,0:T(8,128)(2,1)S(1)} %collective-permute-done.9.bb), custom_call_target="tpu_custom_call" | custom-call | tf_op jit(solution)/shard_map/pallas_call | solution.py:328
  (3 shorter events, 0.1 us)
Async XLA Ops:
  0.8 0.8 %copy-start = (bf16[2,4,2048]{2,1,0:T(4,128)(2,1)S(1)}, bf16[2,4,2048]{2,1,0:T(4,128)(2,1)}, u32[]{:S(2)}) copy-start(bf16[2,4,2048]{2,1,0:T(4,128)(2,1)} %raw.1) | copy-start | bytes 98308
  1.5 0.7 copy-start.1
  2.2 0.7 copy-start.2
  2.8 0.7 copy-start.3
  3.5 0.7 copy-start.4
  5.1 6.0 %collective-permute-start.2 = (bf16[4,2176]{1,0:T(4,128)(2,1)S(1)}, bf16[4,2176]{1,0:T(4,128)(2,1)S(1)}, u32[]{:S(2)}, u32[]{:S(2)}) collective-permute-start(bf16[4,2176]{1,0:T(4,128)(2,1)S(1)} %shard_map.73), channel_id=1, source_target_pairs={{0,64},{1,65},{2,66},{3,67},{4,68},{5,69},{6,70},{7,71},{16,80},{1... | collective-permute-start | bytes 52232 | tf_op jit(solution)/shard_map/ppermute | solution.py:297
  9.6 2.6 %collective-permute-start.1 = (bf16[4,2176]{1,0:T(4,128)(2,1)S(1)}, bf16[4,2176]{1,0:T(4,128)(2,1)S(1)}, u32[]{:S(2)}, u32[]{:S(2)}) collective-permute-start(bf16[4,2176]{1,0:T(4,128)(2,1)S(1)} %shard_map.73), channel_id=1, source_target_pairs={{0,96},{1,97},{2,98},{3,99},{4,100},{5,101},{6,102},{7,103},{16,11... | collective-permute-start | bytes 52232 | tf_op jit(solution)/shard_map/ppermute | solution.py:297
  10.0 3.8 %collective-permute-start = (bf16[4,2176]{1,0:T(4,128)(2,1)S(1)}, bf16[4,2176]{1,0:T(4,128)(2,1)S(1)}, u32[]{:S(2)}, u32[]{:S(2)}) collective-permute-start(bf16[4,2176]{1,0:T(4,128)(2,1)S(1)} %shard_map.73), channel_id=1, source_target_pairs={{0,32},{1,33},{2,34},{3,35},{4,36},{5,37},{6,38},{7,39},{16,48},{1... | collective-permute-start | bytes 52232 | tf_op jit(solution)/shard_map/ppermute | solution.py:297
  13.9 4.7 %collective-permute-start.5 = (bf16[16,2176]{1,0:T(8,128)(2,1)S(1)}, bf16[16,2176]{1,0:T(8,128)(2,1)S(1)}, u32[]{:S(2)}, u32[]{:S(2)}) collective-permute-start(bf16[16,2176]{1,0:T(8,128)(2,1)S(1)} %pad_maximum_fusion), channel_id=1, source_target_pairs={{0,8},{1,9},{2,10},{3,11},{4,12},{5,13},{6,14},{7,15},{16,24},{17,... | collective-permute-start | bytes 208904 | tf_op jit(solution)/shard_map/ppermute | solution.py:298
  16.9 3.2 %collective-permute-start.4 = (bf16[16,2176]{1,0:T(8,128)(2,1)S(1)}, bf16[16,2176]{1,0:T(8,128)(2,1)S(1)}, u32[]{:S(2)}, u32[]{:S(2)}) collective-permute-start(bf16[16,2176]{1,0:T(8,128)(2,1)S(1)} %pad_maximum_fusion), channel_id=1, source_target_pairs={{0,24},{1,25},{2,26},{3,27},{4,28},{5,29},{6,30},{7,31},{16,0},{17... | collective-permute-start | bytes 208904 | tf_op jit(solution)/shard_map/ppermute | solution.py:298
  17.6 4.6 %collective-permute-start.3 = (bf16[16,2176]{1,0:T(8,128)(2,1)S(1)}, bf16[16,2176]{1,0:T(8,128)(2,1)S(1)}, u32[]{:S(2)}, u32[]{:S(2)}) collective-permute-start(bf16[16,2176]{1,0:T(8,128)(2,1)S(1)} %pad_maximum_fusion), channel_id=1, source_target_pairs={{0,16},{1,17},{2,18},{3,19},{4,20},{5,21},{6,22},{7,23},{16,8},{17... | collective-permute-start | bytes 208904 | tf_op jit(solution)/shard_map/ppermute | solution.py:298
  22.4 7.0 %collective-permute-start.8 = (bf16[64,2176]{1,0:T(8,128)(2,1)S(1)}, bf16[64,2176]{1,0:T(8,128)(2,1)S(1)}, u32[]{:S(2)}, u32[]{:S(2)}) collective-permute-start(bf16[64,2176]{1,0:T(8,128)(2,1)S(1)} %concatenate.8.m0), channel_id=1, source_target_pairs={{0,4},{1,5},{2,6},{3,7},{4,0},{5,1},{6,2},{7,3},{16,20},{17,21},{1... | collective-permute-start | bytes 835592 | tf_op jit(solution)/shard_map/ppermute | solution.py:299
  25.2 10.3 %collective-permute-start.7 = (bf16[64,2176]{1,0:T(8,128)(2,1)S(1)}, bf16[64,2176]{1,0:T(8,128)(2,1)S(1)}, u32[]{:S(2)}, u32[]{:S(2)}) collective-permute-start(bf16[64,2176]{1,0:T(8,128)(2,1)S(1)} %concatenate.8.m0), channel_id=1, source_target_pairs={{0,6},{1,7},{2,0},{3,1},{4,2},{5,3},{6,4},{7,5},{16,22},{17,23},{1... | collective-permute-start | bytes 835592 | tf_op jit(solution)/shard_map/ppermute | solution.py:299
  26.1 10.0 %collective-permute-start.6 = (bf16[64,2176]{1,0:T(8,128)(2,1)S(1)}, bf16[64,2176]{1,0:T(8,128)(2,1)S(1)}, u32[]{:S(2)}, u32[]{:S(2)}) collective-permute-start(bf16[64,2176]{1,0:T(8,128)(2,1)S(1)} %concatenate.8.m0), channel_id=1, source_target_pairs={{0,2},{1,3},{2,4},{3,5},{4,6},{5,7},{6,0},{7,1},{16,18},{17,19},{1... | collective-permute-start | bytes 835592 | tf_op jit(solution)/shard_map/ppermute | solution.py:299
  51.1 5.8 %collective-permute-start.9 = (bf16[512,1152]{1,0:T(8,128)(2,1)S(1)}, bf16[512,1152]{1,0:T(8,128)(2,1)S(1)}, u32[]{:S(2)}, u32[]{:S(2)}) collective-permute-start(bf16[512,1152]{1,0:T(8,128)(2,1)S(1)} %get-tuple-element.10), channel_id=1, source_target_pairs={{0,1},{1,0},{2,3},{3,2},{4,5},{5,4},{6,7},{7,6},{16,17},{17,16},{1... | collective-permute-start | bytes 3538952 | tf_op jit(solution)/shard_map/ppermute | solution.py:318

commit v2 on v0

v2 whole, which is shorter than its diff:
```python
import jax
import jax.numpy as jnp
from jax import lax
from jax.experimental import pallas as pl
from jax.experimental.pallas import tpu as pltpu
from jax.sharding import PartitionSpec as P

AXES = ("pulse", "tile")
WIN = 1024
UPS = 2048
BW = WIN + 128
ROWS = 128
CHUNK = 128
STEPS = (0, 1, 3, 2)
F32 = jnp.float32
BF16 = jnp.bfloat16
NT = (((1,), (1,)), ((), ()))
MIB = 1024 * 1024


def linear(z, y, x, core):
    return (z * 2 + y % 2) * 16 + ((y // 2) * 4 + x) * 2 + core


PLACES = [(z, y, x, c) for z in range(4) for y in range(4) for x in range(4) for c in range(2)]


def planes():
    groups = {}
    for z, y, x, c in PLACES:
        groups.setdefault((c, x if c == 0 else y), []).append(linear(z, y, x, c))
    return [groups[key] for key in sorted(groups)]


def along_last(k):
    return [
        (
            linear(z, y, x, c),
            linear(z, y, (x + k) % 4, c) if c == 0 else linear(z, (y + k) % 4, x, c),
        )
        for z, y, x, c in PLACES
    ]


def other_core():
    return [(linear(z, y, x, c), linear(z, y, x, 1 - c)) for z, y, x, c in PLACES]


def iota(shape, axis):
    return lax.broadcasted_iota(jnp.int32, shape, axis)


def window_kernel(order_h, off_h, fine_h, dop_h, band_h, raw_h, out, order, off, fine, dop, band, raw, sems):
    pairs = ((order_h, order), (off_h, off), (fine_h, fine), (dop_h, dop), (band_h, band), (raw_h, raw))
    copies = [pltpu.make_async_copy(a, b, sems.at[i]) for i, (a, b) in enumerate(pairs)]
    for copy in copies:
        copy.start()
    for copy in copies:
        copy.wait()
    x = jnp.concatenate([raw[0].astype(F32), raw[1].astype(F32)], 0)
    row = iota((8, WIN), 0)
    lane = iota((1, 128), 1)
    meta_row = iota((8, 128), 0)
    both = jnp.zeros((8, WIN), F32)
    meta = jnp.zeros((8, 128), jnp.int32)
    for j in range(4):
        k = order[0, j]
        y = pltpu.roll(x, lax.rem(UPS - off[k], UPS), 1)[:, :WIN]
        one_re = jnp.sum(jnp.where(row == k, y, 0.0), axis=0, keepdims=True)
        one_im = jnp.sum(jnp.where(row == k + 4, y, 0.0), axis=0, keepdims=True)
        both = jnp.where(row == j, one_re, jnp.where(row == j + 4, one_im, both))
        d = dop[k]
        v = jnp.where(lane == 1, fine[k], 0)
        v = jnp.where(lane == 2, d >> 5, v)
        v = jnp.where(lane == 3, d & 31, v)
        for t in range(16):
            b = band[k, t]
            v = jnp.where(lane == 16 + t, b >> 5, v)
            v = jnp.where(lane == 32 + t, b & 31, v)
        meta = jnp.where((meta_row & 3) == j, v, meta)
    both = both.astype(BF16)
    meta = meta.astype(F32).astype(BF16)
    for i in range(16):
        out[i, :, :WIN] = both
        out[i, :, WIN:] = meta


def band_kernel(m, filt, theirs, mine, w, prof, cut, starts_v, starts_s, sem):
    tile = lax.axis_index("tile")
    sibling = tile + 1 - 2 * lax.rem(tile, 2)
    lane8 = iota((8, 128), 1)
    row8 = iota((8, 128), 0)
    info = m[:, WIN:]
    want = jnp.where(row8 == 0, tile, sibling)
    pick = jnp.where(lane8 == want + 16, 32.0, jnp.where(lane8 == want + 32, 1.0, 0.0)).astype(BF16)
    starts_v[...] = lax.dot_general(pick, info, NT, preferred_element_type=F32).astype(jnp.int32)
    copy = pltpu.make_async_copy(starts_v, starts_s, sem)
    copy.start()
    k = iota((128, 256), 0)
    want = jnp.where(iota((128, 256), 1) < 128, tile, sibling)
    spread = jnp.where(k == want + 16, 32.0, jnp.where(k == want + 32, 1.0, 0.0)).astype(BF16)
    turns = jnp.dot(info, spread, preferred_element_type=F32).astype(jnp.int32) & 127

    sign = jnp.where(iota((8, WIN), 0) < 4, -1.0, 1.0)
    w[:, :WIN] = m[:, :WIN]
    for g in range(0, CHUNK, 16):
        v = m[g : g + 16, :WIN].astype(F32)
        top = pltpu.roll(v[:8], 4, 0) * sign
        low = pltpu.roll(v[8:], 4, 0) * sign
        w[g : g + 16, WIN:] = jnp.concatenate([top, low], 0).astype(BF16)
    for n in range(0, UPS, 512):
        f = filt[:, :, n : n + 512].reshape(2 * WIN, 512)
        r = jnp.dot(w[...], f, preferred_element_type=F32)
        for h in range(4):
            for g in range(16):
                at = g * 128 + (n // 128 + h) * 8
                prof[at : at + 8, :] = r[8 * g : 8 * g + 8, 128 * h : 128 * h + 128]
    copy.wait()
    for which, out in enumerate((theirs, mine)):
        for g in range(16):
            for j in range(4):
                start = starts_s[1 - which, 8 * g + j]
                turn = (128 - (start & 127)) & 127
                at = g * 128 + (start >> 7) * 8 + j
                re = pltpu.roll(prof[pl.ds(at, 8, 8), :], turn, 1)
                im = pltpu.roll(prof[pl.ds(at + 4, 8, 8), :], turn, 1)
                end = pltpu.roll(prof[pl.ds(at + 64, 2, 4), :], turn, 1)
                to = g * 72 + j
                cut[which, pl.ds(to, 8, 8), :] = re
                cut[which, pl.ds(to + 4, 8, 8), :] = im
                cut[which, pl.ds(to + 64, 2, 4), :] = end
    for which, out in enumerate((theirs, mine)):
        for pair in range(8):
            done = [[], []]
            for e in range(2):
                g = 2 * pair + e
                turn = turns[8 * g : 8 * g + 8, 128 * (1 - which) : 128 * (1 - which) + 128]
                inside = lane8 + turn < 128
                parts = [cut[which, g * 72 + 8 * c : g * 72 + 8 * c + 8, :] for c in range(9)]
                done[e] = [jnp.where(inside, parts[c], parts[c + 1]) for c in range(8)]
                meta = info[8 * g : 8 * g + 8].astype(F32)
                done[e].append(
                    jnp.where(lane8 == 0, parts[8], jnp.where(lane8 < 4, meta, 0.0))
                )
            for c in range(9):
                v = jnp.concatenate([done[0][c], done[1][c]], 0).astype(BF16)
                out[16 * pair : 16 * pair + 16, 128 * c : 128 * c + 128] = v


def positions():
    tile = lax.axis_index("tile")
    core = lax.rem(tile, 2)
    x = lax.rem(tile // 2, 4)
    y = tile // 8 * 2 + lax.rem(lax.axis_index("pulse"), 2)
    own = jnp.where(core == 0, x, y)
    other = jnp.where(core == 0, y, x)
    return [core * 4 + lax.rem(own + 4 - k, 4) for k in STEPS] + [
        (1 - core) * 4 + lax.rem(other + 4 - k, 4) for k in STEPS
    ]


def gradient_kernel(*refs):
    parts = refs[:8]
    g_out, meta_out, b = refs[8:11]
    place = refs[11]
    for i, part in enumerate(parts):
        b[CHUNK * i : CHUNK * (i + 1), :] = part[...]
    row8 = iota((8, 128), 0)
    lane8 = iota((8, 128), 1)
    pick = jnp.where(
        row8 == 0,
        jnp.where(lane8 == 1, 1.0, 0.0),
        jnp.where(row8 == 1, jnp.where(lane8 == 2, 32.0, jnp.where(lane8 == 3, 1.0, 0.0)), 0.0),
    ).astype(BF16)
    meta = lax.dot_general(pick, b[:, WIN:], NT, preferred_element_type=F32)
    for i in range(8):
        meta_out[0, i : i + 1, :] = meta[0:1, CHUNK * i : CHUNK * (i + 1)]
        meta_out[1, i : i + 1, :] = meta[1:2, CHUNK * i : CHUNK * (i + 1)]
    shift = meta[0:1] * 0.0625
    keep = jnp.where((iota((8, WIN), 1) & 7) == iota((8, WIN), 0), 1.0, 0.0)
    lhs = jnp.concatenate([keep, keep * shift], 0).astype(BF16)
    sums = jnp.dot(lhs, b[...], preferred_element_type=F32)
    s = sums[:8]
    t = sums[8:]
    inner = iota((8, BW), 1) < WIN
    x0 = s + pltpu.roll(t, BW - 1, 1) - t
    dr = pltpu.roll(s, BW - 1, 1) - s
    a = jnp.where(inner, 4.0 * x0 + 1.5 * dr, 0.0)
    d = jnp.where(inner, 1.5 * x0 + 0.875 * dr, 0.0)
    p = a - d + pltpu.roll(d, 1, 1)
    q = pltpu.roll(a, 1, 1) - a
    both = jnp.concatenate([p, q], 0)
    high = both.astype(BF16)
    low = (both - high.astype(F32)).astype(BF16)
    g = lax.dot_general(jnp.concatenate([high, low], 0), b[...], NT, preferred_element_type=F32)
    g = g[:16] + g[16:]
    g = g[:8] + g[8:] * shift
    j = iota((8, WIN), 1) & 3
    row = iota((8, WIN), 0)
    by_re = jnp.sum(jnp.where(row == j, g, 0.0), axis=0, keepdims=True)
    by_im = jnp.sum(jnp.where(row == j + 4, g, 0.0), axis=0, keepdims=True)
    even = (iota((1, WIN), 1) & 4) == 0
    swapped = jnp.where(even, pltpu.roll(by_im, WIN - 4, 1), -pltpu.roll(by_im, 4, 1))
    grads = by_re + swapped
    for i, at in enumerate(positions()):
        place[pl.ds(at, 1), :] = grads[:, CHUNK * i : CHUNK * (i + 1)]
    for t in range(16):
        g_out[t] = place[...]


def image_kernel(g_in, meta, b, out_h, total, lhs, xd, out, sems):
    total[...] = jnp.sum(g_in[...], axis=0)
    even8 = (iota((8, 128), 1) & 4) == 0
    local = jnp.concatenate([total[pl.ds(at, 1), :] for at in positions()], 0)
    g_re = jnp.where(even8, local, pltpu.roll(local, 4, 1))
    g_im = jnp.where(even8, pltpu.roll(local, 124, 1), local)
    inv = (512.0**-0.5) / jnp.sqrt(g_re * g_re + g_im * g_im + 1.0)
    c_re = jnp.where(even8, g_re, g_im) * inv
    c_im = jnp.where(even8, -g_im, g_re) * inv

    def wide(v):
        return jnp.concatenate([v[i : i + 1] for i in range(8)], 1)

    shift = wide(meta[0]) * 0.0625
    dop = wide(meta[1].astype(jnp.int32))
    c_re = wide(c_re)
    c_im = wide(c_im)
    pulse = lax.axis_index("pulse")
    step = 2.0 * jnp.pi / 1024.0
    coarse = (((iota((16, WIN), 0) * 8 + pulse * ROWS) * dop) & 1023).astype(F32) * step
    finer = ((iota((8, WIN), 0) * dop) & 1023).astype(F32) * step
    cu = jnp.cos(coarse)
    su = jnp.sin(coarse)
    cv = jnp.cos(finer)
    sv = jnp.sin(finer)
    vr = cv * c_re - sv * c_im
    vi = cv * c_im + sv * c_re
    for u in range(0, 16, 2):
        pair = []
        for e in range(2):
            ur = cu[u + e : u + e + 1]
            ui = su[u + e : u + e + 1]
            pair.append((ur * vr - ui * vi, ur * vi + ui * vr))
        at = 8 * u
        for z in range(2):
            v = jnp.concatenate([pair[0][z], pair[1][z]], 0)
            lhs[at + 128 * z : at + 128 * z + 16, :] = v.astype(BF16)
            lhs[at + 256 + 128 * z : at + 272 + 128 * z, :] = (v * shift).astype(BF16)
    uv = jnp.dot(lhs[...], b[...], preferred_element_type=F32)
    diff = pltpu.roll(uv, BW - 1, 1) - uv
    xd[:, :WIN] = (uv[:256] + diff[256:])[:, :WIN].astype(BF16)
    xd[:, WIN:] = diff[:256, :WIN].astype(BF16)
    k = iota((256, 512), 0)
    col = iota((256, 512), 1)
    quarter = (col & 3).astype(F32) * 0.25
    spread = jnp.where((k & 127) == (col >> 2), jnp.where(k < 128, 1.0, quarter), 0.0).astype(BF16)
    copies = []
    for j in range(8):
        at = 128 * j
        part = jnp.concatenate([xd[:, at : at + 128], xd[:, WIN + at : WIN + at + 128]], 1)
        res = jnp.dot(part, spread, preferred_element_type=F32).astype(BF16)
        out[0, :, 512 * j : 512 * j + 512] = res[:128]
        out[1, :, 512 * j : 512 * j + 512] = res[128:]
        block = (slice(None), slice(None), pl.ds(512 * j, 512))
        copies.append(pltpu.make_async_copy(out.at[block], out_h.at[block], sems.at[j]))
        copies[-1].start()
    for copy in copies:
        copy.wait()


def vmem():
    return pl.BlockSpec(memory_space=pltpu.VMEM)


def hbm():
    return pl.BlockSpec(memory_space=pltpu.HBM)


def params(mib):
    return pltpu.CompilerParams(vmem_limit_bytes=mib * MIB)


def cost(flops, size):
    return pl.CostEstimate(flops=flops, bytes_accessed=size, transcendentals=0)


def shards(raw, filt, range_off, fine, dop, pulse_order, band_idx):
    own = pl.pallas_call(
        window_kernel,
        out_shape=jax.ShapeDtypeStruct((16, 8, BW), BF16),
        in_specs=[hbm()] * 6,
        out_specs=vmem(),
        scratch_shapes=[
            pltpu.SMEM((1, 4), jnp.int32),
            pltpu.SMEM((4,), jnp.int32),
            pltpu.SMEM((4,), jnp.int32),
            pltpu.SMEM((4,), jnp.int32),
            pltpu.SMEM((4, 16), jnp.int32),
            pltpu.VMEM((2, 4, UPS), BF16),
            pltpu.SemaphoreType.DMA((6,)),
        ],
        compiler_params=params(8),
    )(pulse_order, range_off, fine, dop, band_idx.T, raw)
    plane = lax.all_to_all(
        own, AXES, split_axis=0, concat_axis=0, axis_index_groups=planes(), tiled=True
    ).reshape(CHUNK, BW)
    chunks = [plane] + [lax.ppermute(plane, AXES, along_last(k)) for k in STEPS[1:]]
    bands = pl.pallas_call(
        band_kernel,
        out_shape=[jax.ShapeDtypeStruct((CHUNK, BW), BF16)] * 2,
        in_specs=[vmem()] * 2,
        out_specs=[vmem()] * 2,
        scratch_shapes=[
            pltpu.VMEM((CHUNK, 2 * WIN), BF16),
            pltpu.VMEM((2048, 128), F32),
            pltpu.VMEM((2, 16 * 72, 128), F32),
            pltpu.VMEM((8, 128), jnp.int32),
            pltpu.SMEM((8, 128), jnp.int32),
            pltpu.SemaphoreType.DMA,
        ],
        compiler_params=params(12),
        cost_estimate=cost(2 * CHUNK * UPS * UPS, 8 * MIB),
    )
    mine = []
    given = []
    for chunk in chunks:
        theirs, ours = bands(chunk, filt)
        mine.append(ours)
        given.append(lax.ppermute(theirs, AXES, other_core()))
    partial, meta, b = pl.pallas_call(
        gradient_kernel,
        out_shape=[
            jax.ShapeDtypeStruct((16, 8, 128), F32),
            jax.ShapeDtypeStruct((2, 8, 128), F32),
            jax.ShapeDtypeStruct((WIN, BW), BF16),
        ],
        in_specs=[vmem()] * 8,
        out_specs=[vmem()] * 3,
        scratch_shapes=[pltpu.VMEM((8, 128), F32)],
        compiler_params=params(12),
    )(*mine, *given)
    grads = lax.all_to_all(partial, "tile", split_axis=0, concat_axis=0, tiled=True)
    return pl.pallas_call(
        image_kernel,
        out_shape=jax.ShapeDtypeStruct((2, ROWS, 4 * WIN), BF16),
        in_specs=[vmem()] * 3,
        out_specs=hbm(),
        scratch_shapes=[
            pltpu.VMEM((8, 128), F32),
            pltpu.VMEM((512, WIN), BF16),
            pltpu.VMEM((256, 2 * WIN), BF16),
            pltpu.VMEM((2, ROWS, 4 * WIN), BF16),
            pltpu.SemaphoreType.DMA((8,)),
        ],
        compiler_params=params(20),
    )(grads, meta, b)


def solution(mesh):
    return jax.shard_map(
        shards,
        mesh=mesh,
        in_specs=(
            P(None, AXES, None),
            P(),
            P(AXES),
            P(AXES),
            P(AXES),
            P(AXES, None),
            P(None, AXES),
        ),
        out_specs=P(None, "pulse", "tile"),
        check_vma=False,
    )
```

time: 918 us -> 61 us (0.07)
  blocking collectives: 471 us -> 28.1 us
  local copies, waits for them, and re-layouts: 215 us -> 7.44 us
  starting transfers between devices: 92.3 us -> 8.94 us
  other arithmetic: 74 us -> 0 us
  matrix products: 46 us -> 0 us
  Pallas kernels: 0 us -> 14.8 us
  between operations: 11.6 us -> 0.06 us
    all_gather x9 -> x0, blocking collectives: 364 us -> none  [the longest x1 178 us: shards(): lax.all_gather(pulse_order, ('pulse', 'tile'), axis=0, tiled=True)]
    gather x203 -> x0, local copies, waits for them, and re-layouts: 95.7 us -> none
    all_to_all x8 -> x0, starting transfers between devices: 92.3 us -> none  [the longest x4 51.4 us: shards(): lax.all_to_all(pieces, 'tile', split_axis=0, concat_axis=0, tiled=True)]
    unnamed x1 -> x0, blocking collectives: 62 us -> none
    reshape x12 -> x0, local copies, waits for them, and re-layouts: 48.2 us -> none  [the longest x4 22.9 us: interpolate(): first = jnp.repeat(first, 4, axis=-1)]
    dot_general x20 -> x0, matrix products: 46 us -> none  [the longest x4 11.9 us: compress(): jnp.dot(wi, filt[1], preferred_element_type=jnp.float32)]
    psum x1 -> x0, blocking collectives: 44.6 us -> none  [shards(): g_re, g_im = lax.psum((g_re, g_im), 'tile')]
    all_to_all x0 -> x2, blocking collectives: none -> 28.1 us  [the longest x1 16.1 us: shards(): lax.all_to_all(own, AXES, split_axis=0, concat_axis=0, axis_index_groups=...]
  transfers between devices with their start and end apart: 8 -> 7, of which waited for: 0 -> 1; matrix products, arithmetic and copies ran while one was open for 16% -> 0% of each run, Pallas kernels for 0% -> 15%
where the time goes in v2:
time: 61 us; the launch traced here: 60.6 us
  blocking collectives  28.1 us (46%)
  Pallas kernels  14.8 us (24%)
  starting transfers between devices  8.94 us (15%)
  local copies, waits for them, and re-layouts  7.44 us (12%)
  waiting for transfers between devices  1.21 us (2%)
    all_to_all x1, blocking collectives, shards(): lax.all_to_all(own, AXES, split_axis=0, concat_axis=0, axis_index_groups=...  16.1 us
    all_to_all x1, blocking collectives, shards(): lax.all_to_all(partial, 'tile', split_axis=0, concat_axis=0, tiled=True)  12 us
    pallas_call x4, Pallas kernels, shards(): theirs, ours = bands(chunk, filt)  9.25 us
    unnamed x16, local copies, waits for them, and re-layouts  7.44 us
    ppermute x4, starting transfers between devices, shards(): given.append(lax.ppermute(theirs, AXES, other_core()))  4.61 us
    ppermute x3, starting transfers between devices, shards(): lax.ppermute(plane, AXES, along_last(k))  4.33 us
    pallas_call x1, Pallas kernels, shards(): pl.pallas_call(image_kernel, out_shape=jax.ShapeDtypeStruct((2, ROWS, 4 *...  3.22 us
    pallas_call x1, Pallas kernels, shards(): pl.pallas_call(gradient_kernel, out_shape=[jax.ShapeDtypeStruct((16, 8, 1...  1.45 us
  transfers between devices with their start and end apart: 7, of which 1 were waited for; matrix products, arithmetic and copies ran while one was open for 0% of the time, Pallas kernels for 15%

profile of v2, /device:TPU:1, one launch (start us, length us, event | category | flops | bytes accessed | tf_op | source)
XLA Modules:
  0.0 60.6 jit_solution(12600672291976108671)
XLA Ops:
  0.0 0.0 copy-start.2
  0.0 0.8 %copy-done.2 = bf16[2,4,2048]{2,1,0:T(4,128)(2,1)S(1)} copy-done((bf16[2,4,2048]{2,1,0:T(4,128)(2,1)S(1)}, bf16[2,4,2048]{2,1,0:T(4,128)(2,1)}, u32[]{:S(2)}) %copy-start.2) | copy-done | bytes 32792
  0.8 0.0 copy-start.3
  0.8 0.7 %copy-done.3 = s32[16,4]{0,1:T(4,128)S(1)} copy-done((s32[16,4]{0,1:T(4,128)S(1)}, s32[16,4]{0,1:T(4,128)}, u32[]{:S(2)}) %copy-start.3) | copy-done | bytes 280
  1.4 0.0 copy-start.4
  1.4 0.7 %copy-done.4 = s32[1,4]{1,0:T(1,128)S(1)} copy-done((s32[1,4]{1,0:T(1,128)S(1)}, s32[1,4]{1,0:T(1,128)}, u32[]{:S(2)}) %copy-start.4) | copy-done | bytes 40
  2.1 0.0 copy-start.5
  2.1 0.7 %copy-done.5 = s32[4]{0:T(128)S(1)} copy-done((s32[4]{0:T(128)S(1)}, s32[4]{0:T(128)}, u32[]{:S(2)}) %copy-start.5) | copy-done | bytes 40
  2.8 0.0 copy-start.6
  2.8 0.7 %copy-done.6 = s32[4]{0:T(128)S(1)} copy-done((s32[4]{0:T(128)S(1)}, s32[4]{0:T(128)}, u32[]{:S(2)}) %copy-start.6) | copy-done | bytes 40
  3.4 0.0 copy-start.7
  3.4 0.7 %copy-done.7 = s32[4]{0:T(128)S(1)} copy-done((s32[4]{0:T(128)S(1)}, s32[4]{0:T(128)}, u32[]{:S(2)}) %copy-start.7) | copy-done | bytes 40
  4.1 0.9 %shard_map.73 = bf16[16,8,1152]{2,1,0:T(8,128)(2,1)S(1)} custom-call(s32[1,4]{1,0:T(1,128)S(1)} %copy-done.4, s32[4]{0:T(128)S(1)} %copy-done.5, s32[4]{0:T(128)S(1)} %copy-done.6, s32[4]{0:T(128)S(1)} %copy-done.7, s32[4,16]{1,0:T(4,128)S(1)} %bitcast.6, bf16[2,4,2048]{2,1,0:T(4,128)(2,1)S(1)} %copy-done.2), custom_call_target="tpu_custom_call" | custom-call | tf_op jit(solution)/shard_map/pallas_call | solution.py:288
  4.9 16.1 %all_to_all.10 = bf16[16,8,1152]{2,1,0:T(8,128)(2,1)S(1)} all-to-all(bf16[16,8,1152]{2,1,0:T(8,128)(2,1)S(1)} %shard_map.73), channel_id=1, replica_groups={{0,16,8,24,32,48,40,56,64,80,72,88,96,112,104,120},{2,18,10,26,34,50,42..., dimensions={0} | all-to-all | bytes 589824 | tf_op jit(solution)/shard_map/all_to_all | solution.py:304
  21.1 2.9 %collective-permute-start.2 = (bf16[128,1152]{1,0:T(8,128)(2,1)S(1)}, bf16[128,1152]{1,0:T(8,128)(2,1)S(1)}, u32[]{:S(2)}, u32[]{:S(2)}) collective-permute-start(bf16[128,1152]{1,0:T(8,128)(2,1)S(1)} %bitcast.2), channel_id=1, source_target_pairs={{0,4},{1,9},{2,6},{3,11},{4,0},{5,13},{6,2},{7,15},{16,20},{17,25}... | collective-permute-start | bytes 884744 | tf_op jit(solution)/shard_map/ppermute | solution.py:307
  23.9 0.8 %collective-permute-start.1 = (bf16[128,1152]{1,0:T(8,128)(2,1)S(1)}, bf16[128,1152]{1,0:T(8,128)(2,1)S(1)}, u32[]{:S(2)}, u32[]{:S(2)}) collective-permute-start(bf16[128,1152]{1,0:T(8,128)(2,1)S(1)} %bitcast.3), channel_id=1, source_target_pairs={{0,6},{1,25},{2,0},{3,27},{4,2},{5,29},{6,4},{7,31},{16,22},{17,1}... | collective-permute-start | bytes 884744 | tf_op jit(solution)/shard_map/ppermute | solution.py:307
  24.8 0.6 %collective-permute-start = (bf16[128,1152]{1,0:T(8,128)(2,1)S(1)}, bf16[128,1152]{1,0:T(8,128)(2,1)S(1)}, u32[]{:S(2)}, u32[]{:S(2)}) collective-permute-start(bf16[128,1152]{1,0:T(8,128)(2,1)S(1)} %bitcast.4), channel_id=1, source_target_pairs={{0,2},{1,17},{2,4},{3,19},{4,6},{5,21},{6,0},{7,23},{16,18},{17,9}... | collective-permute-start | bytes 884744 | tf_op jit(solution)/shard_map/ppermute | solution.py:307
  25.4 0.0 copy-start
  25.4 3.4 %copy-done = bf16[2,1024,2048]{2,1,0:T(8,128)(2,1)S(1)} copy-done((bf16[2,1024,2048]{2,1,0:T(8,128)(2,1)S(1)}, bf16[2,1024,2048]{2,1,0:T(8,128)(2,1)}, u32[]{:S(2)}) %copy-start) | copy-done | bytes 8388632
  28.8 0.0 copy-start.1
  28.8 2.3 %shard_map.74 = (bf16[128,1152]{1,0:T(8,128)(2,1)S(1)}, bf16[128,1152]{1,0:T(8,128)(2,1)S(1)}) custom-call(bf16[128,1152]{1,0:T(8,128)(2,1)S(1)} %bitcast.5, bf16[2,1024,2048]{2,1,0:T(8,128)(2,1)S(1)} %copy-done), custom_call_target="tpu_custom_call" | custom-call | flops 1073741824 | bytes 8388608 | tf_op jit(solution)/shard_map/pallas_call | solution.py:327
  31.1 2.9 %collective-permute-start.3 = (bf16[128,1152]{1,0:T(8,128)(2,1)S(1)}, bf16[128,1152]{1,0:T(8,128)(2,1)S(1)}, u32[]{:S(2)}, u32[]{:S(2)}) collective-permute-start(bf16[128,1152]{1,0:T(8,128)(2,1)S(1)} %get-tuple-element.20), channel_id=1, source_target_pairs={{0,1},{1,0},{2,3},{3,2},{4,5},{5,4},{6,7},{7,6},{16,17},{17,16},{1... | collective-permute-start | bytes 884744 | tf_op jit(solution)/shard_map/ppermute | solution.py:329
  34.0 0.0 collective-permute-done.2.m
  34.0 0.0 copy-done.1
  34.0 2.3 %shard_map.77 = (bf16[128,1152]{1,0:T(8,128)(2,1)S(1)}, bf16[128,1152]{1,0:T(8,128)(2,1)S(1)}) custom-call(bf16[128,1152]{1,0:T(8,128)(2,1)S(1)} %collective-permute-done.2.m, bf16[2,1024,2048]{2,1,0:T(8,128)(2,1)S(1)} %copy-done.1), custom_call_target="tpu_custom_call" | custom-call | flops 1073741824 | bytes 8388608 | tf_op jit(solution)/shard_map/pallas_call | solution.py:327
  36.3 1.0 %collective-permute-start.6 = (bf16[128,1152]{1,0:T(8,128)(2,1)S(1)}, bf16[128,1152]{1,0:T(8,128)(2,1)S(1)}, u32[]{:S(2)}, u32[]{:S(2)}) collective-permute-start(bf16[128,1152]{1,0:T(8,128)(2,1)S(1)} %get-tuple-element.23), channel_id=1, source_target_pairs={{0,1},{1,0},{2,3},{3,2},{4,5},{5,4},{6,7},{7,6},{16,17},{17,16},{1... | collective-permute-start | bytes 884744 | tf_op jit(solution)/shard_map/ppermute | solution.py:329
  37.4 0.0 collective-permute-done.1.m
  37.4 2.3 %shard_map.76 = (bf16[128,1152]{1,0:T(8,128)(2,1)S(1)}, bf16[128,1152]{1,0:T(8,128)(2,1)S(1)}) custom-call(bf16[128,1152]{1,0:T(8,128)(2,1)S(1)} %collective-permute-done.1.m, bf16[2,1024,2048]{2,1,0:T(8,128)(2,1)S(1)} %copy-done.1), custom_call_target="tpu_custom_call" | custom-call | flops 1073741824 | bytes 8388608 | tf_op jit(solution)/shard_map/pallas_call | solution.py:327
  39.7 0.1 collective-permute-start.5
  39.8 0.0 collective-permute-done.m
  39.8 2.3 %shard_map.75 = (bf16[128,1152]{1,0:T(8,128)(2,1)S(1)}, bf16[128,1152]{1,0:T(8,128)(2,1)S(1)}) custom-call(bf16[128,1152]{1,0:T(8,128)(2,1)S(1)} %collective-permute-done.m, bf16[2,1024,2048]{2,1,0:T(8,128)(2,1)S(1)} %copy-done.1), custom_call_target="tpu_custom_call" | custom-call | flops 1073741824 | bytes 8388608 | tf_op jit(solution)/shard_map/pallas_call | solution.py:327
  42.1 0.6 collective-permute-start.4
  42.7 0.0 collective-permute-done.3.refs_4_
  42.7 0.0 collective-permute-done.6.refs_7_
  42.7 0.0 collective-permute-done.5.refs_6_
  42.7 1.2 %collective-permute-done.4.refs_5_ = bf16[128,1152]{1,0:T(8,128)(2,1)S(1)} collective-permute-done((bf16[128,1152]{1,0:T(8,128)(2,1)S(1)}, bf16[128,1152]{1,0:T(8,128)(2,1)S(1)}, u32[]{:S(2)}, u32[]{:S(2)}) %collective-permute-start.4) | collective-permute-done | bytes 294944 | tf_op jit(solution)/shard_map/ppermute | solution.py:329
  43.9 1.4 %shard_map.78 = (f32[16,8,128]{2,1,0:T(8,128)S(1)}, f32[2,8,128]{2,1,0:T(8,128)S(1)}, bf16[1024,1152]{1,0:T(8,128)(2,1)S(1)}) custom-call(bf16[128,1152]{1,0:T(8,128)(2,1)S(1)} %get-tuple-element.16.refs_0_, bf16[128,1152]{1,0:T(8,128)(2,1)S(1)} %get-tuple-element.17.refs_1_, bf16[128,1152]{1,0:T(8,128)(2,1)S(1)} %get-tuple-element.18.refs_2_, ...), custom_call_target="tpu_custom_call" | custom-call | tf_op jit(solution)/shard_map/pallas_call | solution.py:330
  45.4 12.0 %all_to_all.11.g_in = f32[16,8,128]{2,1,0:T(8,128)S(1)} all-to-all(f32[16,8,128]{2,1,0:T(8,128)S(1)} %get-tuple-element.24), channel_id=1, replica_groups=mesh['pulse'=8,'tile'=16] {'tile'}, dimensions={0} | all-to-all | bytes 131072 | tf_op jit(solution)/shard_map/all_to_all | solution.py:342
  57.4 3.2 %shard_map.79 = bf16[2,128,4096]{2,1,0:T(8,128)(2,1)} custom-call(f32[16,8,128]{2,1,0:T(8,128)S(1)} %all_to_all.11.g_in, f32[2,8,128]{2,1,0:T(8,128)S(1)} %get-tuple-element.25.meta, bf16[1024,1152]{1,0:T(8,128)(2,1)S(1)} %get-tuple-element.26.b), custom_call_target="tpu_custom_call" | custom-call | tf_op jit(solution)/shard_map/pallas_call | solution.py:343
Async XLA Ops:
  0.0 0.8 %copy-start.2 = (bf16[2,4,2048]{2,1,0:T(4,128)(2,1)S(1)}, bf16[2,4,2048]{2,1,0:T(4,128)(2,1)}, u32[]{:S(2)}) copy-start(bf16[2,4,2048]{2,1,0:T(4,128)(2,1)} %raw_h.1) | copy-start | bytes 98308
  0.8 0.7 %copy-start.3 = (s32[16,4]{0,1:T(4,128)S(1)}, s32[16,4]{0,1:T(4,128)}, u32[]{:S(2)}) copy-start(s32[16,4]{0,1:T(4,128)} %param.13) | copy-start | bytes 772
  1.4 0.7 %copy-start.4 = (s32[1,4]{1,0:T(1,128)S(1)}, s32[1,4]{1,0:T(1,128)}, u32[]{:S(2)}) copy-start(s32[1,4]{1,0:T(1,128)} %order_h.1) | copy-start | bytes 52
  2.1 0.7 %copy-start.5 = (s32[4]{0:T(128)S(1)}, s32[4]{0:T(128)}, u32[]{:S(2)}) copy-start(s32[4]{0:T(128)} %off_h.1) | copy-start | bytes 52
  2.8 0.7 %copy-start.6 = (s32[4]{0:T(128)S(1)}, s32[4]{0:T(128)}, u32[]{:S(2)}) copy-start(s32[4]{0:T(128)} %fine_h.1) | copy-start | bytes 52
  3.4 0.7 %copy-start.7 = (s32[4]{0:T(128)S(1)}, s32[4]{0:T(128)}, u32[]{:S(2)}) copy-start(s32[4]{0:T(128)} %dop_h.1) | copy-start | bytes 52
  21.1 12.9 %collective-permute-start.2 = (bf16[128,1152]{1,0:T(8,128)(2,1)S(1)}, bf16[128,1152]{1,0:T(8,128)(2,1)S(1)}, u32[]{:S(2)}, u32[]{:S(2)}) collective-permute-start(bf16[128,1152]{1,0:T(8,128)(2,1)S(1)} %bitcast.2), channel_id=1, source_target_pairs={{0,4},{1,9},{2,6},{3,11},{4,0},{5,13},{6,2},{7,15},{16,20},{17,25}... | collective-permute-start | bytes 884744 | tf_op jit(solution)/shard_map/ppermute | solution.py:307
  23.9 13.4 %collective-permute-start.1 = (bf16[128,1152]{1,0:T(8,128)(2,1)S(1)}, bf16[128,1152]{1,0:T(8,128)(2,1)S(1)}, u32[]{:S(2)}, u32[]{:S(2)}) collective-permute-start(bf16[128,1152]{1,0:T(8,128)(2,1)S(1)} %bitcast.3), channel_id=1, source_target_pairs={{0,6},{1,25},{2,0},{3,27},{4,2},{5,29},{6,4},{7,31},{16,22},{17,1}... | collective-permute-start | bytes 884744 | tf_op jit(solution)/shard_map/ppermute | solution.py:307
  24.8 15.0 %collective-permute-start = (bf16[128,1152]{1,0:T(8,128)(2,1)S(1)}, bf16[128,1152]{1,0:T(8,128)(2,1)S(1)}, u32[]{:S(2)}, u32[]{:S(2)}) collective-permute-start(bf16[128,1152]{1,0:T(8,128)(2,1)S(1)} %bitcast.4), channel_id=1, source_target_pairs={{0,2},{1,17},{2,4},{3,19},{4,6},{5,21},{6,0},{7,23},{16,18},{17,9}... | collective-permute-start | bytes 884744 | tf_op jit(solution)/shard_map/ppermute | solution.py:307
  25.4 3.4 %copy-start = (bf16[2,1024,2048]{2,1,0:T(8,128)(2,1)S(1)}, bf16[2,1024,2048]{2,1,0:T(8,128)(2,1)}, u32[]{:S(2)}) copy-start(bf16[2,1024,2048]{2,1,0:T(8,128)(2,1)} %filt.7) | copy-start | bytes 25165828
  28.8 5.2 %copy-start.1 = (bf16[2,1024,2048]{2,1,0:T(8,128)(2,1)S(1)}, bf16[2,1024,2048]{2,1,0:T(8,128)(2,1)}, u32[]{:S(2)}) copy-start(bf16[2,1024,2048]{2,1,0:T(8,128)(2,1)} %filt.7) | copy-start | bytes 25165828
  31.1 11.6 %collective-permute-start.3 = (bf16[128,1152]{1,0:T(8,128)(2,1)S(1)}, bf16[128,1152]{1,0:T(8,128)(2,1)S(1)}, u32[]{:S(2)}, u32[]{:S(2)}) collective-permute-start(bf16[128,1152]{1,0:T(8,128)(2,1)S(1)} %get-tuple-element.20), channel_id=1, source_target_pairs={{0,1},{1,0},{2,3},{3,2},{4,5},{5,4},{6,7},{7,6},{16,17},{17,16},{1... | collective-permute-start | bytes 884744 | tf_op jit(solution)/shard_map/ppermute | solution.py:329
  36.3 6.4 %collective-permute-start.6 = (bf16[128,1152]{1,0:T(8,128)(2,1)S(1)}, bf16[128,1152]{1,0:T(8,128)(2,1)S(1)}, u32[]{:S(2)}, u32[]{:S(2)}) collective-permute-start(bf16[128,1152]{1,0:T(8,128)(2,1)S(1)} %get-tuple-element.23), channel_id=1, source_target_pairs={{0,1},{1,0},{2,3},{3,2},{4,5},{5,4},{6,7},{7,6},{16,17},{17,16},{1... | collective-permute-start | bytes 884744 | tf_op jit(solution)/shard_map/ppermute | solution.py:329
  39.7 3.0 %collective-permute-start.5 = (bf16[128,1152]{1,0:T(8,128)(2,1)S(1)}, bf16[128,1152]{1,0:T(8,128)(2,1)S(1)}, u32[]{:S(2)}, u32[]{:S(2)}) collective-permute-start(bf16[128,1152]{1,0:T(8,128)(2,1)S(1)} %get-tuple-element.22), channel_id=1, source_target_pairs={{0,1},{1,0},{2,3},{3,2},{4,5},{5,4},{6,7},{7,6},{16,17},{17,16},{1... | collective-permute-start | bytes 884744 | tf_op jit(solution)/shard_map/ppermute | solution.py:329
  42.1 1.8 %collective-permute-start.4 = (bf16[128,1152]{1,0:T(8,128)(2,1)S(1)}, bf16[128,1152]{1,0:T(8,128)(2,1)S(1)}, u32[]{:S(2)}, u32[]{:S(2)}) collective-permute-start(bf16[128,1152]{1,0:T(8,128)(2,1)S(1)} %get-tuple-element.21), channel_id=1, source_target_pairs={{0,1},{1,0},{2,3},{3,2},{4,5},{5,4},{6,7},{7,6},{16,17},{17,16},{1... | collective-permute-start | bytes 884744 | tf_op jit(solution)/shard_map/ppermute | solution.py:329

commit v3 on v2

--- a/solution.py
+++ b/solution.py
@@ -16,6 +16,7 @@
 BF16 = jnp.bfloat16
 NT = (((1,), (1,)), ((), ()))
 MIB = 1024 * 1024
+FIRST = 42
 
 
 def linear(z, y, x, core):
@@ -85,7 +86,16 @@
         out[i, :, WIN:] = meta
 
 
-def band_kernel(m, filt, theirs, mine, w, prof, cut, starts_v, starts_s, sem):
+def first_band_kernel(m, filt_h, theirs, mine, filt, w, prof, cut, starts_v, starts_s, sem, sems):
+    copies = []
+    for i in range(4):
+        block = (slice(None), slice(None), pl.ds(512 * i, 512))
+        copies.append(pltpu.make_async_copy(filt_h.at[block], filt.at[block], sems.at[i]))
+        copies[-1].start()
+    band_kernel(m, filt, theirs, mine, w, prof, cut, starts_v, starts_s, sem, copies)
+
+
+def band_kernel(m, filt, theirs, mine, w, prof, cut, starts_v, starts_s, sem, copies=None):
     tile = lax.axis_index("tile")
     sibling = tile + 1 - 2 * lax.rem(tile, 2)
     lane8 = iota((8, 128), 1)
@@ -109,6 +119,8 @@
         low = pltpu.roll(v[8:], 4, 0) * sign
         w[g : g + 16, WIN:] = jnp.concatenate([top, low], 0).astype(BF16)
     for n in range(0, UPS, 512):
+        if copies:
+            copies[n // 512].wait()
         f = filt[:, :, n : n + 512].reshape(2 * WIN, 512)
         r = jnp.dot(w[...], f, preferred_element_type=F32)
         for h in range(4):
@@ -299,32 +311,47 @@
             pltpu.VMEM((2, 4, UPS), BF16),
             pltpu.SemaphoreType.DMA((6,)),
         ],
-        compiler_params=params(8),
+        compiler_params=params(60),
     )(pulse_order, range_off, fine, dop, band_idx.T, raw)
     plane = lax.all_to_all(
         own, AXES, split_axis=0, concat_axis=0, axis_index_groups=planes(), tiled=True
     ).reshape(CHUNK, BW)
     chunks = [plane] + [lax.ppermute(plane, AXES, along_last(k)) for k in STEPS[1:]]
+    band = jax.ShapeDtypeStruct((CHUNK, BW), BF16)
+    scratch = [
+        pltpu.VMEM((CHUNK, 2 * WIN), BF16),
+        pltpu.VMEM((2048, 128), F32),
+        pltpu.VMEM((2, 16 * 72, 128), F32),
+        pltpu.VMEM((8, 128), jnp.int32),
+        pltpu.SMEM((8, 128), jnp.int32),
+        pltpu.SemaphoreType.DMA,
+    ]
+    first_bands = pl.pallas_call(
+        first_band_kernel,
+        out_shape=[band, band, jax.ShapeDtypeStruct(filt.shape, BF16)],
+        in_specs=[vmem(), hbm()],
+        out_specs=[vmem()] * 3,
+        scratch_shapes=scratch + [pltpu.SemaphoreType.DMA((4,))],
+        compiler_params=params(FIRST),
+        cost_estimate=cost(2 * CHUNK * UPS * UPS, 8 * MIB),
+    )
     bands = pl.pallas_call(
         band_kernel,
-        out_shape=[jax.ShapeDtypeStruct((CHUNK, BW), BF16)] * 2,
+        out_shape=[band, band],
         in_specs=[vmem()] * 2,
         out_specs=[vmem()] * 2,
-        scratch_shapes=[
-            pltpu.VMEM((CHUNK, 2 * WIN), BF16),
-            pltpu.VMEM((2048, 128), F32),
-            pltpu.VMEM((2, 16 * 72, 128), F32),
-            pltpu.VMEM((8, 128), jnp.int32),
-            pltpu.SMEM((8, 128), jnp.int32),
-            pltpu.SemaphoreType.DMA,
-        ],
+        scratch_shapes=scratch,
         compiler_params=params(12),
         cost_estimate=cost(2 * CHUNK * UPS * UPS, 8 * MIB),
     )
     mine = []
     given = []
+    filt_v = None
     for chunk in chunks:
-        theirs, ours = bands(chunk, filt)
+        if filt_v is None:
+            theirs, ours, filt_v = first_bands(chunk, filt)
+        else:
+            theirs, ours = bands(chunk, filt_v)
         mine.append(ours)
         given.append(lax.ppermute(theirs, AXES, other_core()))
     partial, meta, b = pl.pallas_call(

time: 61 us -> 55.3 us (0.907)
  local copies, waits for them, and re-layouts: 7.44 us -> 0 us
  Pallas kernels: 14.8 us -> 18 us
  blocking collectives: 28.1 us -> 26.3 us
    unnamed x16 -> x0, local copies, waits for them, and re-layouts: 7.44 us -> none
    pallas_call x4, Pallas kernels: 9.25 us -> 11.6 us  [the longest x3 6.94 us: shards(): theirs, ours = bands(chunk, filt_v)]
    all_to_all x1, blocking collectives: 12 us -> 9.93 us  [shards(): lax.all_to_all(partial, 'tile', split_axis=0, concat_axis=0, tiled=True)]
    pallas_call x1, Pallas kernels: 0.87 us -> 1.76 us  [shards(): pl.pallas_call(window_kernel, out_shape=jax.ShapeDtypeStruct((16, 8, BW),...]
  transfers between devices with their start and end apart: 7 -> 7, of which waited for: 1 -> 1; matrix products, arithmetic and copies ran while one was open for 0% -> 0% of each run, Pallas kernels for 15% -> 21%
where the time goes in v3:
time: 55.3 us; the launch traced here: 55 us
  blocking collectives  26.3 us (48%)
  Pallas kernels  18 us (33%)
  starting transfers between devices  9.16 us (17%)
  waiting for transfers between devices  1.55 us (3%)
    all_to_all x1, blocking collectives, shards(): lax.all_to_all(own, AXES, split_axis=0, concat_axis=0, axis_index_groups=...  16.3 us
    all_to_all x1, blocking collectives, shards(): lax.all_to_all(partial, 'tile', split_axis=0, concat_axis=0, tiled=True)  9.93 us
    pallas_call x3, Pallas kernels, shards(): theirs, ours = bands(chunk, filt_v)  6.94 us
    ppermute x4, starting transfers between devices, shards(): given.append(lax.ppermute(theirs, AXES, other_core()))  4.83 us
    pallas_call x1, Pallas kernels, shards(): theirs, ours, filt_v = first_bands(chunk, filt)  4.62 us
    ppermute x3, starting transfers between devices, shards(): lax.ppermute(plane, AXES, along_last(k))  4.33 us
    pallas_call x1, Pallas kernels, shards(): pl.pallas_call(image_kernel, out_shape=jax.ShapeDtypeStruct((2, ROWS, 4 *...  3.2 us
    pallas_call x1, Pallas kernels, shards(): pl.pallas_call(window_kernel, out_shape=jax.ShapeDtypeStruct((16, 8, BW),...  1.76 us
  transfers between devices with their start and end apart: 7, of which 1 were waited for; matrix products, arithmetic and copies ran while one was open for 0% of the time, Pallas kernels for 21%

profile of v3, /device:TPU:1, one launch (start us, length us, event | category | flops | bytes accessed | tf_op | source)
XLA Modules:
  0.0 55.0 jit_solution(17672526951571423513)
XLA Ops:
  0.0 1.8 %shard_map.73 = bf16[16,8,1152]{2,1,0:T(8,128)(2,1)} custom-call(s32[1,4]{1,0:T(1,128)} %order_h.1, s32[4]{0:T(128)} %off_h.1, s32[4]{0:T(128)} %fine_h.1, s32[4]{0:T(128)} %dop_h.1, s32[4,16]{1,0:T(4,128)} %bitcast.6, bf16[2,4,2048]{2,1,0:T(4,128)(2,1)} %raw_h.1), custom_call_target="tpu_custom_call" | custom-call | tf_op jit(solution)/shard_map/pallas_call | solution.py:300
  1.8 16.3 %all_to_all.10 = bf16[16,8,1152]{2,1,0:T(8,128)(2,1)S(1)} all-to-all(bf16[16,8,1152]{2,1,0:T(8,128)(2,1)} %shard_map.73), channel_id=1, replica_groups={{0,16,8,24,32,48,40,56,64,80,72,88,96,112,104,120},{2,18,10,26,34,50,42..., dimensions={0} | all-to-all | bytes 589824 | tf_op jit(solution)/shard_map/all_to_all | solution.py:316
  18.1 2.8 %collective-permute-start.1 = (bf16[128,1152]{1,0:T(8,128)(2,1)S(1)}, bf16[128,1152]{1,0:T(8,128)(2,1)S(1)}, u32[]{:S(2)}, u32[]{:S(2)}) collective-permute-start(bf16[128,1152]{1,0:T(8,128)(2,1)S(1)} %bitcast.2), channel_id=1, source_target_pairs={{0,6},{1,25},{2,0},{3,27},{4,2},{5,29},{6,4},{7,31},{16,22},{17,1}... | collective-permute-start | bytes 884744 | tf_op jit(solution)/shard_map/ppermute | solution.py:319
  20.9 0.0 collective-permute-start
  20.9 1.6 %collective-permute-start.2 = (bf16[128,1152]{1,0:T(8,128)(2,1)S(1)}, bf16[128,1152]{1,0:T(8,128)(2,1)S(1)}, u32[]{:S(2)}, u32[]{:S(2)}) collective-permute-start(bf16[128,1152]{1,0:T(8,128)(2,1)S(1)} %bitcast.4), channel_id=1, source_target_pairs={{0,4},{1,9},{2,6},{3,11},{4,0},{5,13},{6,2},{7,15},{16,20},{17,25}... | collective-permute-start | bytes 884744 | tf_op jit(solution)/shard_map/ppermute | solution.py:319
  22.4 4.6 %shard_map.74 = (bf16[128,1152]{1,0:T(8,128)(2,1)S(1)}, bf16[128,1152]{1,0:T(8,128)(2,1)S(1)}, bf16[2,1024,2048]{2,1,0:T(8,128)(2,1)S(1)}) custom-call(bf16[128,1152]{1,0:T(8,128)(2,1)S(1)} %bitcast.5, bf16[2,1024,2048]{2,1,0:T(8,128)(2,1)} %filt_h.1), custom_call_target="tpu_custom_call" | custom-call | flops 1073741824 | bytes 8388608 | tf_op jit(solution)/shard_map/pallas_call | solution.py:352
  27.1 2.9 %collective-permute-start.3 = (bf16[128,1152]{1,0:T(8,128)(2,1)S(1)}, bf16[128,1152]{1,0:T(8,128)(2,1)S(1)}, u32[]{:S(2)}, u32[]{:S(2)}) collective-permute-start(bf16[128,1152]{1,0:T(8,128)(2,1)S(1)} %get-tuple-element.22), channel_id=1, source_target_pairs={{0,1},{1,0},{2,3},{3,2},{4,5},{5,4},{6,7},{7,6},{16,17},{17,16},{1... | collective-permute-start | bytes 884744 | tf_op jit(solution)/shard_map/ppermute | solution.py:356
  30.0 0.0 collective-permute-done.1.m
  30.0 2.3 %shard_map.76 = (bf16[128,1152]{1,0:T(8,128)(2,1)S(1)}, bf16[128,1152]{1,0:T(8,128)(2,1)S(1)}) custom-call(bf16[128,1152]{1,0:T(8,128)(2,1)S(1)} %collective-permute-done.1.m, bf16[2,1024,2048]{2,1,0:T(8,128)(2,1)S(1)} %get-tuple-element.18.filt), custom_call_target="tpu_custom_call" | custom-call | flops 1073741824 | bytes 8388608 | tf_op jit(solution)/shard_map/pallas_call | solution.py:354
  32.3 0.1 collective-permute-start.5
  32.4 0.0 collective-permute-done.m
  32.4 2.3 %shard_map.75 = (bf16[128,1152]{1,0:T(8,128)(2,1)S(1)}, bf16[128,1152]{1,0:T(8,128)(2,1)S(1)}) custom-call(bf16[128,1152]{1,0:T(8,128)(2,1)S(1)} %collective-permute-done.m, bf16[2,1024,2048]{2,1,0:T(8,128)(2,1)S(1)} %get-tuple-element.18.filt), custom_call_target="tpu_custom_call" | custom-call | flops 1073741824 | bytes 8388608 | tf_op jit(solution)/shard_map/pallas_call | solution.py:354
  34.7 1.7 %collective-permute-start.4 = (bf16[128,1152]{1,0:T(8,128)(2,1)S(1)}, bf16[128,1152]{1,0:T(8,128)(2,1)S(1)}, u32[]{:S(2)}, u32[]{:S(2)}) collective-permute-start(bf16[128,1152]{1,0:T(8,128)(2,1)S(1)} %get-tuple-element.23), channel_id=1, source_target_pairs={{0,1},{1,0},{2,3},{3,2},{4,5},{5,4},{6,7},{7,6},{16,17},{17,16},{1... | collective-permute-start | bytes 884744 | tf_op jit(solution)/shard_map/ppermute | solution.py:356
  36.4 0.0 collective-permute-done.2.m
  36.5 2.3 %shard_map.77 = (bf16[128,1152]{1,0:T(8,128)(2,1)S(1)}, bf16[128,1152]{1,0:T(8,128)(2,1)S(1)}) custom-call(bf16[128,1152]{1,0:T(8,128)(2,1)S(1)} %collective-permute-done.2.m, bf16[2,1024,2048]{2,1,0:T(8,128)(2,1)S(1)} %get-tuple-element.18.filt), custom_call_target="tpu_custom_call" | custom-call | flops 1073741824 | bytes 8388608 | tf_op jit(solution)/shard_map/pallas_call | solution.py:354
  38.8 0.1 collective-permute-start.6
  38.9 0.0 collective-permute-done.3.refs_4_
  38.9 0.0 collective-permute-done.5.refs_6_
  38.9 0.0 collective-permute-done.4.refs_5_
  38.9 1.5 %collective-permute-done.6.refs_7_ = bf16[128,1152]{1,0:T(8,128)(2,1)S(1)} collective-permute-done((bf16[128,1152]{1,0:T(8,128)(2,1)S(1)}, bf16[128,1152]{1,0:T(8,128)(2,1)S(1)}, u32[]{:S(2)}, u32[]{:S(2)}) %collective-permute-start.6) | collective-permute-done | bytes 294944 | tf_op jit(solution)/shard_map/ppermute | solution.py:356
  40.4 1.4 %shard_map.78 = (f32[16,8,128]{2,1,0:T(8,128)S(1)}, f32[2,8,128]{2,1,0:T(8,128)S(1)}, bf16[1024,1152]{1,0:T(8,128)(2,1)S(1)}) custom-call(bf16[128,1152]{1,0:T(8,128)(2,1)S(1)} %get-tuple-element.17.refs_0_, bf16[128,1152]{1,0:T(8,128)(2,1)S(1)} %get-tuple-element.19.refs_1_, bf16[128,1152]{1,0:T(8,128)(2,1)S(1)} %get-tuple-element.20.refs_2_, ...), custom_call_target="tpu_custom_call" | custom-call | tf_op jit(solution)/shard_map/pallas_call | solution.py:357
  41.9 9.9 %all_to_all.11.g_in = f32[16,8,128]{2,1,0:T(8,128)S(1)} all-to-all(f32[16,8,128]{2,1,0:T(8,128)S(1)} %get-tuple-element.26), channel_id=1, replica_groups=mesh['pulse'=8,'tile'=16] {'tile'}, dimensions={0} | all-to-all | bytes 131072 | tf_op jit(solution)/shard_map/all_to_all | solution.py:369
  51.8 3.2 %shard_map.79 = bf16[2,128,4096]{2,1,0:T(8,128)(2,1)} custom-call(f32[16,8,128]{2,1,0:T(8,128)S(1)} %all_to_all.11.g_in, f32[2,8,128]{2,1,0:T(8,128)S(1)} %get-tuple-element.27.meta, bf16[1024,1152]{1,0:T(8,128)(2,1)S(1)} %get-tuple-element.28.b), custom_call_target="tpu_custom_call" | custom-call | tf_op jit(solution)/shard_map/pallas_call | solution.py:370
Async XLA Ops:
  18.1 11.9 %collective-permute-start.1 = (bf16[128,1152]{1,0:T(8,128)(2,1)S(1)}, bf16[128,1152]{1,0:T(8,128)(2,1)S(1)}, u32[]{:S(2)}, u32[]{:S(2)}) collective-permute-start(bf16[128,1152]{1,0:T(8,128)(2,1)S(1)} %bitcast.2), channel_id=1, source_target_pairs={{0,6},{1,25},{2,0},{3,27},{4,2},{5,29},{6,4},{7,31},{16,22},{17,1}... | collective-permute-start | bytes 884744 | tf_op jit(solution)/shard_map/ppermute | solution.py:319
  20.9 11.5 %collective-permute-start = (bf16[128,1152]{1,0:T(8,128)(2,1)S(1)}, bf16[128,1152]{1,0:T(8,128)(2,1)S(1)}, u32[]{:S(2)}, u32[]{:S(2)}) collective-permute-start(bf16[128,1152]{1,0:T(8,128)(2,1)S(1)} %bitcast.3), channel_id=1, source_target_pairs={{0,2},{1,17},{2,4},{3,19},{4,6},{5,21},{6,0},{7,23},{16,18},{17,9}... | collective-permute-start | bytes 884744 | tf_op jit(solution)/shard_map/ppermute | solution.py:319
  20.9 15.6 %collective-permute-start.2 = (bf16[128,1152]{1,0:T(8,128)(2,1)S(1)}, bf16[128,1152]{1,0:T(8,128)(2,1)S(1)}, u32[]{:S(2)}, u32[]{:S(2)}) collective-permute-start(bf16[128,1152]{1,0:T(8,128)(2,1)S(1)} %bitcast.4), channel_id=1, source_target_pairs={{0,4},{1,9},{2,6},{3,11},{4,0},{5,13},{6,2},{7,15},{16,20},{17,25}... | collective-permute-start | bytes 884744 | tf_op jit(solution)/shard_map/ppermute | solution.py:319
  27.1 11.8 %collective-permute-start.3 = (bf16[128,1152]{1,0:T(8,128)(2,1)S(1)}, bf16[128,1152]{1,0:T(8,128)(2,1)S(1)}, u32[]{:S(2)}, u32[]{:S(2)}) collective-permute-start(bf16[128,1152]{1,0:T(8,128)(2,1)S(1)} %get-tuple-element.22), channel_id=1, source_target_pairs={{0,1},{1,0},{2,3},{3,2},{4,5},{5,4},{6,7},{7,6},{16,17},{17,16},{1... | collective-permute-start | bytes 884744 | tf_op jit(solution)/shard_map/ppermute | solution.py:356
  32.3 6.6 %collective-permute-start.5 = (bf16[128,1152]{1,0:T(8,128)(2,1)S(1)}, bf16[128,1152]{1,0:T(8,128)(2,1)S(1)}, u32[]{:S(2)}, u32[]{:S(2)}) collective-permute-start(bf16[128,1152]{1,0:T(8,128)(2,1)S(1)} %get-tuple-element.24), channel_id=1, source_target_pairs={{0,1},{1,0},{2,3},{3,2},{4,5},{5,4},{6,7},{7,6},{16,17},{17,16},{1... | collective-permute-start | bytes 884744 | tf_op jit(solution)/shard_map/ppermute | solution.py:356
  34.7 4.2 %collective-permute-start.4 = (bf16[128,1152]{1,0:T(8,128)(2,1)S(1)}, bf16[128,1152]{1,0:T(8,128)(2,1)S(1)}, u32[]{:S(2)}, u32[]{:S(2)}) collective-permute-start(bf16[128,1152]{1,0:T(8,128)(2,1)S(1)} %get-tuple-element.23), channel_id=1, source_target_pairs={{0,1},{1,0},{2,3},{3,2},{4,5},{5,4},{6,7},{7,6},{16,17},{17,16},{1... | collective-permute-start | bytes 884744 | tf_op jit(solution)/shard_map/ppermute | solution.py:356
  38.8 1.7 %collective-permute-start.6 = (bf16[128,1152]{1,0:T(8,128)(2,1)S(1)}, bf16[128,1152]{1,0:T(8,128)(2,1)S(1)}, u32[]{:S(2)}, u32[]{:S(2)}) collective-permute-start(bf16[128,1152]{1,0:T(8,128)(2,1)S(1)} %get-tuple-element.25), channel_id=1, source_target_pairs={{0,1},{1,0},{2,3},{3,2},{4,5},{5,4},{6,7},{7,6},{16,17},{17,16},{1... | collective-permute-start | bytes 884744 | tf_op jit(solution)/shard_map/ppermute | solution.py:356

commit v4 on v3

--- a/solution.py
+++ b/solution.py
@@ -11,6 +11,7 @@
 BW = WIN + 128
 ROWS = 128
 CHUNK = 128
+EARLY = 7 * CHUNK
 STEPS = (0, 1, 3, 2)
 F32 = jnp.float32
 BF16 = jnp.bfloat16
@@ -45,6 +46,13 @@
 
 def other_core():
     return [(linear(z, y, x, c), linear(z, y, x, 1 - c)) for z, y, x, c in PLACES]
+
+
+def near():
+    groups = {}
+    for z, y, x, c in PLACES:
+        groups.setdefault((z, y in (0, 3), c), []).append(linear(z, y, x, c))
+    return [groups[key] for key in sorted(groups)]
 
 
 def iota(shape, axis):
@@ -171,12 +179,7 @@
     ]
 
 
-def gradient_kernel(*refs):
-    parts = refs[:8]
-    g_out, meta_out, b = refs[8:11]
-    place = refs[11]
-    for i, part in enumerate(parts):
-        b[CHUNK * i : CHUNK * (i + 1), :] = part[...]
+def lane_info(b):
     row8 = iota((8, 128), 0)
     lane8 = iota((8, 128), 1)
     pick = jnp.where(
@@ -184,14 +187,35 @@
         jnp.where(lane8 == 1, 1.0, 0.0),
         jnp.where(row8 == 1, jnp.where(lane8 == 2, 32.0, jnp.where(lane8 == 3, 1.0, 0.0)), 0.0),
     ).astype(BF16)
-    meta = lax.dot_general(pick, b[:, WIN:], NT, preferred_element_type=F32)
+    return lax.dot_general(pick, b, NT, preferred_element_type=F32)
+
+
+def block_rows(shift):
+    size = shift.shape[1]
+    keep = jnp.where((iota((8, size), 1) & 7) == iota((8, size), 0), 1.0, 0.0)
+    return jnp.concatenate([keep, keep * shift], 0).astype(BF16)
+
+
+def sum_kernel(*refs):
+    parts = refs[:7]
+    sums, info, b = refs[7:]
+    for i, part in enumerate(parts):
+        b[CHUNK * i : CHUNK * (i + 1), :] = part[...]
+    b[EARLY:, :] = jnp.zeros((CHUNK, BW), BF16)
+    info[...] = lane_info(b[:EARLY, WIN:])
+    lhs = block_rows(info[0:1] * 0.0625)
+    sums[...] = jnp.dot(lhs, b[:EARLY], preferred_element_type=F32)
+
+
+def gradient_kernel(last, early, info, b_in, g_out, meta_out, b, place):
+    b[EARLY:, :] = last[...]
+    late = lane_info(last[:, WIN:])
+    meta = jnp.concatenate([info[0:2], late[0:2]], 1)
     for i in range(8):
-        meta_out[0, i : i + 1, :] = meta[0:1, CHUNK * i : CHUNK * (i + 1)]
-        meta_out[1, i : i + 1, :] = meta[1:2, CHUNK * i : CHUNK * (i + 1)]
+        for e in range(2):
+            meta_out[e, i : i + 1, :] = meta[e : e + 1, CHUNK * i : CHUNK * (i + 1)]
     shift = meta[0:1] * 0.0625
-    keep = jnp.where((iota((8, WIN), 1) & 7) == iota((8, WIN), 0), 1.0, 0.0)
-    lhs = jnp.concatenate([keep, keep * shift], 0).astype(BF16)
-    sums = jnp.dot(lhs, b[...], preferred_element_type=F32)
+    sums = early[...] + jnp.dot(block_rows(late[0:1] * 0.0625), last[...], preferred_element_type=F32)
     s = sums[:8]
     t = sums[8:]
     inner = iota((8, BW), 1) < WIN
@@ -204,7 +228,14 @@
     both = jnp.concatenate([p, q], 0)
     high = both.astype(BF16)
     low = (both - high.astype(F32)).astype(BF16)
-    g = lax.dot_general(jnp.concatenate([high, low], 0), b[...], NT, preferred_element_type=F32)
+    lhs = jnp.concatenate([high, low], 0)
+    g = jnp.concatenate(
+        [
+            lax.dot_general(lhs, b_in[:EARLY], NT, preferred_element_type=F32),
+            lax.dot_general(lhs, last[...], NT, preferred_element_type=F32),
+        ],
+        1,
+    )
     g = g[:16] + g[16:]
     g = g[:8] + g[8:] * shift
     j = iota((8, WIN), 1) & 3
@@ -216,12 +247,26 @@
     grads = by_re + swapped
     for i, at in enumerate(positions()):
         place[pl.ds(at, 1), :] = grads[:, CHUNK * i : CHUNK * (i + 1)]
-    for t in range(16):
+    for t in range(8):
         g_out[t] = place[...]
 
 
-def image_kernel(g_in, meta, b, out_h, total, lhs, xd, out, sems):
-    total[...] = jnp.sum(g_in[...], axis=0)
+def turn(m):
+    quadrant = (m + 128) >> 8
+    p = (m - (quadrant << 8)).astype(F32) * (2.0 * jnp.pi / 1024.0)
+    p2 = p * p
+    c = 1.0 + p2 * (-1.0 / 2 + p2 * (1.0 / 24 + p2 * (-1.0 / 720 + p2 * (1.0 / 40320))))
+    s = p * (1.0 + p2 * (-1.0 / 6 + p2 * (1.0 / 120 + p2 * (-1.0 / 5040 + p2 * (1.0 / 362880)))))
+    odd = (quadrant & 1) == 1
+    cos = jnp.where(odd, s, c)
+    sin = jnp.where(odd, c, s)
+    cos = jnp.where(((quadrant + 1) & 2) == 2, -cos, cos)
+    sin = jnp.where((quadrant & 2) == 2, -sin, sin)
+    return cos, sin
+
+
+def image_kernel(g_in, g_other, meta, b, out_h, total, lhs, xd, out, sems):
+    total[...] = jnp.sum(g_in[...], axis=0) + jnp.sum(g_other[...], axis=0)
     even8 = (iota((8, 128), 1) & 4) == 0
     local = jnp.concatenate([total[pl.ds(at, 1), :] for at in positions()], 0)
     g_re = jnp.where(even8, local, pltpu.roll(local, 4, 1))
@@ -238,13 +283,8 @@
     c_re = wide(c_re)
     c_im = wide(c_im)
     pulse = lax.axis_index("pulse")
-    step = 2.0 * jnp.pi / 1024.0
-    coarse = (((iota((16, WIN), 0) * 8 + pulse * ROWS) * dop) & 1023).astype(F32) * step
-    finer = ((iota((8, WIN), 0) * dop) & 1023).astype(F32) * step
-    cu = jnp.cos(coarse)
-    su = jnp.sin(coarse)
-    cv = jnp.cos(finer)
-    sv = jnp.sin(finer)
+    cu, su = turn(((iota((16, WIN), 0) * 8 + pulse * ROWS) * dop) & 1023)
+    cv, sv = turn((iota((8, WIN), 0) * dop) & 1023)
     vr = cv * c_re - sv * c_im
     vi = cv * c_im + sv * c_re
     for u in range(0, 16, 2):
@@ -354,23 +394,39 @@
             theirs, ours = bands(chunk, filt_v)
         mine.append(ours)
         given.append(lax.ppermute(theirs, AXES, other_core()))
+    sums, info, early = pl.pallas_call(
+        sum_kernel,
+        out_shape=[
+            jax.ShapeDtypeStruct((16, BW), F32),
+            jax.ShapeDtypeStruct((8, EARLY), F32),
+            jax.ShapeDtypeStruct((WIN, BW), BF16),
+        ],
+        in_specs=[vmem()] * 7,
+        out_specs=[vmem()] * 3,
+        compiler_params=params(12),
+        cost_estimate=cost(2 * 16 * EARLY * BW, 4 * MIB),
+    )(*mine, *given[:3])
     partial, meta, b = pl.pallas_call(
         gradient_kernel,
         out_shape=[
-            jax.ShapeDtypeStruct((16, 8, 128), F32),
+            jax.ShapeDtypeStruct((8, 8, 128), F32),
             jax.ShapeDtypeStruct((2, 8, 128), F32),
             jax.ShapeDtypeStruct((WIN, BW), BF16),
         ],
-        in_specs=[vmem()] * 8,
+        in_specs=[vmem()] * 4,
         out_specs=[vmem()] * 3,
         scratch_shapes=[pltpu.VMEM((8, 128), F32)],
+        input_output_aliases={3: 2},
         compiler_params=params(12),
-    )(*mine, *given)
-    grads = lax.all_to_all(partial, "tile", split_axis=0, concat_axis=0, tiled=True)
+    )(given[3], sums, info, early)
+    grads = lax.all_to_all(
+        partial, AXES, split_axis=0, concat_axis=0, axis_index_groups=near(), tiled=True
+    )
+    others = lax.ppermute(grads, AXES, other_core())
     return pl.pallas_call(
         image_kernel,
         out_shape=jax.ShapeDtypeStruct((2, ROWS, 4 * WIN), BF16),
-        in_specs=[vmem()] * 3,
+        in_specs=[vmem()] * 4,
         out_specs=hbm(),
         scratch_shapes=[
             pltpu.VMEM((8, 128), F32),
@@ -380,7 +436,7 @@
             pltpu.SemaphoreType.DMA((8,)),
         ],
         compiler_params=params(20),
-    )(grads, meta, b)
+    )(grads, others, meta, b)
 
 
 def solution(mesh):

time: 55.3 us -> 56.5 us (1.022)
    ppermute x0 -> x1, starting transfers between devices: none -> 1.58 us  [shards(): others = lax.ppermute(grads, AXES, other_core())]
    ppermute x4, starting transfers between devices: 4.83 us -> 3.66 us  [shards(): given.append(lax.ppermute(theirs, AXES, other_core()))]
    ppermute x0 -> x1, waiting for transfers between devices: none -> 0.86 us  [shards(): others = lax.ppermute(grads, AXES, other_core())]
    ppermute x4, waiting for transfers between devices: 1.55 us -> 0.97 us  [shards(): given.append(lax.ppermute(theirs, AXES, other_core()))]
    pallas_call x1 -> x2, Pallas kernels: 1.45 us -> 1.9 us  [the longest x1 1.32 us: shards(): pl.pallas_call(gradient_kernel, out_shape=[jax.ShapeDtypeStruct((8, 8, 12...]
  transfers between devices with their start and end apart: 7 -> 8, of which waited for: 1 -> 2; matrix products, arithmetic and copies ran while one was open for 0% -> 0% of each run, Pallas kernels for 21% -> 22%
where the time goes in v4:
time: 56.5 us; the launch traced here: 56.2 us
  blocking collectives  26.4 us (47%)
  Pallas kernels  18.3 us (32%)
  starting transfers between devices  9.58 us (17%)
  waiting for transfers between devices  1.83 us (3%)
    all_to_all x1, blocking collectives, shards(): lax.all_to_all(own, AXES, split_axis=0, concat_axis=0, axis_index_groups=...  16.3 us
    all_to_all x1, blocking collectives, shards(): lax.all_to_all(partial, AXES, split_axis=0, concat_axis=0, axis_index_gro...  10 us
    pallas_call x3, Pallas kernels, shards(): theirs, ours = bands(chunk, filt_v)  6.93 us
    pallas_call x1, Pallas kernels, shards(): theirs, ours, filt_v = first_bands(chunk, filt)  4.62 us
    ppermute x3, starting transfers between devices, shards(): lax.ppermute(plane, AXES, along_last(k))  4.33 us
    ppermute x4, starting transfers between devices, shards(): given.append(lax.ppermute(theirs, AXES, other_core()))  3.66 us
    pallas_call x1, Pallas kernels, shards(): pl.pallas_call(image_kernel, out_shape=jax.ShapeDtypeStruct((2, ROWS, 4 *...  3.14 us
    pallas_call x1, Pallas kernels, shards(): pl.pallas_call(window_kernel, out_shape=jax.ShapeDtypeStruct((16, 8, BW),...  1.76 us
  transfers between devices with their start and end apart: 8, of which 2 were waited for; matrix products, arithmetic and copies ran while one was open for 0% of the time, Pallas kernels for 22%

profile of v4, /device:TPU:1, one launch (start us, length us, event | category | flops | bytes accessed | tf_op | source)
XLA Modules:
  0.0 56.2 jit_solution(5907182055078458837)
XLA Ops:
  0.0 1.8 %shard_map.73 = bf16[16,8,1152]{2,1,0:T(8,128)(2,1)} custom-call(s32[1,4]{1,0:T(1,128)} %order_h.1, s32[4]{0:T(128)} %off_h.1, s32[4]{0:T(128)} %fine_h.1, s32[4]{0:T(128)} %dop_h.1, s32[4,16]{1,0:T(4,128)} %bitcast.6, bf16[2,4,2048]{2,1,0:T(4,128)(2,1)} %raw_h.1), custom_call_target="tpu_custom_call" | custom-call | tf_op jit(solution)/shard_map/pallas_call | solution.py:340
  1.8 16.3 %all_to_all.10 = bf16[16,8,1152]{2,1,0:T(8,128)(2,1)S(1)} all-to-all(bf16[16,8,1152]{2,1,0:T(8,128)(2,1)} %shard_map.73), channel_id=1, replica_groups={{0,16,8,24,32,48,40,56,64,80,72,88,96,112,104,120},{2,18,10,26,34,50,42..., dimensions={0} | all-to-all | bytes 589824 | tf_op jit(solution)/shard_map/all_to_all | solution.py:356
  18.1 1.3 %collective-permute-start.2 = (bf16[128,1152]{1,0:T(8,128)(2,1)S(1)}, bf16[128,1152]{1,0:T(8,128)(2,1)S(1)}, u32[]{:S(2)}, u32[]{:S(2)}) collective-permute-start(bf16[128,1152]{1,0:T(8,128)(2,1)S(1)} %bitcast.2), channel_id=1, source_target_pairs={{0,2},{1,17},{2,4},{3,19},{4,6},{5,21},{6,0},{7,23},{16,18},{17,9}... | collective-permute-start | bytes 884744 | tf_op jit(solution)/shard_map/ppermute | solution.py:359
  19.4 1.5 %collective-permute-start.3 = (bf16[128,1152]{1,0:T(8,128)(2,1)S(1)}, bf16[128,1152]{1,0:T(8,128)(2,1)S(1)}, u32[]{:S(2)}, u32[]{:S(2)}) collective-permute-start(bf16[128,1152]{1,0:T(8,128)(2,1)S(1)} %bitcast.3), channel_id=1, source_target_pairs={{0,6},{1,25},{2,0},{3,27},{4,2},{5,29},{6,4},{7,31},{16,22},{17,1}... | collective-permute-start | bytes 884744 | tf_op jit(solution)/shard_map/ppermute | solution.py:359
  20.9 1.6 %collective-permute-start = (bf16[128,1152]{1,0:T(8,128)(2,1)S(1)}, bf16[128,1152]{1,0:T(8,128)(2,1)S(1)}, u32[]{:S(2)}, u32[]{:S(2)}) collective-permute-start(bf16[128,1152]{1,0:T(8,128)(2,1)S(1)} %bitcast.4), channel_id=1, source_target_pairs={{0,4},{1,9},{2,6},{3,11},{4,0},{5,13},{6,2},{7,15},{16,20},{17,25}... | collective-permute-start | bytes 884744 | tf_op jit(solution)/shard_map/ppermute | solution.py:359
  22.4 4.6 %shard_map.74 = (bf16[128,1152]{1,0:T(8,128)(2,1)S(1)}, bf16[128,1152]{1,0:T(8,128)(2,1)S(1)}, bf16[2,1024,2048]{2,1,0:T(8,128)(2,1)S(1)}) custom-call(bf16[128,1152]{1,0:T(8,128)(2,1)S(1)} %bitcast.5, bf16[2,1024,2048]{2,1,0:T(8,128)(2,1)} %filt_h.1), custom_call_target="tpu_custom_call" | custom-call | flops 1073741824 | bytes 8388608 | tf_op jit(solution)/shard_map/pallas_call | solution.py:392
  27.1 2.9 %collective-permute-start.4 = (bf16[128,1152]{1,0:T(8,128)(2,1)S(1)}, bf16[128,1152]{1,0:T(8,128)(2,1)S(1)}, u32[]{:S(2)}, u32[]{:S(2)}) collective-permute-start(bf16[128,1152]{1,0:T(8,128)(2,1)S(1)} %get-tuple-element.26), channel_id=1, source_target_pairs={{0,1},{1,0},{2,3},{3,2},{4,5},{5,4},{6,7},{7,6},{16,17},{17,16},{1... | collective-permute-start | bytes 884744 | tf_op jit(solution)/shard_map/ppermute | solution.py:396
  30.0 0.0 collective-permute-done.2.m
  30.0 2.3 %shard_map.76 = (bf16[128,1152]{1,0:T(8,128)(2,1)S(1)}, bf16[128,1152]{1,0:T(8,128)(2,1)S(1)}) custom-call(bf16[128,1152]{1,0:T(8,128)(2,1)S(1)} %collective-permute-done.2.m, bf16[2,1024,2048]{2,1,0:T(8,128)(2,1)S(1)} %get-tuple-element.20.filt), custom_call_target="tpu_custom_call" | custom-call | flops 1073741824 | bytes 8388608 | tf_op jit(solution)/shard_map/pallas_call | solution.py:394
  32.3 0.1 collective-permute-start.5
  32.4 0.0 collective-permute-done.3.m
  32.4 2.3 %shard_map.77 = (bf16[128,1152]{1,0:T(8,128)(2,1)S(1)}, bf16[128,1152]{1,0:T(8,128)(2,1)S(1)}) custom-call(bf16[128,1152]{1,0:T(8,128)(2,1)S(1)} %collective-permute-done.3.m, bf16[2,1024,2048]{2,1,0:T(8,128)(2,1)S(1)} %get-tuple-element.20.filt), custom_call_target="tpu_custom_call" | custom-call | flops 1073741824 | bytes 8388608 | tf_op jit(solution)/shard_map/pallas_call | solution.py:394
  34.7 0.6 %collective-permute-start.6 = (bf16[128,1152]{1,0:T(8,128)(2,1)S(1)}, bf16[128,1152]{1,0:T(8,128)(2,1)S(1)}, u32[]{:S(2)}, u32[]{:S(2)}) collective-permute-start(bf16[128,1152]{1,0:T(8,128)(2,1)S(1)} %get-tuple-element.28), channel_id=1, source_target_pairs={{0,1},{1,0},{2,3},{3,2},{4,5},{5,4},{6,7},{7,6},{16,17},{17,16},{1... | collective-permute-start | bytes 884744 | tf_op jit(solution)/shard_map/ppermute | solution.py:396
  35.3 0.0 collective-permute-done.m
  35.3 2.3 %shard_map.75 = (bf16[128,1152]{1,0:T(8,128)(2,1)S(1)}, bf16[128,1152]{1,0:T(8,128)(2,1)S(1)}) custom-call(bf16[128,1152]{1,0:T(8,128)(2,1)S(1)} %collective-permute-done.m, bf16[2,1024,2048]{2,1,0:T(8,128)(2,1)S(1)} %get-tuple-element.20.filt), custom_call_target="tpu_custom_call" | custom-call | flops 1073741824 | bytes 8388608 | tf_op jit(solution)/shard_map/pallas_call | solution.py:394
  37.6 0.1 collective-permute-start.1
  37.7 0.0 collective-permute-done.4.refs_4_
  37.7 0.0 collective-permute-done.5.refs_5_
  37.7 0.0 collective-permute-done.6.refs_6_
  37.7 0.6 %shard_map.78 = (f32[16,1152]{1,0:T(8,128)S(1)}, f32[8,896]{1,0:T(8,128)S(1)}, bf16[1024,1152]{1,0:T(8,128)(2,1)S(1)}) custom-call(bf16[128,1152]{1,0:T(8,128)(2,1)S(1)} %get-tuple-element.22.refs_0_, bf16[128,1152]{1,0:T(8,128)(2,1)S(1)} %get-tuple-element.23.refs_1_, bf16[128,1152]{1,0:T(8,128)(2,1)S(1)} %get-tuple-element.24.refs_2_, ...), custom_call_target="tpu_custom_call" | custom-call | flops 33030144 | bytes 4194304 | tf_op jit(solution)/shard_map/pallas_call | solution.py:397
  38.3 1.0 %collective-permute-done.1.last = bf16[128,1152]{1,0:T(8,128)(2,1)S(1)} collective-permute-done((bf16[128,1152]{1,0:T(8,128)(2,1)S(1)}, bf16[128,1152]{1,0:T(8,128)(2,1)S(1)}, u32[]{:S(2)}, u32[]{:S(2)}) %collective-permute-start.1) | collective-permute-done | bytes 294944 | tf_op jit(solution)/shard_map/ppermute | solution.py:396
  39.3 1.3 %shard_map.79 = (f32[8,8,128]{2,1,0:T(8,128)S(1)}, f32[2,8,128]{2,1,0:T(8,128)S(1)}, bf16[1024,1152]{1,0:T(8,128)(2,1)S(1)}) custom-call(bf16[128,1152]{1,0:T(8,128)(2,1)S(1)} %collective-permute-done.1.last, f32[16,1152]{1,0:T(8,128)S(1)} %get-tuple-element.29.early, f32[8,896]{1,0:T(8,128)S(1)} %get-tuple-element.30.info, ...), custom_call_target="tpu_custom_call", output_to_operand_aliasing={{2}: (3, {})} | custom-call | tf_op jit(solution)/shard_map/pallas_call | solution.py:409
  40.6 10.0 %all_to_all.11.g_in = f32[8,8,128]{2,1,0:T(8,128)S(1)} all-to-all(f32[8,8,128]{2,1,0:T(8,128)S(1)} %get-tuple-element.32), channel_id=1, replica_groups={{16,18,20,22,8,10,12,14},{17,19,21,23,9,11,13,15},{0,2,4,6,24,26,28,30}..., dimensions={0} | all-to-all | bytes 65536 | tf_op jit(solution)/shard_map/all_to_all | solution.py:422
  50.6 1.6 %collective-permute-start.7 = (f32[8,8,128]{2,1,0:T(8,128)S(1)}, f32[8,8,128]{2,1,0:T(8,128)S(1)}, u32[]{:S(2)}, u32[]{:S(2)}) collective-permute-start(f32[8,8,128]{2,1,0:T(8,128)S(1)} %all_to_all.11.g_in), channel_id=1, source_target_pairs={{0,1},{1,0},{2,3},{3,2},{4,5},{5,4},{6,7},{7,6},{16,17},{17,16},{1... | collective-permute-start | bytes 98312 | tf_op jit(solution)/shard_map/ppermute | solution.py:425
  52.2 0.9 %collective-permute-done.7.g_other = f32[8,8,128]{2,1,0:T(8,128)S(1)} collective-permute-done((f32[8,8,128]{2,1,0:T(8,128)S(1)}, f32[8,8,128]{2,1,0:T(8,128)S(1)}, u32[]{:S(2)}, u32[]{:S(2)}) %collective-permute-start.7) | collective-permute-done | bytes 32800 | tf_op jit(solution)/shard_map/ppermute | solution.py:425
  53.0 3.1 %shard_map.80 = bf16[2,128,4096]{2,1,0:T(8,128)(2,1)} custom-call(f32[8,8,128]{2,1,0:T(8,128)S(1)} %all_to_all.11.g_in, f32[8,8,128]{2,1,0:T(8,128)S(1)} %collective-permute-done.7.g_other, f32[2,8,128]{2,1,0:T(8,128)S(1)} %get-tuple-element.33.meta, bf16[1024,1152]{1,0:T(8,128)(2,1)S(1)} %get-tuple-element.34.b), custom_call_target="tpu_custom_call" | custom-call | tf_op jit(solution)/shard_map/pallas_call | solution.py:426
Async XLA Ops:
  18.1 11.9 %collective-permute-start.2 = (bf16[128,1152]{1,0:T(8,128)(2,1)S(1)}, bf16[128,1152]{1,0:T(8,128)(2,1)S(1)}, u32[]{:S(2)}, u32[]{:S(2)}) collective-permute-start(bf16[128,1152]{1,0:T(8,128)(2,1)S(1)} %bitcast.2), channel_id=1, source_target_pairs={{0,2},{1,17},{2,4},{3,19},{4,6},{5,21},{6,0},{7,23},{16,18},{17,9}... | collective-permute-start | bytes 884744 | tf_op jit(solution)/shard_map/ppermute | solution.py:359
  19.4 13.0 %collective-permute-start.3 = (bf16[128,1152]{1,0:T(8,128)(2,1)S(1)}, bf16[128,1152]{1,0:T(8,128)(2,1)S(1)}, u32[]{:S(2)}, u32[]{:S(2)}) collective-permute-start(bf16[128,1152]{1,0:T(8,128)(2,1)S(1)} %bitcast.3), channel_id=1, source_target_pairs={{0,6},{1,25},{2,0},{3,27},{4,2},{5,29},{6,4},{7,31},{16,22},{17,1}... | collective-permute-start | bytes 884744 | tf_op jit(solution)/shard_map/ppermute | solution.py:359
  20.9 14.4 %collective-permute-start = (bf16[128,1152]{1,0:T(8,128)(2,1)S(1)}, bf16[128,1152]{1,0:T(8,128)(2,1)S(1)}, u32[]{:S(2)}, u32[]{:S(2)}) collective-permute-start(bf16[128,1152]{1,0:T(8,128)(2,1)S(1)} %bitcast.4), channel_id=1, source_target_pairs={{0,4},{1,9},{2,6},{3,11},{4,0},{5,13},{6,2},{7,15},{16,20},{17,25}... | collective-permute-start | bytes 884744 | tf_op jit(solution)/shard_map/ppermute | solution.py:359
  27.1 10.6 %collective-permute-start.4 = (bf16[128,1152]{1,0:T(8,128)(2,1)S(1)}, bf16[128,1152]{1,0:T(8,128)(2,1)S(1)}, u32[]{:S(2)}, u32[]{:S(2)}) collective-permute-start(bf16[128,1152]{1,0:T(8,128)(2,1)S(1)} %get-tuple-element.26), channel_id=1, source_target_pairs={{0,1},{1,0},{2,3},{3,2},{4,5},{5,4},{6,7},{7,6},{16,17},{17,16},{1... | collective-permute-start | bytes 884744 | tf_op jit(solution)/shard_map/ppermute | solution.py:396
  32.3 5.4 %collective-permute-start.5 = (bf16[128,1152]{1,0:T(8,128)(2,1)S(1)}, bf16[128,1152]{1,0:T(8,128)(2,1)S(1)}, u32[]{:S(2)}, u32[]{:S(2)}) collective-permute-start(bf16[128,1152]{1,0:T(8,128)(2,1)S(1)} %get-tuple-element.27), channel_id=1, source_target_pairs={{0,1},{1,0},{2,3},{3,2},{4,5},{5,4},{6,7},{7,6},{16,17},{17,16},{1... | collective-permute-start | bytes 884744 | tf_op jit(solution)/shard_map/ppermute | solution.py:396
  34.7 3.0 %collective-permute-start.6 = (bf16[128,1152]{1,0:T(8,128)(2,1)S(1)}, bf16[128,1152]{1,0:T(8,128)(2,1)S(1)}, u32[]{:S(2)}, u32[]{:S(2)}) collective-permute-start(bf16[128,1152]{1,0:T(8,128)(2,1)S(1)} %get-tuple-element.28), channel_id=1, source_target_pairs={{0,1},{1,0},{2,3},{3,2},{4,5},{5,4},{6,7},{7,6},{16,17},{17,16},{1... | collective-permute-start | bytes 884744 | tf_op jit(solution)/shard_map/ppermute | solution.py:396
  37.6 1.7 %collective-permute-start.1 = (bf16[128,1152]{1,0:T(8,128)(2,1)S(1)}, bf16[128,1152]{1,0:T(8,128)(2,1)S(1)}, u32[]{:S(2)}, u32[]{:S(2)}) collective-permute-start(bf16[128,1152]{1,0:T(8,128)(2,1)S(1)} %get-tuple-element.21), channel_id=1, source_target_pairs={{0,1},{1,0},{2,3},{3,2},{4,5},{5,4},{6,7},{7,6},{16,17},{17,16},{1... | collective-permute-start | bytes 884744 | tf_op jit(solution)/shard_map/ppermute | solution.py:396
  50.6 2.4 %collective-permute-start.7 = (f32[8,8,128]{2,1,0:T(8,128)S(1)}, f32[8,8,128]{2,1,0:T(8,128)S(1)}, u32[]{:S(2)}, u32[]{:S(2)}) collective-permute-start(f32[8,8,128]{2,1,0:T(8,128)S(1)} %all_to_all.11.g_in), channel_id=1, source_target_pairs={{0,1},{1,0},{2,3},{3,2},{4,5},{5,4},{6,7},{7,6},{16,17},{17,16},{1... | collective-permute-start | bytes 98312 | tf_op jit(solution)/shard_map/ppermute | solution.py:425

commit v5 on v4

--- a/solution.py
+++ b/solution.py
@@ -1,3 +1,5 @@
+import functools
+
 import jax
 import jax.numpy as jnp
 from jax import lax
@@ -46,13 +48,6 @@
 
 def other_core():
     return [(linear(z, y, x, c), linear(z, y, x, 1 - c)) for z, y, x, c in PLACES]
-
-
-def near():
-    groups = {}
-    for z, y, x, c in PLACES:
-        groups.setdefault((z, y in (0, 3), c), []).append(linear(z, y, x, c))
-    return [groups[key] for key in sorted(groups)]
 
 
 def iota(shape, axis):
@@ -100,10 +95,21 @@
         block = (slice(None), slice(None), pl.ds(512 * i, 512))
         copies.append(pltpu.make_async_copy(filt_h.at[block], filt.at[block], sems.at[i]))
         copies[-1].start()
-    band_kernel(m, filt, theirs, mine, w, prof, cut, starts_v, starts_s, sem, copies)
-
-
-def band_kernel(m, filt, theirs, mine, w, prof, cut, starts_v, starts_s, sem, copies=None):
+    outs = (theirs, 0, mine, 0)
+    cut_bands(m, filt, outs, (w, prof, cut, starts_v, starts_s, sem), copies)
+
+
+def middle_band_kernel(index, m, filt, theirs_in, mine_in, theirs, mine, *scratch):
+    cut_bands(m, filt, (theirs, CHUNK * index, mine, CHUNK * index), scratch)
+
+
+def last_band_kernel(m, filt, mine_in, theirs, mine, *scratch):
+    cut_bands(m, filt, (theirs, 0, mine, CHUNK * 3), scratch)
+
+
+def cut_bands(m, filt, outs, scratch, copies=None):
+    theirs, theirs_at, mine, mine_at = outs
+    w, prof, cut, starts_v, starts_s, sem = scratch
     tile = lax.axis_index("tile")
     sibling = tile + 1 - 2 * lax.rem(tile, 2)
     lane8 = iota((8, 128), 1)
@@ -136,7 +142,7 @@
                 at = g * 128 + (n // 128 + h) * 8
                 prof[at : at + 8, :] = r[8 * g : 8 * g + 8, 128 * h : 128 * h + 128]
     copy.wait()
-    for which, out in enumerate((theirs, mine)):
+    for which in range(2):
         for g in range(16):
             for j in range(4):
                 start = starts_s[1 - which, 8 * g + j]
@@ -149,7 +155,7 @@
                 cut[which, pl.ds(to, 8, 8), :] = re
                 cut[which, pl.ds(to + 4, 8, 8), :] = im
                 cut[which, pl.ds(to + 64, 2, 4), :] = end
-    for which, out in enumerate((theirs, mine)):
+    for which, (out, to) in enumerate(((theirs, theirs_at), (mine, mine_at))):
         for pair in range(8):
             done = [[], []]
             for e in range(2):
@@ -164,7 +170,8 @@
                 )
             for c in range(9):
                 v = jnp.concatenate([done[0][c], done[1][c]], 0).astype(BF16)
-                out[16 * pair : 16 * pair + 16, 128 * c : 128 * c + 128] = v
+                at = to + 16 * pair
+                out[at : at + 16, 128 * c : 128 * c + 128] = v
 
 
 def positions():
@@ -196,15 +203,16 @@
     return jnp.concatenate([keep, keep * shift], 0).astype(BF16)
 
 
-def sum_kernel(*refs):
-    parts = refs[:7]
-    sums, info, b = refs[7:]
-    for i, part in enumerate(parts):
-        b[CHUNK * i : CHUNK * (i + 1), :] = part[...]
-    b[EARLY:, :] = jnp.zeros((CHUNK, BW), BF16)
-    info[...] = lane_info(b[:EARLY, WIN:])
-    lhs = block_rows(info[0:1] * 0.0625)
-    sums[...] = jnp.dot(lhs, b[:EARLY], preferred_element_type=F32)
+def sum_kernel(given, b_in, sums, info, b):
+    b[4 * CHUNK : EARLY, :] = given[...]
+    halves = ((b_in, 0, 4 * CHUNK), (given, 4 * CHUNK, EARLY))
+    for part, low, high in halves:
+        info[:, low:high] = lane_info(part[: high - low, WIN:])
+    total = jnp.zeros((16, BW), F32)
+    for part, low, high in halves:
+        lhs = block_rows(info[0:1, low:high] * 0.0625)
+        total += jnp.dot(lhs, part[: high - low], preferred_element_type=F32)
+    sums[...] = total
 
 
 def gradient_kernel(last, early, info, b_in, g_out, meta_out, b, place):
@@ -247,7 +255,7 @@
     grads = by_re + swapped
     for i, at in enumerate(positions()):
         place[pl.ds(at, 1), :] = grads[:, CHUNK * i : CHUNK * (i + 1)]
-    for t in range(8):
+    for t in range(16):
         g_out[t] = place[...]
 
 
@@ -265,8 +273,8 @@
     return cos, sin
 
 
-def image_kernel(g_in, g_other, meta, b, out_h, total, lhs, xd, out, sems):
-    total[...] = jnp.sum(g_in[...], axis=0) + jnp.sum(g_other[...], axis=0)
+def image_kernel(g_in, meta, b, out_h, total, lhs, xd, out, sems):
+    total[...] = jnp.sum(g_in[...], axis=0)
     even8 = (iota((8, 128), 1) & 4) == 0
     local = jnp.concatenate([total[pl.ds(at, 1), :] for at in positions()], 0)
     g_re = jnp.where(even8, local, pltpu.roll(local, 4, 1))
@@ -358,6 +366,9 @@
     ).reshape(CHUNK, BW)
     chunks = [plane] + [lax.ppermute(plane, AXES, along_last(k)) for k in STEPS[1:]]
     band = jax.ShapeDtypeStruct((CHUNK, BW), BF16)
+    three = jax.ShapeDtypeStruct((3 * CHUNK, BW), BF16)
+    whole = jax.ShapeDtypeStruct((WIN, BW), BF16)
+    effort = cost(2 * CHUNK * UPS * UPS, 8 * MIB)
     scratch = [
         pltpu.VMEM((CHUNK, 2 * WIN), BF16),
         pltpu.VMEM((2048, 128), F32),
@@ -368,48 +379,55 @@
     ]
     first_bands = pl.pallas_call(
         first_band_kernel,
-        out_shape=[band, band, jax.ShapeDtypeStruct(filt.shape, BF16)],
+        out_shape=[three, whole, jax.ShapeDtypeStruct(filt.shape, BF16)],
         in_specs=[vmem(), hbm()],
         out_specs=[vmem()] * 3,
         scratch_shapes=scratch + [pltpu.SemaphoreType.DMA((4,))],
         compiler_params=params(FIRST),
-        cost_estimate=cost(2 * CHUNK * UPS * UPS, 8 * MIB),
+        cost_estimate=effort,
     )
-    bands = pl.pallas_call(
-        band_kernel,
-        out_shape=[band, band],
-        in_specs=[vmem()] * 2,
+    theirs, mine, filt_v = first_bands(chunks[0], filt)
+    for index in (1, 2):
+        theirs, mine = pl.pallas_call(
+            functools.partial(middle_band_kernel, index),
+            out_shape=[three, whole],
+            in_specs=[vmem()] * 4,
+            out_specs=[vmem()] * 2,
+            scratch_shapes=scratch,
+            input_output_aliases={2: 0, 3: 1},
+            compiler_params=params(12),
+            cost_estimate=effort,
+        )(chunks[index], filt_v, theirs, mine)
+    theirs, chunks[3] = lax.optimization_barrier((theirs, chunks[3]))
+    given = lax.ppermute(theirs, AXES, other_core())
+    theirs, mine = pl.pallas_call(
+        last_band_kernel,
+        out_shape=[band, whole],
+        in_specs=[vmem()] * 3,
         out_specs=[vmem()] * 2,
         scratch_shapes=scratch,
+        input_output_aliases={2: 1},
         compiler_params=params(12),
-        cost_estimate=cost(2 * CHUNK * UPS * UPS, 8 * MIB),
-    )
-    mine = []
-    given = []
-    filt_v = None
-    for chunk in chunks:
-        if filt_v is None:
-            theirs, ours, filt_v = first_bands(chunk, filt)
-        else:
-            theirs, ours = bands(chunk, filt_v)
-        mine.append(ours)
-        given.append(lax.ppermute(theirs, AXES, other_core()))
+        cost_estimate=effort,
+    )(chunks[3], filt_v, mine)
+    last = lax.ppermute(theirs, AXES, other_core())
     sums, info, early = pl.pallas_call(
         sum_kernel,
         out_shape=[
             jax.ShapeDtypeStruct((16, BW), F32),
             jax.ShapeDtypeStruct((8, EARLY), F32),
-            jax.ShapeDtypeStruct((WIN, BW), BF16),
+            whole,
         ],
-        in_specs=[vmem()] * 7,
+        in_specs=[vmem()] * 2,
         out_specs=[vmem()] * 3,
+        input_output_aliases={1: 2},
         compiler_params=params(12),
         cost_estimate=cost(2 * 16 * EARLY * BW, 4 * MIB),
-    )(*mine, *given[:3])
+    )(given, mine)
     partial, meta, b = pl.pallas_call(
         gradient_kernel,
         out_shape=[
-            jax.ShapeDtypeStruct((8, 8, 128), F32),
+            jax.ShapeDtypeStruct((16, 8, 128), F32),
             jax.ShapeDtypeStruct((2, 8, 128), F32),
             jax.ShapeDtypeStruct((WIN, BW), BF16),
         ],
@@ -418,15 +436,12 @@
         scratch_shapes=[pltpu.VMEM((8, 128), F32)],
         input_output_aliases={3: 2},
         compiler_params=params(12),
-    )(given[3], sums, info, early)
-    grads = lax.all_to_all(
-        partial, AXES, split_axis=0, concat_axis=0, axis_index_groups=near(), tiled=True
-    )
-    others = lax.ppermute(grads, AXES, other_core())
+    )(last, sums, info, early)
+    grads = lax.all_to_all(partial, "tile", split_axis=0, concat_axis=0, tiled=True)
     return pl.pallas_call(
         image_kernel,
         out_shape=jax.ShapeDtypeStruct((2, ROWS, 4 * WIN), BF16),
-        in_specs=[vmem()] * 4,
+        in_specs=[vmem()] * 3,
         out_specs=hbm(),
         scratch_shapes=[
             pltpu.VMEM((8, 128), F32),
@@ -436,7 +451,7 @@
             pltpu.SemaphoreType.DMA((8,)),
         ],
         compiler_params=params(20),
-    )(grads, others, meta, b)
+    )(grads, meta, b)
 
 
 def solution(mesh):

time: 56.5 us -> 55.7 us (0.986)
  blocking collectives: 26.4 us -> 28.7 us
  starting transfers between devices: 9.58 us -> 7.32 us
  waiting for transfers between devices: 1.83 us -> 1 us
    all_to_all x1, blocking collectives: 10 us -> 12.3 us  [shards(): lax.all_to_all(partial, 'tile', split_axis=0, concat_axis=0, tiled=True)]
    ppermute x5 -> x2, starting transfers between devices: 5.24 us -> 2.98 us  [the longest x1 2.89 us: shards(): given = lax.ppermute(theirs, AXES, other_core())]
    ppermute x5 -> x2, waiting for transfers between devices: 1.83 us -> 1 us  [the longest x1 0.99 us: shards(): last = lax.ppermute(theirs, AXES, other_core())]
  transfers between devices with their start and end apart: 8 -> 5, of which waited for: 2 -> 1; matrix products, arithmetic and copies ran while one was open for 0% -> 0% of each run, Pallas kernels for 22% -> 22%
where the time goes in v5:
time: 55.7 us; the launch traced here: 55.4 us
  blocking collectives  28.7 us (52%)
  Pallas kernels  18.3 us (33%)
  starting transfers between devices  7.32 us (13%)
  waiting for transfers between devices  1 us (2%)
    all_to_all x1, blocking collectives, shards(): lax.all_to_all(own, AXES, split_axis=0, concat_axis=0, axis_index_groups=...  16.3 us
    all_to_all x1, blocking collectives, shards(): lax.all_to_all(partial, 'tile', split_axis=0, concat_axis=0, tiled=True)  12.3 us
    pallas_call x2, Pallas kernels, shards(): pl.pallas_call(functools.partial(middle_band_kernel, index), out_shape=[t...  4.63 us
    pallas_call x1, Pallas kernels, shards(): theirs, mine, filt_v = first_bands(chunks[0], filt)  4.62 us
    ppermute x3, starting transfers between devices, shards(): lax.ppermute(plane, AXES, along_last(k))  4.33 us
    pallas_call x1, Pallas kernels, shards(): pl.pallas_call(image_kernel, out_shape=jax.ShapeDtypeStruct((2, ROWS, 4 *...  3.14 us
    ppermute x1, starting transfers between devices, shards(): given = lax.ppermute(theirs, AXES, other_core())  2.89 us
    pallas_call x1, Pallas kernels, shards(): pl.pallas_call(last_band_kernel, out_shape=[band, whole], in_specs=[vmem(...  2.31 us
  transfers between devices with their start and end apart: 5, of which 1 were waited for; matrix products, arithmetic and copies ran while one was open for 0% of the time, Pallas kernels for 22%

profile of v5, /device:TPU:1, one launch (start us, length us, event | category | flops | bytes accessed | tf_op | source)
XLA Modules:
  0.0 55.4 jit_solution(9263752937995249039)
XLA Ops:
  0.0 1.8 %shard_map.73 = bf16[16,8,1152]{2,1,0:T(8,128)(2,1)} custom-call(s32[1,4]{1,0:T(1,128)} %order_h.1, s32[4]{0:T(128)} %off_h.1, s32[4]{0:T(128)} %fine_h.1, s32[4]{0:T(128)} %dop_h.1, s32[4,16]{1,0:T(4,128)} %bitcast.6, bf16[2,4,2048]{2,1,0:T(4,128)(2,1)} %raw_h.1), custom_call_target="tpu_custom_call" | custom-call | tf_op jit(solution)/shard_map/pallas_call | solution.py:348
  1.8 16.3 %all_to_all.10 = bf16[16,8,1152]{2,1,0:T(8,128)(2,1)S(1)} all-to-all(bf16[16,8,1152]{2,1,0:T(8,128)(2,1)} %shard_map.73), channel_id=1, replica_groups={{0,16,8,24,32,48,40,56,64,80,72,88,96,112,104,120},{2,18,10,26,34,50,42..., dimensions={0} | all-to-all | bytes 589824 | tf_op jit(solution)/shard_map/all_to_all | solution.py:364
  18.1 1.3 %collective-permute-start.1 = (bf16[128,1152]{1,0:T(8,128)(2,1)S(1)}, bf16[128,1152]{1,0:T(8,128)(2,1)S(1)}, u32[]{:S(2)}, u32[]{:S(2)}) collective-permute-start(bf16[128,1152]{1,0:T(8,128)(2,1)S(1)} %bitcast.2), channel_id=1, source_target_pairs={{0,2},{1,17},{2,4},{3,19},{4,6},{5,21},{6,0},{7,23},{16,18},{17,9}... | collective-permute-start | bytes 884744 | tf_op jit(solution)/shard_map/ppermute | solution.py:367
  19.4 1.5 %collective-permute-start = (bf16[128,1152]{1,0:T(8,128)(2,1)S(1)}, bf16[128,1152]{1,0:T(8,128)(2,1)S(1)}, u32[]{:S(2)}, u32[]{:S(2)}) collective-permute-start(bf16[128,1152]{1,0:T(8,128)(2,1)S(1)} %bitcast.3), channel_id=1, source_target_pairs={{0,6},{1,25},{2,0},{3,27},{4,2},{5,29},{6,4},{7,31},{16,22},{17,1}... | collective-permute-start | bytes 884744 | tf_op jit(solution)/shard_map/ppermute | solution.py:367
  20.9 1.6 %collective-permute-start.2 = (bf16[128,1152]{1,0:T(8,128)(2,1)S(1)}, bf16[128,1152]{1,0:T(8,128)(2,1)S(1)}, u32[]{:S(2)}, u32[]{:S(2)}) collective-permute-start(bf16[128,1152]{1,0:T(8,128)(2,1)S(1)} %bitcast.4), channel_id=1, source_target_pairs={{0,4},{1,9},{2,6},{3,11},{4,0},{5,13},{6,2},{7,15},{16,20},{17,25}... | collective-permute-start | bytes 884744 | tf_op jit(solution)/shard_map/ppermute | solution.py:367
  22.4 4.6 %shard_map.74 = (bf16[384,1152]{1,0:T(8,128)(2,1)S(1)}, bf16[1024,1152]{1,0:T(8,128)(2,1)S(1)}, bf16[2,1024,2048]{2,1,0:T(8,128)(2,1)S(1)}) custom-call(bf16[128,1152]{1,0:T(8,128)(2,1)S(1)} %bitcast.5, bf16[2,1024,2048]{2,1,0:T(8,128)(2,1)} %filt_h.1), custom_call_target="tpu_custom_call" | custom-call | flops 1073741824 | bytes 8388608 | tf_op jit(solution)/shard_map/pallas_call | solution.py:389
  27.1 0.0 collective-permute-done.1.m
  27.1 2.3 %shard_map.75 = (bf16[384,1152]{1,0:T(8,128)(2,1)S(1)}, bf16[1024,1152]{1,0:T(8,128)(2,1)S(1)}) custom-call(bf16[128,1152]{1,0:T(8,128)(2,1)S(1)} %collective-permute-done.1.m, bf16[2,1024,2048]{2,1,0:T(8,128)(2,1)S(1)} %get-tuple-element.22.filt, bf16[384,1152]{1,0:T(8,128)(2,1)S(1)} %get-tuple-element.23.theirs_in, ...), custom_call_target="tpu_custom_call", output_to_operand_aliasing={{0}: (2, {}), {1}: (3, {})} | custom-call | flops 1073741824 | bytes 8388608 | tf_op jit(solution)/shard_map/pallas_call | solution.py:391
  29.4 0.0 collective-permute-done.m
  29.4 2.3 %shard_map.76 = (bf16[384,1152]{1,0:T(8,128)(2,1)S(1)}, bf16[1024,1152]{1,0:T(8,128)(2,1)S(1)}) custom-call(bf16[128,1152]{1,0:T(8,128)(2,1)S(1)} %collective-permute-done.m, bf16[2,1024,2048]{2,1,0:T(8,128)(2,1)S(1)} %get-tuple-element.22.filt, bf16[384,1152]{1,0:T(8,128)(2,1)S(1)} %get-tuple-element.25.theirs_in, ...), custom_call_target="tpu_custom_call", output_to_operand_aliasing={{0}: (2, {}), {1}: (3, {})} | custom-call | flops 1073741824 | bytes 8388608 | tf_op jit(solution)/shard_map/pallas_call | solution.py:391
  31.7 0.0 collective-permute-done.2.m
  31.7 2.9 %collective-permute-start.4 = (bf16[384,1152]{1,0:T(8,128)(2,1)S(1)}, bf16[384,1152]{1,0:T(8,128)(2,1)S(1)}, u32[]{:S(2)}, u32[]{:S(2)}) collective-permute-start(bf16[384,1152]{1,0:T(8,128)(2,1)S(1)} %get-tuple-element.31), channel_id=1, source_target_pairs={{0,1},{1,0},{2,3},{3,2},{4,5},{5,4},{6,7},{7,6},{16,17},{17,16},{1... | collective-permute-start | bytes 2654216 | tf_op jit(solution)/shard_map/ppermute | solution.py:402
  34.6 2.3 %shard_map.77 = (bf16[128,1152]{1,0:T(8,128)(2,1)S(1)}, bf16[1024,1152]{1,0:T(8,128)(2,1)S(1)}) custom-call(bf16[128,1152]{1,0:T(8,128)(2,1)S(1)} %collective-permute-done.2.m, bf16[2,1024,2048]{2,1,0:T(8,128)(2,1)S(1)} %get-tuple-element.22.filt, bf16[1024,1152]{1,0:T(8,128)(2,1)S(1)} %get-tuple-element.29.mine_in), custom_call_target="tpu_custom_call", output_to_operand_aliasing={{1}: (2, {})} | custom-call | flops 1073741824 | bytes 8388608 | tf_op jit(solution)/shard_map/pallas_call | solution.py:403
  36.9 0.1 collective-permute-start.3
  37.0 0.0 collective-permute-done.4.given
  37.1 0.6 %shard_map.78 = (f32[16,1152]{1,0:T(8,128)S(1)}, f32[8,896]{1,0:T(8,128)S(1)}, bf16[1024,1152]{1,0:T(8,128)(2,1)S(1)}) custom-call(bf16[384,1152]{1,0:T(8,128)(2,1)S(1)} %collective-permute-done.4.given, bf16[1024,1152]{1,0:T(8,128)(2,1)S(1)} %get-tuple-element.32.b_in), custom_call_target="tpu_custom_call", output_to_operand_aliasing={{2}: (1, {})} | custom-call | flops 33030144 | bytes 4194304 | tf_op jit(solution)/shard_map/pallas_call | solution.py:414
  37.6 1.0 %collective-permute-done.3.last = bf16[128,1152]{1,0:T(8,128)(2,1)S(1)} collective-permute-done((bf16[128,1152]{1,0:T(8,128)(2,1)S(1)}, bf16[128,1152]{1,0:T(8,128)(2,1)S(1)}, u32[]{:S(2)}, u32[]{:S(2)}) %collective-permute-start.3) | collective-permute-done | bytes 294944 | tf_op jit(solution)/shard_map/ppermute | solution.py:413
  38.6 1.3 %shard_map.79 = (f32[16,8,128]{2,1,0:T(8,128)S(1)}, f32[2,8,128]{2,1,0:T(8,128)S(1)}, bf16[1024,1152]{1,0:T(8,128)(2,1)S(1)}) custom-call(bf16[128,1152]{1,0:T(8,128)(2,1)S(1)} %collective-permute-done.3.last, f32[16,1152]{1,0:T(8,128)S(1)} %get-tuple-element.33.early, f32[8,896]{1,0:T(8,128)S(1)} %get-tuple-element.34.info, ...), custom_call_target="tpu_custom_call", output_to_operand_aliasing={{2}: (3, {})} | custom-call | tf_op jit(solution)/shard_map/pallas_call | solution.py:427
  39.9 12.3 %all_to_all.11.g_in = f32[16,8,128]{2,1,0:T(8,128)S(1)} all-to-all(f32[16,8,128]{2,1,0:T(8,128)S(1)} %get-tuple-element.36), channel_id=1, replica_groups=mesh['pulse'=8,'tile'=16] {'tile'}, dimensions={0} | all-to-all | bytes 131072 | tf_op jit(solution)/shard_map/all_to_all | solution.py:440
  52.3 3.1 %shard_map.80 = bf16[2,128,4096]{2,1,0:T(8,128)(2,1)} custom-call(f32[16,8,128]{2,1,0:T(8,128)S(1)} %all_to_all.11.g_in, f32[2,8,128]{2,1,0:T(8,128)S(1)} %get-tuple-element.37.meta, bf16[1024,1152]{1,0:T(8,128)(2,1)S(1)} %get-tuple-element.38.b), custom_call_target="tpu_custom_call" | custom-call | tf_op jit(solution)/shard_map/pallas_call | solution.py:441
Async XLA Ops:
  18.1 9.0 %collective-permute-start.1 = (bf16[128,1152]{1,0:T(8,128)(2,1)S(1)}, bf16[128,1152]{1,0:T(8,128)(2,1)S(1)}, u32[]{:S(2)}, u32[]{:S(2)}) collective-permute-start(bf16[128,1152]{1,0:T(8,128)(2,1)S(1)} %bitcast.2), channel_id=1, source_target_pairs={{0,2},{1,17},{2,4},{3,19},{4,6},{5,21},{6,0},{7,23},{16,18},{17,9}... | collective-permute-start | bytes 884744 | tf_op jit(solution)/shard_map/ppermute | solution.py:367
  19.4 10.0 %collective-permute-start = (bf16[128,1152]{1,0:T(8,128)(2,1)S(1)}, bf16[128,1152]{1,0:T(8,128)(2,1)S(1)}, u32[]{:S(2)}, u32[]{:S(2)}) collective-permute-start(bf16[128,1152]{1,0:T(8,128)(2,1)S(1)} %bitcast.3), channel_id=1, source_target_pairs={{0,6},{1,25},{2,0},{3,27},{4,2},{5,29},{6,4},{7,31},{16,22},{17,1}... | collective-permute-start | bytes 884744 | tf_op jit(solution)/shard_map/ppermute | solution.py:367
  20.9 10.8 %collective-permute-start.2 = (bf16[128,1152]{1,0:T(8,128)(2,1)S(1)}, bf16[128,1152]{1,0:T(8,128)(2,1)S(1)}, u32[]{:S(2)}, u32[]{:S(2)}) collective-permute-start(bf16[128,1152]{1,0:T(8,128)(2,1)S(1)} %bitcast.4), channel_id=1, source_target_pairs={{0,4},{1,9},{2,6},{3,11},{4,0},{5,13},{6,2},{7,15},{16,20},{17,25}... | collective-permute-start | bytes 884744 | tf_op jit(solution)/shard_map/ppermute | solution.py:367
  31.7 5.3 %collective-permute-start.4 = (bf16[384,1152]{1,0:T(8,128)(2,1)S(1)}, bf16[384,1152]{1,0:T(8,128)(2,1)S(1)}, u32[]{:S(2)}, u32[]{:S(2)}) collective-permute-start(bf16[384,1152]{1,0:T(8,128)(2,1)S(1)} %get-tuple-element.31), channel_id=1, source_target_pairs={{0,1},{1,0},{2,3},{3,2},{4,5},{5,4},{6,7},{7,6},{16,17},{17,16},{1... | collective-permute-start | bytes 2654216 | tf_op jit(solution)/shard_map/ppermute | solution.py:402
  36.9 1.7 %collective-permute-start.3 = (bf16[128,1152]{1,0:T(8,128)(2,1)S(1)}, bf16[128,1152]{1,0:T(8,128)(2,1)S(1)}, u32[]{:S(2)}, u32[]{:S(2)}) collective-permute-start(bf16[128,1152]{1,0:T(8,128)(2,1)S(1)} %get-tuple-element.30), channel_id=1, source_target_pairs={{0,1},{1,0},{2,3},{3,2},{4,5},{5,4},{6,7},{7,6},{16,17},{17,16},{1... | collective-permute-start | bytes 884744 | tf_op jit(solution)/shard_map/ppermute | solution.py:413

commit v6 on v5

--- a/solution.py
+++ b/solution.py
@@ -48,6 +48,10 @@
 
 def other_core():
     return [(linear(z, y, x, c), linear(z, y, x, 1 - c)) for z, y, x, c in PLACES]
+
+
+def pairs(partner):
+    return [(linear(*place), linear(*partner(*place))) for place in PLACES]
 
 
 def iota(shape, axis):
@@ -215,7 +219,7 @@
     sums[...] = total
 
 
-def gradient_kernel(last, early, info, b_in, g_out, meta_out, b, place):
+def gradient_kernel(last, early, info, b_in, g_out, meta_out, b):
     b[EARLY:, :] = last[...]
     late = lane_info(last[:, WIN:])
     meta = jnp.concatenate([info[0:2], late[0:2]], 1)
@@ -254,9 +258,7 @@
     swapped = jnp.where(even, pltpu.roll(by_im, WIN - 4, 1), -pltpu.roll(by_im, 4, 1))
     grads = by_re + swapped
     for i, at in enumerate(positions()):
-        place[pl.ds(at, 1), :] = grads[:, CHUNK * i : CHUNK * (i + 1)]
-    for t in range(16):
-        g_out[t] = place[...]
+        g_out[pl.ds(at, 1), :] = grads[:, CHUNK * i : CHUNK * (i + 1)]
 
 
 def turn(m):
@@ -273,8 +275,8 @@
     return cos, sin
 
 
-def image_kernel(g_in, meta, b, out_h, total, lhs, xd, out, sems):
-    total[...] = jnp.sum(g_in[...], axis=0)
+def image_kernel(g_in, g_other, meta, b, out_h, total, lhs, xd, out, sems):
+    total[...] = g_in[...] + g_other[...]
     even8 = (iota((8, 128), 1) & 4) == 0
     local = jnp.concatenate([total[pl.ds(at, 1), :] for at in positions()], 0)
     g_re = jnp.where(even8, local, pltpu.roll(local, 4, 1))
@@ -427,21 +429,26 @@
     partial, meta, b = pl.pallas_call(
         gradient_kernel,
         out_shape=[
-            jax.ShapeDtypeStruct((16, 8, 128), F32),
+            jax.ShapeDtypeStruct((8, 128), F32),
             jax.ShapeDtypeStruct((2, 8, 128), F32),
             jax.ShapeDtypeStruct((WIN, BW), BF16),
         ],
         in_specs=[vmem()] * 4,
         out_specs=[vmem()] * 3,
-        scratch_shapes=[pltpu.VMEM((8, 128), F32)],
         input_output_aliases={3: 2},
         compiler_params=params(12),
     )(last, sums, info, early)
-    grads = lax.all_to_all(partial, "tile", split_axis=0, concat_axis=0, tiled=True)
+    for partner in (
+        other_core(),
+        pairs(lambda z, y, x, c: (z, y, x ^ 1, c)),
+        pairs(lambda z, y, x, c: (z, y, x ^ 3, c)),
+    ):
+        partial = partial + lax.ppermute(partial, AXES, partner)
+    others = lax.ppermute(partial, AXES, pairs(lambda z, y, x, c: (z, 3 - y, x, c)))
     return pl.pallas_call(
         image_kernel,
         out_shape=jax.ShapeDtypeStruct((2, ROWS, 4 * WIN), BF16),
-        in_specs=[vmem()] * 3,
+        in_specs=[vmem()] * 4,
         out_specs=hbm(),
         scratch_shapes=[
             pltpu.VMEM((8, 128), F32),
@@ -451,7 +458,7 @@
             pltpu.SemaphoreType.DMA((8,)),
         ],
         compiler_params=params(20),
-    )(grads, meta, b)
+    )(partial, others, meta, b)
 
 
 def solution(mesh):

time: 55.7 us -> 56.5 us (1.014)
  the two profiles are of different devices: /device:TPU:1 before, /device:TPU:0 now
where the time goes in v6:
time: 56.5 us; the launch traced here: 56.3 us
  Pallas kernels  18.3 us (32%)
  blocking collectives  17 us (30%)
  waiting for transfers between devices  11 us (19%)
  starting transfers between devices  9.9 us (18%)
    all_to_all x1, blocking collectives, shards(): lax.all_to_all(own, AXES, split_axis=0, concat_axis=0, axis_index_groups=...  17 us
    ppermute x3, waiting for transfers between devices, shards(): partial = partial + lax.ppermute(partial, AXES, partner)  6.34 us
    ppermute x3, starting transfers between devices, shards(): lax.ppermute(plane, AXES, along_last(k))  5.05 us
    pallas_call x2, Pallas kernels, shards(): pl.pallas_call(functools.partial(middle_band_kernel, index), out_shape=[t...  4.62 us
    pallas_call x1, Pallas kernels, shards(): theirs, mine, filt_v = first_bands(chunks[0], filt)  4.62 us
    ppermute x1, waiting for transfers between devices, shards(): lax.ppermute(partial, AXES, pairs(lambda z, y, x, c: (z, 3 - y, x, c)))  3.96 us
    ppermute x3, starting transfers between devices, shards(): partial = partial + lax.ppermute(partial, AXES, partner)  3.34 us
    pallas_call x1, Pallas kernels, shards(): pl.pallas_call(image_kernel, out_shape=jax.ShapeDtypeStruct((2, ROWS, 4 *...  3.14 us
  transfers between devices with their start and end apart: 9, of which 5 were waited for; matrix products, arithmetic and copies ran while one was open for 0% of the time, Pallas kernels for 22%

profile of v6, /device:TPU:0, one launch (start us, length us, event | category | flops | bytes accessed | tf_op | source)
XLA Modules:
  0.0 56.3 jit_solution(17201678591280277193)
XLA Ops:
  0.0 1.8 %shard_map.73 = bf16[16,8,1152]{2,1,0:T(8,128)(2,1)} custom-call(s32[1,4]{1,0:T(1,128)} %order_h.1, s32[4]{0:T(128)} %off_h.1, s32[4]{0:T(128)} %fine_h.1, s32[4]{0:T(128)} %dop_h.1, s32[4,16]{1,0:T(4,128)} %bitcast.6, bf16[2,4,2048]{2,1,0:T(4,128)(2,1)} %raw_h.1), custom_call_target="tpu_custom_call" | custom-call | tf_op jit(solution)/shard_map/pallas_call | solution.py:350
  1.8 17.0 %all_to_all.5 = bf16[16,8,1152]{2,1,0:T(8,128)(2,1)S(1)} all-to-all(bf16[16,8,1152]{2,1,0:T(8,128)(2,1)} %shard_map.73), channel_id=1, replica_groups={{0,16,8,24,32,48,40,56,64,80,72,88,96,112,104,120},{2,18,10,26,34,50,42..., dimensions={0} | all-to-all | bytes 589824 | tf_op jit(solution)/shard_map/all_to_all | solution.py:366
  18.8 1.5 %collective-permute-start.1 = (bf16[128,1152]{1,0:T(8,128)(2,1)S(1)}, bf16[128,1152]{1,0:T(8,128)(2,1)S(1)}, u32[]{:S(2)}, u32[]{:S(2)}) collective-permute-start(bf16[128,1152]{1,0:T(8,128)(2,1)S(1)} %bitcast.2), channel_id=1, source_target_pairs={{0,2},{1,17},{2,4},{3,19},{4,6},{5,21},{6,0},{7,23},{16,18},{17,9}... | collective-permute-start | bytes 884744 | tf_op jit(solution)/shard_map/ppermute | solution.py:369
  20.3 1.7 %collective-permute-start = (bf16[128,1152]{1,0:T(8,128)(2,1)S(1)}, bf16[128,1152]{1,0:T(8,128)(2,1)S(1)}, u32[]{:S(2)}, u32[]{:S(2)}) collective-permute-start(bf16[128,1152]{1,0:T(8,128)(2,1)S(1)} %bitcast.3), channel_id=1, source_target_pairs={{0,6},{1,25},{2,0},{3,27},{4,2},{5,29},{6,4},{7,31},{16,22},{17,1}... | collective-permute-start | bytes 884744 | tf_op jit(solution)/shard_map/ppermute | solution.py:369
  22.0 1.8 %collective-permute-start.2 = (bf16[128,1152]{1,0:T(8,128)(2,1)S(1)}, bf16[128,1152]{1,0:T(8,128)(2,1)S(1)}, u32[]{:S(2)}, u32[]{:S(2)}) collective-permute-start(bf16[128,1152]{1,0:T(8,128)(2,1)S(1)} %bitcast.4), channel_id=1, source_target_pairs={{0,4},{1,9},{2,6},{3,11},{4,0},{5,13},{6,2},{7,15},{16,20},{17,25}... | collective-permute-start | bytes 884744 | tf_op jit(solution)/shard_map/ppermute | solution.py:369
  23.8 4.6 %shard_map.74 = (bf16[384,1152]{1,0:T(8,128)(2,1)S(1)}, bf16[1024,1152]{1,0:T(8,128)(2,1)S(1)}, bf16[2,1024,2048]{2,1,0:T(8,128)(2,1)S(1)}) custom-call(bf16[128,1152]{1,0:T(8,128)(2,1)S(1)} %bitcast.5, bf16[2,1024,2048]{2,1,0:T(8,128)(2,1)} %filt_h.1), custom_call_target="tpu_custom_call" | custom-call | flops 1073741824 | bytes 8388608 | tf_op jit(solution)/shard_map/pallas_call | solution.py:391
  28.5 0.0 collective-permute-done.1.m
  28.5 2.3 %shard_map.75 = (bf16[384,1152]{1,0:T(8,128)(2,1)S(1)}, bf16[1024,1152]{1,0:T(8,128)(2,1)S(1)}) custom-call(bf16[128,1152]{1,0:T(8,128)(2,1)S(1)} %collective-permute-done.1.m, bf16[2,1024,2048]{2,1,0:T(8,128)(2,1)S(1)} %get-tuple-element.22.filt, bf16[384,1152]{1,0:T(8,128)(2,1)S(1)} %get-tuple-element.23.theirs_in, ...), custom_call_target="tpu_custom_call", output_to_operand_aliasing={{0}: (2, {}), {1}: (3, {})} | custom-call | flops 1073741824 | bytes 8388608 | tf_op jit(solution)/shard_map/pallas_call | solution.py:393
  30.8 0.0 collective-permute-done.m
  30.8 2.3 %shard_map.76 = (bf16[384,1152]{1,0:T(8,128)(2,1)S(1)}, bf16[1024,1152]{1,0:T(8,128)(2,1)S(1)}) custom-call(bf16[128,1152]{1,0:T(8,128)(2,1)S(1)} %collective-permute-done.m, bf16[2,1024,2048]{2,1,0:T(8,128)(2,1)S(1)} %get-tuple-element.22.filt, bf16[384,1152]{1,0:T(8,128)(2,1)S(1)} %get-tuple-element.25.theirs_in, ...), custom_call_target="tpu_custom_call", output_to_operand_aliasing={{0}: (2, {}), {1}: (3, {})} | custom-call | flops 1073741824 | bytes 8388608 | tf_op jit(solution)/shard_map/pallas_call | solution.py:393
  33.1 0.0 collective-permute-done.2.m
  33.1 0.1 collective-permute-start.4
  33.2 2.3 %shard_map.77 = (bf16[128,1152]{1,0:T(8,128)(2,1)S(1)}, bf16[1024,1152]{1,0:T(8,128)(2,1)S(1)}) custom-call(bf16[128,1152]{1,0:T(8,128)(2,1)S(1)} %collective-permute-done.2.m, bf16[2,1024,2048]{2,1,0:T(8,128)(2,1)S(1)} %get-tuple-element.22.filt, bf16[1024,1152]{1,0:T(8,128)(2,1)S(1)} %get-tuple-element.29.mine_in), custom_call_target="tpu_custom_call", output_to_operand_aliasing={{1}: (2, {})} | custom-call | flops 1073741824 | bytes 8388608 | tf_op jit(solution)/shard_map/pallas_call | solution.py:405
  35.5 0.6 %collective-permute-start.3 = (bf16[128,1152]{1,0:T(8,128)(2,1)S(1)}, bf16[128,1152]{1,0:T(8,128)(2,1)S(1)}, u32[]{:S(2)}, u32[]{:S(2)}) collective-permute-start(bf16[128,1152]{1,0:T(8,128)(2,1)S(1)} %get-tuple-element.30), channel_id=1, source_target_pairs={{0,1},{1,0},{2,3},{3,2},{4,5},{5,4},{6,7},{7,6},{16,17},{17,16},{1... | collective-permute-start | bytes 884744 | tf_op jit(solution)/shard_map/ppermute | solution.py:415
  36.1 0.0 collective-permute-done.4.given
  36.1 0.6 %shard_map.78 = (f32[16,1152]{1,0:T(8,128)S(1)}, f32[8,896]{1,0:T(8,128)S(1)}, bf16[1024,1152]{1,0:T(8,128)(2,1)S(1)}) custom-call(bf16[384,1152]{1,0:T(8,128)(2,1)S(1)} %collective-permute-done.4.given, bf16[1024,1152]{1,0:T(8,128)(2,1)S(1)} %get-tuple-element.32.b_in), custom_call_target="tpu_custom_call", output_to_operand_aliasing={{2}: (1, {})} | custom-call | flops 33030144 | bytes 4194304 | tf_op jit(solution)/shard_map/pallas_call | solution.py:416
  36.7 0.6 %collective-permute-done.3.last = bf16[128,1152]{1,0:T(8,128)(2,1)S(1)} collective-permute-done((bf16[128,1152]{1,0:T(8,128)(2,1)S(1)}, bf16[128,1152]{1,0:T(8,128)(2,1)S(1)}, u32[]{:S(2)}, u32[]{:S(2)}) %collective-permute-start.3) | collective-permute-done | bytes 294944 | tf_op jit(solution)/shard_map/ppermute | solution.py:415
  37.3 1.3 %shard_map.79 = (f32[8,128]{1,0:T(8,128)S(1)}, f32[2,8,128]{2,1,0:T(8,128)S(1)}, bf16[1024,1152]{1,0:T(8,128)(2,1)S(1)}) custom-call(bf16[128,1152]{1,0:T(8,128)(2,1)S(1)} %collective-permute-done.3.last, f32[16,1152]{1,0:T(8,128)S(1)} %get-tuple-element.33.early, f32[8,896]{1,0:T(8,128)S(1)} %get-tuple-element.34.info, ...), custom_call_target="tpu_custom_call", output_to_operand_aliasing={{2}: (3, {})} | custom-call | tf_op jit(solution)/shard_map/pallas_call | solution.py:429
  38.6 0.4 collective-permute-start.5
  39.1 0.8 %collective-permute-done.5 = f32[8,128]{1,0:T(8,128)S(1)} collective-permute-done((f32[8,128]{1,0:T(8,128)S(1)}, f32[8,128]{1,0:T(8,128)S(1)}, u32[]{:S(2)}, u32[]{:S(2)}) %collective-permute-start.5) | collective-permute-done | bytes 4128 | tf_op jit(solution)/shard_map/ppermute | solution.py:446
  39.9 0.6 %collective-permute-start.6 = (f32[8,128]{1,0:T(8,128)S(1)}, f32[8,128]{1,0:T(8,128)S(1)}, u32[]{:S(2)}, u32[]{:S(2)}) collective-permute-start(f32[8,128]{1,0:T(8,128)S(1)} %add.9), channel_id=1, source_target_pairs={{0,2},{1,3},{2,0},{3,1},{4,6},{5,7},{6,4},{7,5},{16,18},{17,19},{1... | collective-permute-start | bytes 12296 | tf_op jit(solution)/shard_map/ppermute | solution.py:446
  40.5 3.0 %collective-permute-done.6 = f32[8,128]{1,0:T(8,128)S(1)} collective-permute-done((f32[8,128]{1,0:T(8,128)S(1)}, f32[8,128]{1,0:T(8,128)S(1)}, u32[]{:S(2)}, u32[]{:S(2)}) %collective-permute-start.6) | collective-permute-done | bytes 4128 | tf_op jit(solution)/shard_map/ppermute | solution.py:446
  43.5 2.3 %collective-permute-start.7 = (f32[8,128]{1,0:T(8,128)S(1)}, f32[8,128]{1,0:T(8,128)S(1)}, u32[]{:S(2)}, u32[]{:S(2)}) collective-permute-start(f32[8,128]{1,0:T(8,128)S(1)} %add.10), channel_id=1, source_target_pairs={{0,6},{1,7},{2,4},{3,5},{4,2},{5,3},{6,0},{7,1},{16,22},{17,23},{1... | collective-permute-start | bytes 12296 | tf_op jit(solution)/shard_map/ppermute | solution.py:446
  45.8 2.5 %collective-permute-done.7 = f32[8,128]{1,0:T(8,128)S(1)} collective-permute-done((f32[8,128]{1,0:T(8,128)S(1)}, f32[8,128]{1,0:T(8,128)S(1)}, u32[]{:S(2)}, u32[]{:S(2)}) %collective-permute-start.7) | collective-permute-done | bytes 4128 | tf_op jit(solution)/shard_map/ppermute | solution.py:446
  48.3 0.9 %collective-permute-start.8 = (f32[8,128]{1,0:T(8,128)S(1)}, f32[8,128]{1,0:T(8,128)S(1)}, u32[]{:S(2)}, u32[]{:S(2)}) collective-permute-start(f32[8,128]{1,0:T(8,128)S(1)} %add.11.g_in), channel_id=1, source_target_pairs={{0,24},{1,25},{2,26},{3,27},{4,28},{5,29},{6,30},{7,31},{16,8},{17... | collective-permute-start | bytes 12296 | tf_op jit(solution)/shard_map/ppermute | solution.py:447
  49.2 4.0 %collective-permute-done.8.g_other = f32[8,128]{1,0:T(8,128)S(1)} collective-permute-done((f32[8,128]{1,0:T(8,128)S(1)}, f32[8,128]{1,0:T(8,128)S(1)}, u32[]{:S(2)}, u32[]{:S(2)}) %collective-permute-start.8) | collective-permute-done | bytes 4128 | tf_op jit(solution)/shard_map/ppermute | solution.py:447
  53.1 3.1 %shard_map.80 = bf16[2,128,4096]{2,1,0:T(8,128)(2,1)} custom-call(f32[8,128]{1,0:T(8,128)S(1)} %add.11.g_in, f32[8,128]{1,0:T(8,128)S(1)} %collective-permute-done.8.g_other, f32[2,8,128]{2,1,0:T(8,128)S(1)} %get-tuple-element.37.meta, bf16[1024,1152]{1,0:T(8,128)(2,1)S(1)} %get-tuple-element.38.b), custom_call_target="tpu_custom_call" | custom-call | tf_op jit(solution)/shard_map/pallas_call | solution.py:448
  (3 shorter events, 0.0 us)
Async XLA Ops:
  18.8 9.7 %collective-permute-start.1 = (bf16[128,1152]{1,0:T(8,128)(2,1)S(1)}, bf16[128,1152]{1,0:T(8,128)(2,1)S(1)}, u32[]{:S(2)}, u32[]{:S(2)}) collective-permute-start(bf16[128,1152]{1,0:T(8,128)(2,1)S(1)} %bitcast.2), channel_id=1, source_target_pairs={{0,2},{1,17},{2,4},{3,19},{4,6},{5,21},{6,0},{7,23},{16,18},{17,9}... | collective-permute-start | bytes 884744 | tf_op jit(solution)/shard_map/ppermute | solution.py:369
  20.3 10.5 %collective-permute-start = (bf16[128,1152]{1,0:T(8,128)(2,1)S(1)}, bf16[128,1152]{1,0:T(8,128)(2,1)S(1)}, u32[]{:S(2)}, u32[]{:S(2)}) collective-permute-start(bf16[128,1152]{1,0:T(8,128)(2,1)S(1)} %bitcast.3), channel_id=1, source_target_pairs={{0,6},{1,25},{2,0},{3,27},{4,2},{5,29},{6,4},{7,31},{16,22},{17,1}... | collective-permute-start | bytes 884744 | tf_op jit(solution)/shard_map/ppermute | solution.py:369
  22.0 11.1 %collective-permute-start.2 = (bf16[128,1152]{1,0:T(8,128)(2,1)S(1)}, bf16[128,1152]{1,0:T(8,128)(2,1)S(1)}, u32[]{:S(2)}, u32[]{:S(2)}) collective-permute-start(bf16[128,1152]{1,0:T(8,128)(2,1)S(1)} %bitcast.4), channel_id=1, source_target_pairs={{0,4},{1,9},{2,6},{3,11},{4,0},{5,13},{6,2},{7,15},{16,20},{17,25}... | collective-permute-start | bytes 884744 | tf_op jit(solution)/shard_map/ppermute | solution.py:369
  33.1 3.0 %collective-permute-start.4 = (bf16[384,1152]{1,0:T(8,128)(2,1)S(1)}, bf16[384,1152]{1,0:T(8,128)(2,1)S(1)}, u32[]{:S(2)}, u32[]{:S(2)}) collective-permute-start(bf16[384,1152]{1,0:T(8,128)(2,1)S(1)} %get-tuple-element.31), channel_id=1, source_target_pairs={{0,1},{1,0},{2,3},{3,2},{4,5},{5,4},{6,7},{7,6},{16,17},{17,16},{1... | collective-permute-start | bytes 2654216 | tf_op jit(solution)/shard_map/ppermute | solution.py:404
  35.5 1.8 %collective-permute-start.3 = (bf16[128,1152]{1,0:T(8,128)(2,1)S(1)}, bf16[128,1152]{1,0:T(8,128)(2,1)S(1)}, u32[]{:S(2)}, u32[]{:S(2)}) collective-permute-start(bf16[128,1152]{1,0:T(8,128)(2,1)S(1)} %get-tuple-element.30), channel_id=1, source_target_pairs={{0,1},{1,0},{2,3},{3,2},{4,5},{5,4},{6,7},{7,6},{16,17},{17,16},{1... | collective-permute-start | bytes 884744 | tf_op jit(solution)/shard_map/ppermute | solution.py:415
  38.6 1.3 %collective-permute-start.5 = (f32[8,128]{1,0:T(8,128)S(1)}, f32[8,128]{1,0:T(8,128)S(1)}, u32[]{:S(2)}, u32[]{:S(2)}) collective-permute-start(f32[8,128]{1,0:T(8,128)S(1)} %get-tuple-element.36), channel_id=1, source_target_pairs={{0,1},{1,0},{2,3},{3,2},{4,5},{5,4},{6,7},{7,6},{16,17},{17,16},{1... | collective-permute-start | bytes 12296 | tf_op jit(solution)/shard_map/ppermute | solution.py:446
  39.9 3.6 %collective-permute-start.6 = (f32[8,128]{1,0:T(8,128)S(1)}, f32[8,128]{1,0:T(8,128)S(1)}, u32[]{:S(2)}, u32[]{:S(2)}) collective-permute-start(f32[8,128]{1,0:T(8,128)S(1)} %add.9), channel_id=1, source_target_pairs={{0,2},{1,3},{2,0},{3,1},{4,6},{5,7},{6,4},{7,5},{16,18},{17,19},{1... | collective-permute-start | bytes 12296 | tf_op jit(solution)/shard_map/ppermute | solution.py:446
  43.5 4.8 %collective-permute-start.7 = (f32[8,128]{1,0:T(8,128)S(1)}, f32[8,128]{1,0:T(8,128)S(1)}, u32[]{:S(2)}, u32[]{:S(2)}) collective-permute-start(f32[8,128]{1,0:T(8,128)S(1)} %add.10), channel_id=1, source_target_pairs={{0,6},{1,7},{2,4},{3,5},{4,2},{5,3},{6,0},{7,1},{16,22},{17,23},{1... | collective-permute-start | bytes 12296 | tf_op jit(solution)/shard_map/ppermute | solution.py:446
  48.3 4.8 %collective-permute-start.8 = (f32[8,128]{1,0:T(8,128)S(1)}, f32[8,128]{1,0:T(8,128)S(1)}, u32[]{:S(2)}, u32[]{:S(2)}) collective-permute-start(f32[8,128]{1,0:T(8,128)S(1)} %add.11.g_in), channel_id=1, source_target_pairs={{0,24},{1,25},{2,26},{3,27},{4,28},{5,29},{6,30},{7,31},{16,8},{17... | collective-permute-start | bytes 12296 | tf_op jit(solution)/shard_map/ppermute | solution.py:447
